TPU v7x, 32 devices: a whole 2x2x4 slice. The times are simulated.
32 devices in a mesh: batch: 4 (over x, core), seq: 8 (over z, y).
Axes of the slice: x: 2, y: 2, z: 4, core: 2. Of those that a mesh axis runs over, the one named last changes fastest.
Arguments:
- inputs: bfloat16 [3, 4, 2048, 1024], P(None, 'batch', 'seq'), may hold values from -6 to 6
- lengths: int32 [3, 4], P(None, 'batch'), may hold values from 1024 to 2048, as said below
- cotangent: bfloat16 [3, 4, 2048, 1024], P(None, 'batch', 'seq'), may hold values from -6 to 6
- norm1_gain: bfloat16 [1024], P(('batch', 'seq')), may hold values from 0.099609375 to 1.8984375
- norm1_bias: bfloat16 [1024], P(('batch', 'seq')), may hold values from -1.5 to 1.5
- step_size: bfloat16 [1024], P(('batch', 'seq')), may hold values from 0 to 1, as said below
- state_out: bfloat16 [2, 1024, 64], P(None, ('batch', 'seq')), may hold values from -128 to 128
- skip_gain: bfloat16 [1024], P(('batch', 'seq')), may hold values from -4 to 4
- glu_weight: bfloat16 [1024, 2048], P(('batch', 'seq')), may hold values from -0.1875 to 0.1875
- glu_bias: bfloat16 [2048], P(('batch', 'seq')), may hold values from -1.5 to 1.5
- norm2_gain: bfloat16 [1024], P(('batch', 'seq')), may hold values from 0.099609375 to 1.8984375
- norm2_bias: bfloat16 [1024], P(('batch', 'seq')), may hold values from -1.5 to 1.5
- ffn_in_weight: bfloat16 [1024, 4096], P(('batch', 'seq')), may hold values from -0.1875 to 0.1875
- ffn_in_bias: bfloat16 [4096], P(('batch', 'seq')), may hold values from -1.5 to 1.5
- ffn_out_weight: bfloat16 [4096, 1024], P(('batch', 'seq')), may hold values from -0.09375 to 0.09375
- ffn_out_bias: bfloat16 [1024], P(('batch', 'seq')), may hold values from -1.5 to 1.5
Outputs:
- output: bfloat16 [3, 4, 2048, 1024], P(None, 'batch', 'seq')
- input_grad: bfloat16 [3, 4, 2048, 1024], P(None, 'batch', 'seq')
- grad_norm1_gain: float32 [1024], P(('batch', 'seq'))
- grad_norm1_bias: float32 [1024], P(('batch', 'seq'))
- grad_state_out: float32 [2, 1024, 64], P(None, ('batch', 'seq'))
- grad_skip_gain: float32 [1024], P(('batch', 'seq'))
- grad_glu_weight: float32 [1024, 2048], P(('batch', 'seq'))
- grad_glu_bias: float32 [2048], P(('batch', 'seq'))
- grad_norm2_gain: float32 [1024], P(('batch', 'seq'))
- grad_norm2_bias: float32 [1024], P(('batch', 'seq'))
- grad_ffn_in_weight: float32 [1024, 4096], P(('batch', 'seq'))
- grad_ffn_in_bias: float32 [4096], P(('batch', 'seq'))
- grad_ffn_out_weight: float32 [4096, 1024], P(('batch', 'seq'))
- grad_ffn_out_bias: float32 [1024], P(('batch', 'seq'))
Inputs may be any that keep to these rules, and one draw needn't show every extreme that they name: `lengths`: in every column one of the 3 contexts has the full length 2048. `step_size`: positive step sizes.
All inputs are finite; a program needn't handle non-finite values.
Results may differ from a plain program's by a relative error of at most 0.006.
Values may be sent and summed in bfloat16 or wider, within the bound.
No kernel may reach another device: no remote copies, remote signals or barrier semaphores. Data moves between devices by JAX's collectives and lax.ppermute only.
A program may use at most 448 MiB of HBM per device.

v0:
```python
import math

import jax
import jax.numpy as jnp
from jax import lax
from jax.sharding import PartitionSpec as P

norm_eps = 1e-05
channel_block = 256
highest = lax.Precision.HIGHEST


def prefix(part, axis, combine, identity, reverse):
    count = lax.axis_size(axis)
    place = lax.axis_index(axis)
    ahead = count - 1 - place if reverse else place
    gathered = jax.tree.map(lambda a: lax.all_gather(a, axis), part)
    state = jax.tree.map(lambda a, e: jnp.zeros_like(a) + jnp.asarray(e, a.dtype), part, identity)

    def one(hop, state):
        source = count - 1 - hop if reverse else hop
        return combine(
            state, jax.tree.map(lambda a: lax.dynamic_index_in_dim(a, source, 0, False), gathered)
        )

    return lax.fori_loop(0, ahead, one, state)


def layer_stats(values):
    centered = values - jnp.mean(values, axis=-1, keepdims=True)
    scale_inv = lax.rsqrt(jnp.mean(centered * centered, axis=-1, keepdims=True) + norm_eps)
    return (centered * scale_inv, scale_inv)


def norm_back(grad_normed, normed, scale_inv):
    first_mean = jnp.mean(grad_normed, axis=-1, keepdims=True)
    second_mean = jnp.mean(grad_normed * normed, axis=-1, keepdims=True)
    return scale_inv * (grad_normed - first_mean - normed * second_mean)


def with_slope(function, values):
    result, back_fn = jax.vjp(function, values)
    return (result, back_fn(jnp.ones_like(values))[0])


def cmul(first_pair, second_pair):
    return (
        first_pair[0] * second_pair[0] - first_pair[1] * second_pair[1],
        first_pair[0] * second_pair[1] + first_pair[1] * second_pair[0],
    )


def cmul_conj(first_pair, second_pair):
    return (
        first_pair[0] * second_pair[0] + first_pair[1] * second_pair[1],
        first_pair[0] * second_pair[1] - first_pair[1] * second_pair[0],
    )


def chain(earlier, later):
    return (
        earlier[0] * later[0] - earlier[1] * later[1],
        earlier[0] * later[1] + earlier[1] * later[0],
        earlier[2] * later[0] - earlier[3] * later[1] + later[2],
        earlier[2] * later[1] + earlier[3] * later[0] + later[3],
    )


def chain_identity(template):
    return (
        jnp.ones_like(template),
        jnp.zeros_like(template),
        jnp.zeros_like(template),
        jnp.zeros_like(template),
    )


def dft_tables(local_len):
    full_len = 2 * local_len
    freqs = jnp.arange(local_len + 1, dtype=jnp.int32)[:, None]
    positions = jnp.arange(local_len, dtype=jnp.int32)[None, :]
    phase = 2.0 * math.pi / full_len * (freqs * positions % full_len).astype(jnp.float32)
    edge = jnp.logical_or(freqs == 0, freqs == local_len)
    weighting = jnp.where(edge, 1.0, 2.0).astype(jnp.float32) / full_len
    return (
        jnp.cos(phase),
        -jnp.sin(phase),
        (weighting * jnp.cos(phase)).T,
        (-weighting * jnp.sin(phase)).T,
    )


def transform(dft_parts, values):
    return (
        jnp.dot(dft_parts[0], values, precision=highest, preferred_element_type=jnp.float32),
        jnp.dot(dft_parts[1], values, precision=highest, preferred_element_type=jnp.float32),
    )


def inverse(dft_parts, spectrum):
    return jnp.dot(
        dft_parts[2], spectrum[0], precision=highest, preferred_element_type=jnp.float32
    ) + jnp.dot(dft_parts[3], spectrum[1], precision=highest, preferred_element_type=jnp.float32)


def discretize(step_len, mode_count):
    turn_rate = math.pi * jnp.arange(mode_count, dtype=jnp.float32)[:, None]
    decay_rate = -0.5 * step_len[None, :]
    phase_rate = turn_rate * step_len[None, :]
    magnitude = jnp.exp(decay_rate)
    step_mult = (magnitude * jnp.cos(phase_rate), magnitude * jnp.sin(phase_rate))
    minus_one = jnp.expm1(decay_rate) * jnp.cos(phase_rate) - 2.0 * jnp.sin(0.5 * phase_rate) ** 2
    denominator = 0.25 + turn_rate**2
    input_mult = (
        (-0.5 * minus_one + step_mult[1] * turn_rate) / denominator,
        (-0.5 * step_mult[1] - minus_one * turn_rate) / denominator,
    )
    return (decay_rate, phase_rate, step_mult, input_mult)


def power_parts(decay_rate, phase_rate, length):
    near_count = math.gcd(length, 16)
    far_count = length // near_count

    def table(offsets):
        fading = jnp.exp(offsets * decay_rate[None])
        phase = offsets * phase_rate[None]
        return (fading * jnp.cos(phase), fading * jnp.sin(phase))

    near_offsets = jnp.arange(near_count, dtype=jnp.float32)[:, None, None]
    far_offsets = (near_count * jnp.arange(far_count, dtype=jnp.float32))[:, None, None]
    return table(near_offsets) + table(far_offsets)


def project_block(series, near_re, near_im, far_re, far_im):
    near_count = near_re.shape[0]
    far_count = far_re.shape[0]
    folded = series.reshape(far_count, near_count, series.shape[-1])
    inner_re = jnp.einsum("ijh,jnh->inh", folded, near_re, precision=highest)
    inner_im = jnp.einsum("ijh,jnh->inh", folded, near_im, precision=highest)
    joined = cmul((far_re, far_im), (inner_re, inner_im))
    return (jnp.sum(joined[0], axis=0), jnp.sum(joined[1], axis=0))


def pair_block(grad_series, cross_corr, near_re, near_im, far_re, far_im):
    return project_block(grad_series, near_re, near_im, far_re, far_im) + project_block(
        cross_corr, near_re, near_im, far_re, far_im
    )


def expand_block(factor_re, factor_im, near_re, near_im, far_re, far_im):
    lifted = cmul((far_re, far_im), (factor_re[None], factor_im[None]))
    spanned = jnp.einsum("inh,jnh->ijh", lifted[0], near_re, precision=highest) - jnp.einsum(
        "inh,jnh->ijh", lifted[1], near_im, precision=highest
    )
    return (spanned.reshape(-1, spanned.shape[-1]),)


def by_channels(function, *arrays):
    width_all = arrays[-1].shape[-1]
    block_count = width_all // channel_block

    def one_block(block_index):
        offset = block_index * channel_block
        return function(
            *[
                lax.dynamic_slice_in_dim(element, offset, channel_block, element.ndim - 1)
                for element in arrays
            ]
        )

    stacked = lax.map(one_block, jnp.arange(block_count, dtype=jnp.int32))
    return tuple(
        (
            jnp.moveaxis(element, 0, -2).reshape(element.shape[1:-1] + (width_all,))
            for element in stacked
        )
    )


def prepare(full_weights, local_len, dft_parts):
    (
        gain_one,
        bias_one,
        step_len,
        state_out,
        skip_gain,
        glu_weight,
        glu_bias,
        gain_two,
        bias_two,
        in_weight,
        in_bias,
        out_weight,
        out_bias,
    ) = full_weights
    mode_count = state_out.shape[2]
    state_pair = (state_out[0].astype(jnp.float32).T, state_out[1].astype(jnp.float32).T)
    decay_rate, phase_rate, step_mult, input_mult = discretize(
        step_len.astype(jnp.float32), mode_count
    )
    tables = power_parts(decay_rate, phase_rate, local_len)
    joint = cmul(state_pair, input_mult)
    (kernel,) = by_channels(expand_block, joint[0], joint[1], *tables)
    span_size = jnp.exp(local_len * decay_rate)
    return {
        "gain_one": gain_one.astype(jnp.float32),
        "bias_one": bias_one.astype(jnp.float32),
        "skip_gain": skip_gain.astype(jnp.float32),
        "glu_weight": glu_weight,
        "glu_bias": glu_bias.astype(jnp.float32),
        "gain_two": gain_two.astype(jnp.float32),
        "bias_two": bias_two.astype(jnp.float32),
        "in_weight": in_weight,
        "in_bias": in_bias.astype(jnp.float32),
        "out_weight": out_weight,
        "out_bias": out_bias.astype(jnp.float32),
        "state_pair": state_pair,
        "tables": tables,
        "step_mult": step_mult,
        "input_mult": input_mult,
        "state_step": cmul(state_pair, step_mult),
        "kernel_spec": transform(dft_parts, kernel),
        "span_mult": (
            span_size * jnp.cos(local_len * phase_rate),
            span_size * jnp.sin(local_len * phase_rate),
        ),
    }


def state_forward(driven, prepared, dft_parts):
    drive_spec = transform(dft_parts, driven)
    local_part = inverse(dft_parts, cmul(drive_spec, prepared["kernel_spec"]))
    loaded = by_channels(project_block, driven[::-1], *prepared["tables"])
    ends = cmul(loaded, prepared["input_mult"])
    span_mult = prepared["span_mult"]
    carried = prefix(
        (span_mult[0], span_mult[1], ends[0], ends[1]),
        "seq",
        chain,
        chain_identity(span_mult[0]),
        False,
    )
    entry_state = (carried[2], carried[3])
    factor = cmul(prepared["state_step"], entry_state)
    (incoming,) = by_channels(expand_block, factor[0], factor[1], *prepared["tables"])
    mixed_out = local_part + incoming + prepared["skip_gain"] * driven
    return (mixed_out, (drive_spec, entry_state))


def state_backward(grad_mixed, driven, kept_state, prepared, dft_parts):
    drive_spec, entry_state = kept_state
    grad_spec = transform(dft_parts, grad_mixed)
    local_back = inverse(dft_parts, cmul_conj(prepared["kernel_spec"], grad_spec))
    cross_corr = inverse(dft_parts, cmul_conj(drive_spec, grad_spec))
    grad_re, grad_im, held_re, held_im = by_channels(
        pair_block, grad_mixed, cross_corr, *prepared["tables"]
    )
    weighted = cmul((grad_re, grad_im), prepared["step_mult"])
    sent_part = cmul(prepared["state_pair"], weighted)
    span_mult = prepared["span_mult"]
    returned = prefix(
        (span_mult[0], span_mult[1], sent_part[0], sent_part[1]),
        "seq",
        chain,
        chain_identity(span_mult[0]),
        True,
    )
    scaled = cmul((returned[2], returned[3]), prepared["input_mult"])
    (carry_back,) = by_channels(expand_block, scaled[0], scaled[1], *prepared["tables"])
    grad_driven = local_back + carry_back[::-1] + prepared["skip_gain"] * grad_mixed
    local_sum = cmul((held_re, held_im), prepared["input_mult"])
    entry_sum = cmul(weighted, entry_state)
    grad_states = jnp.stack([(local_sum[0] + entry_sum[0]).T, -(local_sum[1] + entry_sum[1]).T])
    grad_skip = jnp.sum(grad_mixed * driven, axis=0)
    return (grad_driven, grad_states, grad_skip)


def layer_pass(input_rows, cot_rows, valid_rows, prepared, dft_parts):
    residual_in = input_rows.astype(jnp.float32)
    width_all = residual_in.shape[1]
    normed_one, scale_one = layer_stats(residual_in)
    driven = valid_rows * (normed_one * prepared["gain_one"] + prepared["bias_one"])
    mixed_out, kept_state = state_forward(driven, prepared, dft_parts)
    act_value, act_slope = with_slope(jax.nn.gelu, mixed_out)
    activated = act_value.astype(jnp.bfloat16)
    gated_pre = (
        jnp.dot(activated, prepared["glu_weight"], preferred_element_type=jnp.float32)
        + prepared["glu_bias"]
    )
    left_half = gated_pre[:, :width_all]
    gate_open = jax.nn.sigmoid(gated_pre[:, width_all:])
    residual = residual_in + left_half * gate_open
    normed_two, scale_two = layer_stats(residual)
    norm_two = (normed_two * prepared["gain_two"] + prepared["bias_two"]).astype(jnp.bfloat16)
    hidden = (
        jnp.dot(norm_two, prepared["in_weight"], preferred_element_type=jnp.float32)
        + prepared["in_bias"]
    )
    spread_value, spread_slope = with_slope(jax.nn.gelu, hidden)
    spread = spread_value.astype(jnp.bfloat16)
    ffn_value = (
        jnp.dot(spread, prepared["out_weight"], preferred_element_type=jnp.float32)
        + prepared["out_bias"]
    )
    result = (residual + ffn_value).astype(jnp.bfloat16)
    grad_out = valid_rows * cot_rows.astype(jnp.float32)
    grad_ffn = grad_out.astype(jnp.bfloat16)
    grad_out_weight = jnp.einsum("tf,td->fd", spread, grad_ffn, preferred_element_type=jnp.float32)
    grad_out_bias = jnp.sum(grad_ffn.astype(jnp.float32), axis=0)
    grad_spread = jnp.einsum(
        "td,fd->tf", grad_ffn, prepared["out_weight"], preferred_element_type=jnp.float32
    )
    grad_hidden = (grad_spread * spread_slope).astype(jnp.bfloat16)
    grad_in_weight = jnp.einsum(
        "td,tf->df", norm_two, grad_hidden, preferred_element_type=jnp.float32
    )
    grad_in_bias = jnp.sum(grad_hidden.astype(jnp.float32), axis=0)
    grad_norm_two = jnp.einsum(
        "tf,df->td", grad_hidden, prepared["in_weight"], preferred_element_type=jnp.float32
    )
    grad_gain_two = jnp.sum(grad_norm_two * normed_two, axis=0)
    grad_bias_two = jnp.sum(grad_norm_two, axis=0)
    grad_resid = grad_out + norm_back(grad_norm_two * prepared["gain_two"], normed_two, scale_two)
    grad_left = grad_resid * gate_open
    grad_right = grad_resid * left_half * gate_open * (1.0 - gate_open)
    grad_gated = jnp.concatenate([grad_left, grad_right], axis=1).astype(jnp.bfloat16)
    grad_glu_weight = jnp.einsum(
        "td,te->de", activated, grad_gated, preferred_element_type=jnp.float32
    )
    grad_glu_bias = jnp.sum(grad_gated.astype(jnp.float32), axis=0)
    grad_act = jnp.einsum(
        "te,de->td", grad_gated, prepared["glu_weight"], preferred_element_type=jnp.float32
    )
    grad_mixed = grad_act * act_slope
    grad_driven, grad_states, grad_skip = state_backward(
        grad_mixed, driven, kept_state, prepared, dft_parts
    )
    grad_norm_one = valid_rows * grad_driven
    grad_gain_one = jnp.sum(grad_norm_one * normed_one, axis=0)
    grad_bias_one = jnp.sum(grad_norm_one, axis=0)
    input_back = (
        grad_resid + norm_back(grad_norm_one * prepared["gain_one"], normed_one, scale_one)
    ).astype(jnp.bfloat16)
    grad_terms = (
        grad_gain_one,
        grad_bias_one,
        grad_states,
        grad_skip,
        grad_glu_weight,
        grad_glu_bias,
        grad_gain_two,
        grad_bias_two,
        grad_in_weight,
        grad_in_bias,
        grad_out_weight,
        grad_out_bias,
    )
    return (result, input_back, grad_terms)


def per_device(
    inputs,
    lengths,
    cotangent,
    norm1_gain,
    norm1_bias,
    step_size,
    state_out,
    skip_gain,
    glu_weight,
    glu_bias,
    norm2_gain,
    norm2_bias,
    ffn_in_weight,
    ffn_in_bias,
    ffn_out_weight,
    ffn_out_bias,
):
    weight_shards = (
        norm1_gain,
        norm1_bias,
        step_size,
        state_out,
        skip_gain,
        glu_weight,
        glu_bias,
        norm2_gain,
        norm2_bias,
        ffn_in_weight,
        ffn_in_bias,
        ffn_out_weight,
        ffn_out_bias,
    )
    micro_count = inputs.shape[0]
    local_len = inputs.shape[2]
    dft_parts = dft_tables(local_len)
    positions = lax.axis_index("seq") * local_len + jnp.arange(local_len, dtype=jnp.int32)
    totals = None
    local_sums = None
    results = []
    input_backs = []
    for micro_index in range(micro_count):
        prepared = prepare(
            (
                lax.all_gather(weight_shards[0], ("batch", "seq"), axis=0, tiled=True),
                lax.all_gather(weight_shards[1], ("batch", "seq"), axis=0, tiled=True),
                lax.all_gather(weight_shards[2], ("batch", "seq"), axis=0, tiled=True),
                lax.all_gather(weight_shards[3], ("batch", "seq"), axis=1, tiled=True),
                lax.all_gather(weight_shards[4], ("batch", "seq"), axis=0, tiled=True),
                lax.all_gather(weight_shards[5], ("batch", "seq"), axis=0, tiled=True),
                lax.all_gather(weight_shards[6], ("batch", "seq"), axis=0, tiled=True),
                lax.all_gather(weight_shards[7], ("batch", "seq"), axis=0, tiled=True),
                lax.all_gather(weight_shards[8], ("batch", "seq"), axis=0, tiled=True),
                lax.all_gather(weight_shards[9], ("batch", "seq"), axis=0, tiled=True),
                lax.all_gather(weight_shards[10], ("batch", "seq"), axis=0, tiled=True),
                lax.all_gather(weight_shards[11], ("batch", "seq"), axis=0, tiled=True),
                lax.all_gather(weight_shards[12], ("batch", "seq"), axis=0, tiled=True),
            ),
            local_len,
            dft_parts,
        )
        valid_rows = (positions < lengths[micro_index, 0]).astype(jnp.float32)[:, None]
        result, input_back, grad_terms = layer_pass(
            inputs[micro_index, 0], cotangent[micro_index, 0], valid_rows, prepared, dft_parts
        )
        results.append(result)
        input_backs.append(input_back)
        if local_sums is None:
            local_sums = grad_terms
        else:
            local_sums = tuple((first + second for first, second in zip(local_sums, grad_terms)))
    totals = (
        lax.psum_scatter(local_sums[0], ("batch", "seq"), scatter_dimension=0, tiled=True),
        lax.psum_scatter(local_sums[1], ("batch", "seq"), scatter_dimension=0, tiled=True),
        lax.psum_scatter(local_sums[2], ("batch", "seq"), scatter_dimension=1, tiled=True),
        lax.psum_scatter(local_sums[3], ("batch", "seq"), scatter_dimension=0, tiled=True),
        lax.psum_scatter(local_sums[4], ("batch", "seq"), scatter_dimension=0, tiled=True),
        lax.psum_scatter(local_sums[5], ("batch", "seq"), scatter_dimension=0, tiled=True),
        lax.psum_scatter(local_sums[6], ("batch", "seq"), scatter_dimension=0, tiled=True),
        lax.psum_scatter(local_sums[7], ("batch", "seq"), scatter_dimension=0, tiled=True),
        lax.psum_scatter(local_sums[8], ("batch", "seq"), scatter_dimension=0, tiled=True),
        lax.psum_scatter(local_sums[9], ("batch", "seq"), scatter_dimension=0, tiled=True),
        lax.psum_scatter(local_sums[10], ("batch", "seq"), scatter_dimension=0, tiled=True),
        lax.psum_scatter(local_sums[11], ("batch", "seq"), scatter_dimension=0, tiled=True),
    )
    output = jnp.stack(results)[:, None]
    input_grad = jnp.stack(input_backs)[:, None]
    return (output, input_grad) + tuple(totals)


def solution(mesh):
    placed = (
        P(None, "batch", "seq", None),
        P(None, "batch"),
        P(None, "batch", "seq", None),
        P(("batch", "seq")),
        P(("batch", "seq")),
        P(("batch", "seq")),
        P(None, ("batch", "seq"), None),
        P(("batch", "seq")),
        P(("batch", "seq"), None),
        P(("batch", "seq")),
        P(("batch", "seq")),
        P(("batch", "seq")),
        P(("batch", "seq"), None),
        P(("batch", "seq")),
        P(("batch", "seq"), None),
        P(("batch", "seq")),
    )
    return jax.shard_map(
        per_device,
        mesh=mesh,
        in_specs=placed,
        out_specs=(
            P(None, "batch", "seq", None),
            P(None, "batch", "seq", None),
            P(("batch", "seq")),
            P(("batch", "seq")),
            P(None, ("batch", "seq"), None),
            P(("batch", "seq")),
            P(("batch", "seq"), None),
            P(("batch", "seq")),
            P(("batch", "seq")),
            P(("batch", "seq")),
            P(("batch", "seq"), None),
            P(("batch", "seq")),
            P(("batch", "seq"), None),
            P(("batch", "seq")),
        ),
        check_vma=False,
    )
```

profile of v0, /device:TPU:0, one launch (start us, length us, event | category | flops | bytes accessed | tf_op | source)
XLA Modules:
  0.0 2895.9 jit_solution(17021071704979994067)
XLA Ops:
  14.1 42.3 %all-reduce.18 = (bf16[2048]{0:T(1024)(128)(2,1)S(1)}, bf16[1024]{0:T(1024)(128)(2,1)S(1)}, bf16[1024]{0:T(1024)(128)(2,1)S(1)}, bf16[1024]{0:T(1024)(128)(2,1)S...) all-reduce(bf16[2048]{0:T(1024)(128)(2,1)S(1)} %dynamic-update-slic, ...), channel_id=1, replica_groups=mesh['batch'=4,'seq'=8] {'batch','seq'}, use_global_device_ids=true, to_apply=%add.4 | all-reduce | flops 9216 | bytes 36864
  72.9 61.2 %sine_multiply_fusion = (f32[16,64,1024]{1,0,2:T(8,128)}, f32[16,64,1024]{1,0,2:T(8,128)}, f32[16,64,1024]{1,0,2:T(8,128)}, f32[16,64,1024]{1,0,2:T(8,128)}) fusion(f32[64,1024]{0,1:T(8,128)S(1)} %copy.274, f32[16,1024]{0,1:T(8,128)S(1)} %copy-done.127, f32[16]{0:T(128)S(1)} %iota_multiply_fusion.1, f32[16,1024]{0,1:T(8,128)S(1)} %copy-done.128), kind=kLoop, calls=%fused_computation.376 | loop fusion | flops 6291456 | bytes 17170496 | tf_op jit(solution)/shard_map/mul | solution.py:128
  135.8 52.5 %while.259 = (s32[]{:T(128)}, f32[4,64,256]{1,2,0:T(8,128)}, f32[4,64,256]{1,2,0:T(8,128)}, s32[4]{0:T(128)S(1)}, f32[16,64,1024]{1,0,2:T(8,128)}, /*index=5*/f3...) while((s32[]{:T(128)}, f32[4,64,256]{1,2,0:T(8,128)}, ...), condition=%wide.region_7.8_spmd, body=%wide.region_4.7_spmd.sunk | while | flops 102727680 | bytes 12584139 | solution.py:172
  194.4 52.1 %while.262 = (s32[]{:T(128)}, f32[4,64,256]{1,2,0:T(8,128)}, f32[4,64,256]{1,2,0:T(8,128)}, s32[4]{0:T(128)S(1)}, f32[16,64,1024]{1,0,2:T(8,128)}, /*index=5*/f3...) while((s32[]{:T(128)}, f32[4,64,256]{1,2,0:T(8,128)}, ...), condition=%wide.region_19.20_spmd, body=%wide.region_16.19_spmd.sunk | while | flops 102727680 | bytes 12584139 | solution.py:172
  252.7 52.1 %while.265 = (s32[]{:T(128)}, f32[4,64,256]{1,2,0:T(8,128)}, f32[4,64,256]{1,2,0:T(8,128)}, s32[4]{0:T(128)S(1)}, f32[16,64,1024]{1,0,2:T(8,128)}, /*index=5*/f3...) while((s32[]{:T(128)}, f32[4,64,256]{1,2,0:T(8,128)}, ...), condition=%wide.region_31.32_spmd, body=%wide.region_28.31_spmd.sunk | while | flops 102727680 | bytes 12584139 | solution.py:172
  340.6 72.5 %all_gather.69 = bf16[2,1024,64]{2,0,1:T(2,128)(2,1)S(1)} all-gather(bf16[2,32,64]{2,0,1:T(2,128)(2,1)S(1)} %copy.276), channel_id=1, replica_groups=mesh['batch'=4,'seq'=8] {'batch','seq'}, dimensions={1}, use_global_device_ids=true | all-gather | bytes 270336 | tf_op jit(solution)/shard_map/all_gather | solution.py:409
  414.6 63.2 %all-gather.6 = bf16[32,1,128]{2,1,0:T(2,128)(2,1)S(1)} all-gather(bf16[1,1,128]{2,1,0:T(2,128)(2,1)S(1)} %bitcast.1172), channel_id=1, replica_groups=mesh['batch'=4,'seq'=8] {'batch','seq'}, dimensions={0}, use_global_device_ids=true | all-gather | bytes 8448 | tf_op jit(solution)/shard_map/all_gather | solution.py:416
  479.6 38.8 %all-gather.31.cloned.1.call-done = f32[8,64,1024]{2,1,0:T(8,128)} async-done(((f32[1,64,1024]{2,1,0:T(8,128)}), f32[8,64,1024]{2,1,0:T(8,128)}) %all-gather.31.cloned.1.call-update) | async-done | bytes 2097168 | tf_op jit(solution)/shard_map/all_gather | solution.py:17
  518.5 50.3 %all-gather.39.cloned.1.call-done = f32[8,64,1024]{2,1,0:T(8,128)} async-done(((f32[1,64,1024]{2,1,0:T(8,128)}), f32[8,64,1024]{2,1,0:T(8,128)}) %all-gather.39.cloned.1.call-update) | async-done | bytes 2097168 | tf_op jit(solution)/shard_map/all_gather | solution.py:17
  568.8 49.8 %all-gather.41.cloned.1.call-done = f32[8,64,1024]{2,1,0:T(8,128)} async-done(((f32[1,64,1024]{2,1,0:T(8,128)}), f32[8,64,1024]{2,1,0:T(8,128)}) %all-gather.41.cloned.1.call-update) | async-done | bytes 2097168 | tf_op jit(solution)/shard_map/all_gather | solution.py:17
  618.7 49.8 %all-gather.43.cloned.1.call-done = f32[8,64,1024]{2,1,0:T(8,128)} async-done(((f32[1,64,1024]{2,1,0:T(8,128)}), f32[8,64,1024]{2,1,0:T(8,128)}) %all-gather.43.cloned.1.call-update) | async-done | bytes 2097168 | tf_op jit(solution)/shard_map/all_gather | solution.py:17
  668.5 49.9 %all-gather.45.cloned.1.call-done = f32[8,64,1024]{2,1,0:T(8,128)} async-done(((f32[1,64,1024]{2,1,0:T(8,128)}), f32[8,64,1024]{2,1,0:T(8,128)}) %all-gather.45.cloned.1.call-update) | async-done | bytes 2097168 | tf_op jit(solution)/shard_map/all_gather | solution.py:17
  722.9 69.0 %while.261 = (s32[]{:T(128)}, f32[4,256,256]{2,1,0:T(8,128)}, s32[4]{0:T(128)S(1)}, f32[16,64,1024]{1,0,2:T(8,128)}, f32[16,64,1024]{1,0,2:T(8,128)}, /*index=5*...) while((s32[]{:T(128)}, f32[4,256,256]{2,1,0:T(8,128)}, ...), condition=%wide.region_11.12_spmd, body=%wide.region_10.11_spmd.sunk | while | flops 102301696 | bytes 15206599 | solution.py:172
  792.9 70.9 %while.264 = (s32[]{:T(128)}, f32[4,256,256]{2,1,0:T(8,128)}, s32[4]{0:T(128)S(1)}, f32[16,64,1024]{1,0,2:T(8,128)}, f32[16,64,1024]{1,0,2:T(8,128)}, /*index=5*...) while((s32[]{:T(128)}, f32[4,256,256]{2,1,0:T(8,128)}, ...), condition=%wide.region_23.24_spmd, body=%wide.region_22.23_spmd.sunk | while | flops 102301696 | bytes 15206599 | solution.py:172
  868.4 69.4 %while.267 = (s32[]{:T(128)}, f32[4,256,256]{2,1,0:T(8,128)}, s32[4]{0:T(128)S(1)}, f32[16,64,1024]{1,0,2:T(8,128)}, f32[16,64,1024]{1,0,2:T(8,128)}, /*index=5*...) while((s32[]{:T(128)}, f32[4,256,256]{2,1,0:T(8,128)}, ...), condition=%wide.region_35.36_spmd, body=%wide.region_34.35_spmd.sunk | while | flops 102301696 | bytes 15206599 | solution.py:172
  940.2 69.9 %while.258 = (s32[]{:T(128)}, f32[4,256,256]{1,2,0:T(8,128)}, s32[4]{0:T(128)S(1)}, f32[16,64,1024]{1,0,2:T(8,128)}, f32[16,64,1024]{1,0,2:T(8,128)}, /*index=5*...) while((s32[]{:T(128)}, f32[4,256,256]{1,2,0:T(8,128)}, ...), condition=%wide.region_3.4_spmd, body=%wide.region_2.3_spmd.sunk | while | flops 102301696 | bytes 15730887 | solution.py:172
  1155.4 108.0 %while.268 = (s32[]{:T(128)}, f32[4,64,256]{1,2,0:T(8,128)}, f32[4,64,256]{1,2,0:T(8,128)}, f32[4,64,256]{1,2,0:T(8,128)}, f32[4,64,256]{1,2,0:T(8,128)}, /*inde...) while((s32[]{:T(128)}, f32[4,64,256]{1,2,0:T(8,128)}, ...), condition=%wide.region_45.46_spmd, body=%wide.region_40.45_spmd.sunk | while | flops 205455360 | bytes 37750140 | solution.py:172
  1282.4 111.3 %while.271 = (s32[]{:T(128)}, f32[4,64,256]{1,2,0:T(8,128)}, f32[4,64,256]{1,2,0:T(8,128)}, f32[4,64,256]{1,2,0:T(8,128)}, f32[4,64,256]{1,2,0:T(8,128)}, /*inde...) while((s32[]{:T(128)}, f32[4,64,256]{1,2,0:T(8,128)}, ...), condition=%wide.region_59.60_spmd, body=%wide.region_54.59_spmd.sunk | while | flops 205455360 | bytes 29361480 | solution.py:172
  1412.6 110.9 %while.274 = (s32[]{:T(128)}, f32[4,64,256]{1,2,0:T(8,128)S(1)}, f32[4,64,256]{1,2,0:T(8,128)}, f32[4,64,256]{1,2,0:T(8,128)}, f32[4,64,256]{1,2,0:T(8,128)}, /*...) while((s32[]{:T(128)}, f32[4,64,256]{1,2,0:T(8,128)S(1)}, ...), condition=%wide.region_73.74_spmd, body=%wide.region_68.73_spmd.sunk | while | flops 205455360 | bytes 29492552 | solution.py:172
  1614.2 21.7 add_add_fusion
  1681.2 49.2 %all-gather.47.cloned.1.call-done = f32[512,1024]{1,0:T(8,128)} async-done(((f32[64,1024]{1,0:T(8,128)}), f32[512,1024]{1,0:T(8,128)}) %all-gather.47.cloned.1.call-update) | async-done | bytes 2097168 | tf_op jit(solution)/shard_map/all_gather | solution.py:17
  1730.4 50.0 %all-gather.49.cloned.1.call-done = f32[512,1024]{1,0:T(8,128)} async-done(((f32[64,1024]{1,0:T(8,128)}), f32[512,1024]{1,0:T(8,128)}) %all-gather.49.cloned.1.call-update) | async-done | bytes 2097168 | tf_op jit(solution)/shard_map/all_gather | solution.py:17
  1790.9 39.5 %all-gather.51.cloned.1.call-done = f32[512,1024]{1,0:T(8,128)} async-done(((f32[64,1024]{1,0:T(8,128)}), f32[512,1024]{1,0:T(8,128)}) %all-gather.51.cloned.1.call-update) | async-done | bytes 2097168 | tf_op jit(solution)/shard_map/all_gather | solution.py:17
  1830.4 50.0 %all-gather.53.cloned.1.call-done = f32[512,1024]{1,0:T(8,128)} async-done(((f32[64,1024]{1,0:T(8,128)}), f32[512,1024]{1,0:T(8,128)}) %all-gather.53.cloned.1.call-update) | async-done | bytes 2097168 | tf_op jit(solution)/shard_map/all_gather | solution.py:17
  1890.9 39.5 %all-gather.55.cloned.1.call-done = f32[512,1024]{1,0:T(8,128)} async-done(((f32[64,1024]{1,0:T(8,128)}), f32[512,1024]{1,0:T(8,128)}) %all-gather.55.cloned.1.call-update) | async-done | bytes 2097168 | tf_op jit(solution)/shard_map/all_gather | solution.py:17
  1930.4 50.0 %all-gather.57.cloned.1.call-done = f32[512,1024]{1,0:T(8,128)} async-done(((f32[64,1024]{1,0:T(8,128)}), f32[512,1024]{1,0:T(8,128)}) %all-gather.57.cloned.1.call-update) | async-done | bytes 2097168 | tf_op jit(solution)/shard_map/all_gather | solution.py:17
  1995.0 69.0 %while.270 = (s32[]{:T(128)}, f32[4,256,256]{2,1,0:T(8,128)}, s32[4]{0:T(128)S(1)}, f32[16,64,1024]{1,0,2:T(8,128)}, f32[16,64,1024]{1,0,2:T(8,128)}, /*index=5*...) while((s32[]{:T(128)}, f32[4,256,256]{2,1,0:T(8,128)}, ...), condition=%wide.region_49.50_spmd, body=%wide.region_48.49_spmd.sunk | while | flops 102301696 | bytes 15206599 | solution.py:172
  2071.7 69.3 %while.273 = (s32[]{:T(128)}, f32[4,256,256]{2,1,0:T(8,128)}, s32[4]{0:T(128)S(1)}, f32[16,64,1024]{1,0,2:T(8,128)}, f32[16,64,1024]{1,0,2:T(8,128)}, /*index=5*...) while((s32[]{:T(128)}, f32[4,256,256]{2,1,0:T(8,128)}, ...), condition=%wide.region_63.64_spmd, body=%wide.region_62.63_spmd.sunk | while | flops 102301696 | bytes 15206599 | solution.py:172
  2148.7 69.2 %while.276 = (s32[]{:T(128)}, f32[4,256,256]{2,1,0:T(8,128)}, s32[4]{0:T(128)S(1)}, f32[16,64,1024]{1,0,2:T(8,128)}, f32[16,64,1024]{1,0,2:T(8,128)}, /*index=5*...) while((s32[]{:T(128)}, f32[4,256,256]{2,1,0:T(8,128)}, ...), condition=%wide.region_77.78_spmd, body=%wide.region_76.77_spmd.sunk | while | flops 102301696 | bytes 15206599 | solution.py:172
  2246.1 44.7 %all-reduce.17 = (f32[1024]{0:T(1024)S(1)}, f32[1024]{0:T(1024)S(1)}, f32[1024]{0:T(1024)S(1)}, f32[2048]{0:T(1024)S(1)}, f32[1024]{0:T(1024)S(1)}, /*index=5*/f...) all-reduce(f32[1024]{0:T(1024)S(1)} %add_add_fusion.10, ...), channel_id=8, replica_groups=mesh['batch'=4,'seq'=8] {'batch','seq'}, use_global_device_ids=true, to_apply=%region_83.84.clone | all-reduce | flops 12288 | bytes 98304
  2301.6 226.7 %reduce-scatter.6.cloned.1.call-done = f32[32,4096]{1,0:T(8,128)} async-done(((f32[1024,4096]{1,0:T(8,128)}), f32[32,4096]{1,0:T(8,128)}) %reduce-scatter.6.cloned.1.call-update) | async-done | bytes 524304 | tf_op jit(solution)/shard_map/reduce_scatter | solution.py:442
  2528.2 360.3 %reduce-scatter.8.cloned.1.call-done = f32[128,1024]{1,0:T(8,128)} async-done(((f32[4096,1024]{1,0:T(8,128)}), f32[128,1024]{1,0:T(8,128)}) %reduce-scatter.8.cloned.1.call-update) | async-done | bytes 524304 | tf_op jit(solution)/shard_map/reduce_scatter | solution.py:444
  (1289 shorter events, 1458.9 us)
Async XLA Ops:
  7.2 472.4 %all-gather.25.cloned.1.call-start = ((), (), s32[]{:S(2)}) async-start(), calls=%async_computation.3 | async-start | bytes 2359296 | tf_op jit(solution)/shard_map/all_gather | solution.py:17
  7.3 711.3 %copy-start.175 = (f32[64]{0:T(128)}, f32[64]{0:T(128)S(1)}, u32[]{:S(2)}) copy-start(f32[64]{0:T(128)S(1)} %get-tuple-element.2288) | copy-start | bytes 772
  7.3 711.3 %copy-start.190 = (f32[64]{0:T(128)}, f32[64]{0:T(128)S(1)}, u32[]{:S(2)}) copy-start(f32[64]{0:T(128)S(1)} %get-tuple-element.2287) | copy-start | bytes 772
  56.4 662.1 %copy-start.147 = (f32[1024]{0:T(1024)}, f32[1024]{0:T(1024)S(1)}, u32[]{:S(2)}) copy-start(f32[1024]{0:T(1024)S(1)} %convert_element_type.278) | copy-start | bytes 12292
  56.4 662.1 %copy-start.149 = (f32[1024]{0:T(1024)}, f32[1024]{0:T(1024)S(1)}, u32[]{:S(2)}) copy-start(f32[1024]{0:T(1024)S(1)} %get-tuple-element.2267) | copy-start | bytes 12292
  56.5 662.1 %copy-start.151 = (f32[1024]{0:T(1024)}, f32[1024]{0:T(1024)S(1)}, u32[]{:S(2)}) copy-start(f32[1024]{0:T(1024)S(1)} %get-tuple-element.2268) | copy-start | bytes 12292
  58.9 1071.4 %copy-start.153 = (f32[1024]{0:T(1024)}, f32[1024]{0:T(1024)S(1)}, u32[]{:S(2)}) copy-start(f32[1024]{0:T(1024)S(1)} %convert_element_type.276) | copy-start | bytes 12292
  59.2 277.2 %copy-start.183 = (f32[256]{0:T(256)}, f32[256]{0:T(256)S(1)}, u32[]{:S(2)}) copy-start(f32[256]{0:T(256)S(1)} %get-tuple-element.2283) | copy-start | bytes 3076
  312.5 167.2 %all-gather.27.cloned.1.call-start = ((), (), s32[]{:S(2)}) async-start(), calls=%async_computation.4 | async-start | bytes 2359296 | tf_op jit(solution)/shard_map/all_gather | solution.py:17
  313.2 166.4 %all-gather.29.cloned.1.call-start = ((), (), s32[]{:S(2)}) async-start(), calls=%async_computation.5 | async-start | bytes 2359296 | tf_op jit(solution)/shard_map/all_gather | solution.py:17
  314.0 204.5 %all-gather.31.cloned.1.call-start = ((), (), s32[]{:S(2)}) async-start(), calls=%async_computation.6 | async-start | bytes 2359296 | tf_op jit(solution)/shard_map/all_gather | solution.py:17
  314.5 254.3 %all-gather.39.cloned.1.call-start = ((), (), s32[]{:S(2)}) async-start(), calls=%async_computation.10 | async-start | bytes 2359296 | tf_op jit(solution)/shard_map/all_gather | solution.py:17
  315.1 303.5 %all-gather.41.cloned.1.call-start = ((), (), s32[]{:S(2)}) async-start(), calls=%async_computation.11 | async-start | bytes 2359296 | tf_op jit(solution)/shard_map/all_gather | solution.py:17
  315.7 352.8 %all-gather.43.cloned.1.call-start = ((), (), s32[]{:S(2)}) async-start(), calls=%async_computation.12 | async-start | bytes 2359296 | tf_op jit(solution)/shard_map/all_gather | solution.py:17
  316.4 402.0 %all-gather.45.cloned.1.call-start = ((), (), s32[]{:S(2)}) async-start(), calls=%async_computation.13 | async-start | bytes 2359296 | tf_op jit(solution)/shard_map/all_gather | solution.py:17
  317.2 723.7 %all-gather.33.cloned.1.call-start = ((), (), s32[]{:S(2)}) async-start(), calls=%async_computation.7 | async-start | bytes 4325376 | tf_op jit(solution)/shard_map/all_gather | solution.py:411
  317.9 733.6 %all-gather.35.cloned.1.call-start = ((), (), s32[]{:S(2)}) async-start(), calls=%async_computation.8 | async-start | bytes 8650752 | tf_op jit(solution)/shard_map/all_gather | solution.py:415
  318.5 750.3 %all-gather.37.cloned.1.call-start = ((), (), s32[]{:S(2)}) async-start(), calls=%async_computation.9 | async-start | bytes 8650752 | tf_op jit(solution)/shard_map/all_gather | solution.py:417
  319.2 1360.5 %all-reduce.21.cloned.1.call-start = ((), (), s32[]{:S(2)}) async-start(), calls=%async_computation.23 | async-start | bytes 2097152
  336.5 700.0 %copy-start.49 = (f32[257,1024]{1,0:T(8,128)}, f32[257,1024]{1,0:T(8,128)S(1)}, u32[]{:S(2)}) copy-start(f32[257,1024]{1,0:T(8,128)S(1)} %fusion.559) | copy-start | bytes 3158020
  414.2 304.4 %copy-start.130 = (bf16[1,1024,64]{1,2,0:T(8,128)(2,1)}, bf16[1,1024,64]{1,2,0:T(8,128)(2,1)S(1)}, u32[]{:S(2)}) copy-start(bf16[1,1024,64]{1,2,0:T(8,128)(2,1)S(1)} %copy.357) | copy-start | bytes 393220
  414.5 304.1 %copy-start.132 = (bf16[1,1024,64]{1,2,0:T(8,128)(2,1)}, bf16[1,1024,64]{1,2,0:T(8,128)(2,1)S(1)}, u32[]{:S(2)}) copy-start(bf16[1,1024,64]{1,2,0:T(8,128)(2,1)S(1)} %copy.356) | copy-start | bytes 393220
  414.5 621.9 %copy-start.157 = (f32[1024]{0:T(1024)}, f32[1024]{0:T(1024)S(1)}, u32[]{:S(2)}) copy-start(f32[1024]{0:T(1024)S(1)} %convert_element_type.281) | copy-start | bytes 12292
  1542.2 188.2 %all-gather.47.cloned.1.call-start = ((), (), s32[]{:S(2)}) async-start(), calls=%async_computation.17 | async-start | bytes 2359296 | tf_op jit(solution)/shard_map/all_gather | solution.py:17
  1543.0 237.4 %all-gather.49.cloned.1.call-start = ((), (), s32[]{:S(2)}) async-start(), calls=%async_computation.18 | async-start | bytes 2359296 | tf_op jit(solution)/shard_map/all_gather | solution.py:17
  1543.6 286.9 %all-gather.51.cloned.1.call-start = ((), (), s32[]{:S(2)}) async-start(), calls=%async_computation.19 | async-start | bytes 2359296 | tf_op jit(solution)/shard_map/all_gather | solution.py:17
  1544.1 336.3 %all-gather.53.cloned.1.call-start = ((), (), s32[]{:S(2)}) async-start(), calls=%async_computation.20 | async-start | bytes 2359296 | tf_op jit(solution)/shard_map/all_gather | solution.py:17
  1544.7 385.7 %all-gather.55.cloned.1.call-start = ((), (), s32[]{:S(2)}) async-start(), calls=%async_computation.21 | async-start | bytes 2359296 | tf_op jit(solution)/shard_map/all_gather | solution.py:17
  1545.3 435.1 %all-gather.57.cloned.1.call-start = ((), (), s32[]{:S(2)}) async-start(), calls=%async_computation.22 | async-start | bytes 2359296 | tf_op jit(solution)/shard_map/all_gather | solution.py:17
  1545.9 755.7 %reduce-scatter.4.cloned.1.call-start = ((), (), s32[]{:S(2)}) async-start(), calls=%async_computation.14 | async-start | bytes 8650752 | tf_op jit(solution)/shard_map/reduce_scatter | solution.py:438
  1554.0 974.2 %reduce-scatter.6.cloned.1.call-start = ((), (), s32[]{:S(2)}) async-start(), calls=%async_computation.15 | async-start | bytes 17301504 | tf_op jit(solution)/shard_map/reduce_scatter | solution.py:442
  1592.7 1295.9 %reduce-scatter.8.cloned.1.call-start = ((), (), s32[]{:S(2)}) async-start(), calls=%async_computation.16 | async-start | bytes 17301504 | tf_op jit(solution)/shard_map/reduce_scatter | solution.py:444
  (254 other events, 4886.8 us)
Sparse Core Ops, SparseCore 0:
  312.6 52.3 all-gather.24
  367.1 49.7 all-gather.26
  419.6 48.3 all-gather.28
  470.6 47.7 all-gather.30
  521.0 47.7 all-gather.38
  570.8 47.7 all-gather.40
  620.7 47.7 all-gather.42
  670.6 47.7 all-gather.44
  721.5 60.6 all-gather.32
  785.1 75.8 all-gather.34
  863.9 76.0 all-gather.36
  1542.4 137.3 all-reduce.20
  1682.1 48.2 all-gather.46
  1732.6 47.7 all-gather.48
  1782.6 47.7 all-gather.50
  1832.6 47.7 all-gather.52
  1882.6 47.7 all-gather.54
  1932.6 47.7 all-gather.56
  1983.4 182.7 reduce-scatter.3
  2169.0 359.1 reduce-scatter.5
  2531.2 357.2 reduce-scatter.7
where the time goes:
time: 2910 us; the launch traced here: 2900 us
  waiting for transfers between devices  1120 us (38%)
  matrix products  1030 us (35%)
  local copies, waits for them, and re-layouts  325 us (11%)
  blocking collectives  223 us (8%)
  other arithmetic  142 us (5%)
  loops' own time  40.2 us (1%)
    all_gather x14, waiting for transfers between devices, prefix(): gathered = jax.tree.map(lambda a: lax.all_gather(a, axis), part)  517 us
    reduce_scatter x1, waiting for transfers between devices, per_device(): lax.psum_scatter(local_sums[10], ('batch', 'seq'), scatter_dimension=0, t...  360 us
    reduce_scatter x1, waiting for transfers between devices, per_device(): lax.psum_scatter(local_sums[8], ('batch', 'seq'), scatter_dimension=0, ti...  227 us
    dot_general x36, matrix products, project_block(): inner_im = jnp.einsum('ijh,jnh->inh', folded, near_im, precision=highest)  203 us
    dot_general x28, matrix products, expand_block(): jnp.einsum('inh,jnh->ijh', lifted[0], near_re, precision=highest)  184 us
    dot_general x28, matrix products, expand_block(): jnp.einsum('inh,jnh->ijh', lifted[1], near_im, precision=highest)  184 us
    dot_general x36, matrix products, project_block(): inner_re = jnp.einsum('ijh,jnh->inh', folded, near_re, precision=highest)  159 us
    unnamed x2, blocking collectives  87.1 us
  transfers between devices with their start and end apart: 21, of which 14 were waited for; matrix products, arithmetic and copies ran while one was open for 27% of the time, Pallas kernels for 0%

commit v1 on v0

v1 whole, which is shorter than its diff:
```python
import functools
import math

import jax
import jax.numpy as jnp
import numpy as np
from jax import lax
from jax.experimental import pallas as pl
from jax.experimental.pallas import tpu as pltpu
from jax.sharding import PartitionSpec as P

f32 = jnp.float32
bf16 = jnp.bfloat16
norm_eps = 1e-05
near_span = 64
vmem_limit = 60 * 1024 * 1024
gelu_scale = math.sqrt(2.0 / math.pi)
gelu_cubic = 0.044715


def after(value, *tokens):
    return jax.tree.map(lambda v: lax.optimization_barrier((v, tokens))[0], value)


together = lax.optimization_barrier


def bits_of(size):
    count = size.bit_length() - 1
    if (1 << count) != size:
        raise ValueError("axis size")
    return count


def reverse_bits(value, count):
    result = 0
    for bit in range(count):
        result = result | (((value >> bit) & 1) << (count - 1 - bit))
    return result


def swap(value, axis, bit):
    size = lax.axis_size(axis)
    return lax.ppermute(value, axis, [(i, i ^ bit) for i in range(size)])


def gather_first(shard):
    return swap(shard[None], "seq", lax.axis_size("seq") // 2)


def gather_direct(shard):
    size = lax.axis_size("seq")
    return [swap(shard[None], "seq", bits) for bits in (size // 2, size // 4, size // 2 + size // 4)]


def gather_more(joined, lowest):
    size = lax.axis_size("seq")
    while joined.shape[0] << lowest < size:
        bit = size // joined.shape[0] // 2
        joined = jnp.concatenate([joined, swap(joined, "seq", bit)], axis=0)
    return joined


class Sum:
    def __init__(self, *terms):
        self.terms = list(terms)

    def total(self, start=0, stop=None):
        values = [term[start:stop].astype(f32) for term in self.terms]
        return functools.reduce(lambda a, b: a + b, values)

    def upper(self):
        return self.total(self.terms[0].shape[0] // 2).astype(bf16)

    def keep(self, came):
        half = self.terms[0].shape[0] // 2
        self.terms = [term[:half] for term in self.terms] + [came]

    def add(self, came):
        self.terms.append(came)

    def middle(self):
        for bit in range(2, bits_of(lax.axis_size("seq")) - 1):
            self.keep(swap(self.upper(), "seq", 1 << bit))


def swap_batch(pieces, bit):
    return [swap(piece, "batch", 1 << bit) for piece in pieces]


def gather_batch(part):
    pieces = [part]
    for bit in reversed(range(bits_of(lax.axis_size("batch")))):
        pieces = pieces + swap_batch(pieces, bit)
    return pieces


def reduce_batch(value):
    for bit in range(bits_of(lax.axis_size("batch"))):
        half = value.shape[0] // 2
        value = value[:half] + swap(value[half:], "batch", 1 << bit)
    return value[0]


def exchange(parts):
    return lax.all_to_all(parts, "seq", 0, 0)


def gelu_parts(values):
    square = values * values
    tanh = jnp.tanh(gelu_scale * values * (1.0 + gelu_cubic * square))
    half = 0.5 * (1.0 + tanh)
    return tanh, square, half


def gelu_value(values):
    return values * gelu_parts(values)[2]


def gelu_slope(values):
    tanh, square, half = gelu_parts(values)
    return half + 0.5 * values * (1.0 - tanh * tanh) * (
        gelu_scale * (1.0 + 3.0 * gelu_cubic * square)
    )


def gelu_both(values):
    tanh, square, half = gelu_parts(values)
    slope = half + 0.5 * values * (1.0 - tanh * tanh) * (
        gelu_scale * (1.0 + 3.0 * gelu_cubic * square)
    )
    return values * half, slope


def layer_stats(values):
    centered = values - jnp.mean(values, axis=-1, keepdims=True)
    scale_inv = lax.rsqrt(jnp.mean(centered * centered, axis=-1, keepdims=True) + norm_eps)
    return centered * scale_inv, scale_inv


def norm_back(grad_normed, normed, scale_inv):
    first_mean = jnp.mean(grad_normed, axis=-1, keepdims=True)
    second_mean = jnp.mean(grad_normed * normed, axis=-1, keepdims=True)
    return scale_inv * (grad_normed - first_mean - normed * second_mean)


def dot(left, right):
    return jnp.dot(left, right, preferred_element_type=f32)


def dot_left_t(left, right):
    return lax.dot_general(left, right, (((0,), (0,)), ((), ())), preferred_element_type=f32)


def dot_right_t(left, right):
    return lax.dot_general(left, right, (((1,), (1,)), ((), ())), preferred_element_type=f32)


def stack_split(values):
    high = values.astype(bf16)
    low = (values - high.astype(f32)).astype(bf16)
    return jnp.concatenate([high, high, low], axis=0)


def table_split(table):
    high = table.astype(jnp.bfloat16)
    low = (table - high.astype(np.float64)).astype(jnp.bfloat16)
    return np.concatenate([high, low, high], axis=1)


def transform_tables(span):
    freqs = np.arange(span, dtype=np.float64) + 0.5
    phase = 2.0 * math.pi / (2 * span) * freqs[:, None] * np.arange(span, dtype=np.float64)[None]
    forward = np.concatenate([np.cos(phase), -np.sin(phase)], axis=0)
    backward = np.concatenate([np.cos(phase).T, -np.sin(phase).T], axis=1) / span
    return table_split(forward), table_split(backward)


def loop(count, body):
    if count <= 8:
        for index in range(count):
            body(index)
    else:
        lax.fori_loop(0, count, lambda index, carry: (body(index), carry)[1], 0)


def sum_loop(first, last, body, init):
    if isinstance(first, int) and isinstance(last, int):
        for index in range(first, last):
            init = body(index, init)
        return init
    return lax.fori_loop(first, last, body, init)


def full_spec(shape, buffered=True):
    zeros = (0,) * len(shape)
    if buffered:
        return pl.BlockSpec(shape, lambda *_: zeros, pipeline_mode=pl.Buffered(1))
    return pl.BlockSpec(shape, lambda *_: zeros)


def parted(parts, span, chan):
    return pl.BlockSpec((parts, span, chan), lambda m, _: (0, m, 0))


def call(kernel, grid, meta, in_specs, operands, out_specs, out_shape, scratch, flops, name):
    return pl.pallas_call(
        kernel,
        grid_spec=pltpu.PrefetchScalarGridSpec(
            num_scalar_prefetch=1,
            grid=grid,
            in_specs=in_specs,
            out_specs=out_specs,
            scratch_shapes=scratch,
        ),
        out_shape=out_shape,
        compiler_params=pltpu.CompilerParams(
            vmem_limit_bytes=vmem_limit, dimension_semantics=("arbitrary",) * len(grid)
        ),
        cost_estimate=pl.CostEstimate(
            flops=int(flops * 0.02), bytes_accessed=int(flops * 0.02 / 400), transcendentals=0
        ),
        name=name,
    )(meta, *operands)


def norm_kernel(batch_bits, shard_rows, seq_size, meta, x_ref, extra_ref, out_ref, perm_ref):
    width = x_ref.shape[2]
    chan = out_ref.shape[-1]

    @pl.when(pl.program_id(0) == 0)
    def _():
        lane = lax.broadcasted_iota(jnp.int32, (width, width), 1)
        piece = (lane & (chan - 1)) // shard_rows
        source = (
            (reverse_bits(piece, batch_bits) ^ meta[0]) * seq_size + lane // chan
        ) * shard_rows + (lane & (shard_rows - 1))
        row = lax.broadcasted_iota(jnp.int32, (width, width), 0)
        perm_ref[...] = jnp.where(row == source, 1.0, 0.0).astype(bf16)
        for d in range(out_ref.shape[0]):
            out_ref[d, pl.ds(out_ref.shape[1] - extra_ref.shape[0], extra_ref.shape[0]), :] = (
                extra_ref[...]
            )

    span = x_ref.shape[1]
    rows = pl.ds(pl.multiple_of(pl.program_id(0) * span, span), span)
    normed, _ = layer_stats(x_ref[0].astype(f32))
    spread = dot(normed.astype(bf16), perm_ref[...]).astype(bf16)
    for d in range(out_ref.shape[0]):
        out_ref[d, rows, :] = spread[:, d * chan : (d + 1) * chan]


def norm_call(meta, x, extra, batch_bits, shard_rows, parts):
    micro, span, width = x.shape
    chan = width // parts
    return call(
        functools.partial(norm_kernel, batch_bits, shard_rows, parts),
        (micro,),
        meta,
        [pl.BlockSpec((1, span, width), lambda m, _: (m, 0, 0)), full_spec(extra.shape)],
        (x, extra),
        [full_spec((parts, micro * span + extra.shape[0], chan)), full_spec((width, width))],
        [
            jax.ShapeDtypeStruct((parts, micro * span + extra.shape[0], chan), bf16),
            jax.ShapeDtypeStruct((width, width), bf16),
        ],
        [],
        2 * micro * span * width * width,
        "norm_one",
    )


def kernel_kernel(meta, lift_re, lift_im, near_re, near_im, fwd_ref, out_ref, series, spec):
    modes, span_near, chan = near_re.shape
    far_count = lift_re.shape[1]
    blocks, _, span, _ = out_ref.shape
    group = 2

    def far_group(index, carry):
        def one_mode(n, acc):
            near_r, near_i = near_re[n], near_im[n]
            result = []
            for g in range(group):
                row = index * group + g
                a = lift_re[n, pl.ds(row, 1), :]
                b = lift_im[n, pl.ds(row, 1), :]
                result.append(acc[g] + (a * near_r - b * near_i))
            return tuple(result)

        zero = jnp.zeros((span_near, chan), f32)
        acc = lax.fori_loop(0, modes, one_mode, (zero,) * group, unroll=4)
        for g in range(group):
            start = pl.multiple_of((index * group + g) * span_near, span_near)
            series[pl.ds(start, span_near), :] = acc[g]
        return carry

    lax.fori_loop(0, far_count // group, far_group, 0)

    def one_pair(index):
        first = index * 2 * span
        pair = [series[pl.ds(first + k * span, span), :] for k in range(2)]
        both = dot(fwd_ref[...], stack_split(jnp.concatenate(pair, axis=1)))
        for k in range(2):
            spec[index * 2 + k] = both[:, k * chan : (k + 1) * chan]

    loop(blocks // 2, one_pair)
    rows = lax.broadcasted_iota(jnp.int32, (span, chan), 0)
    sign = 1.0 - 2.0 * (rows & 1).astype(f32)

    def one_block(d):
        real, imag = spec[d, :span], spec[d, span:]
        before = d - 1 if isinstance(d, int) else jnp.maximum(d - 1, 0)
        if isinstance(d, int) and d == 0:
            out_ref[0, 0], out_ref[0, 1] = real, imag
            return
        keep = 1.0 if isinstance(d, int) else jnp.where(d > 0, 1.0, 0.0)
        out_ref[d, 0] = real - keep * (sign * spec[before, span:])
        out_ref[d, 1] = imag + keep * (sign * spec[before, :span])

    loop(blocks, one_block)


def kernel_call(meta, lift, near, fwd, blocks, span):
    chan = near[0].shape[-1]
    operands = (lift[0], lift[1], near[0], near[1], fwd)
    return call(
        kernel_kernel,
        (1,),
        meta,
        [full_spec(a.shape) for a in operands],
        operands,
        full_spec((blocks, 2, span, chan)),
        jax.ShapeDtypeStruct((blocks, 2, span, chan), f32),
        [pltpu.VMEM((blocks * span, chan), f32), pltpu.VMEM((blocks, 2 * span, chan), f32)],
        1.1e10,
        "state_kernel",
    )


def mask_of(meta, m, block, span, chan):
    rows = block * span + lax.broadcasted_iota(jnp.int32, (span, chan), 0)
    return (rows < meta[1 + m]).astype(f32)


freq_tile = 64


def conv_kernel(
    meta,
    normed_ref,
    vec_ref,
    spec_ref,
    fwd_ref,
    inv_ref,
    drive_ref,
    mixed_ref,
    out_ref,
    drive,
    spectrum,
):
    m = pl.program_id(0)
    blocks, span, chan = drive.shape
    gain, bias, skip = vec_ref[0:1, :], vec_ref[1:2, :], vec_ref[2:3, :]

    def drive_pair(pair):
        values = []
        for k in range(2):
            block = 2 * pair + k
            normed = normed_ref[block].astype(f32)
            u = mask_of(meta, m, block, span, chan) * (normed * gain + bias)
            drive[block] = u
            values.append(u)
        both = dot(fwd_ref[...], stack_split(jnp.concatenate(values, axis=1)))
        for k in range(2):
            drive_ref[0, 2 * pair + k] = both[:, k * chan : (k + 1) * chan]

    loop(blocks // 2, drive_pair)

    def one_pair(index):
        for k in range(2):
            i = index * 2 + k

            def one_tile(tile, carry):
                low = pl.ds(pl.multiple_of(tile * freq_tile, freq_tile), freq_tile)
                high = pl.ds(pl.multiple_of(span + tile * freq_tile, freq_tile), freq_tile)

                def one_term(j, acc):
                    xr, xi = drive_ref[0, j, low], drive_ref[0, j, high]
                    gr, gi = spec_ref[i - j, 0, low], spec_ref[i - j, 1, low]
                    return (acc[0] + (xr * gr - xi * gi), acc[1] + (xr * gi + xi * gr))

                zero = jnp.zeros((freq_tile, chan), f32)
                acc = sum_loop(0, i + 1, one_term, (zero, zero))
                spectrum[k, low] = acc[0]
                spectrum[k, high] = acc[1]
                return carry

            lax.fori_loop(0, span // freq_tile, one_tile, 0)
        both = dot(
            inv_ref[...], stack_split(jnp.concatenate([spectrum[0], spectrum[1]], axis=1))
        )
        for k in range(2):
            i = index * 2 + k
            mixed = both[:, k * chan : (k + 1) * chan] + skip * drive[i]
            mixed_ref[0, i] = mixed
            out_ref[i] = gelu_value(mixed).astype(bf16)

    loop(blocks // 2, one_pair)


def conv_call(meta, micro, normed, vec, spec, fwd, inv):
    parts, _, chan = normed.shape
    span = spec.shape[2]
    wide = lambda rows: pl.BlockSpec((1, parts, rows, chan), lambda m, _: (m, 0, 0, 0))
    return call(
        conv_kernel,
        (micro,),
        meta,
        [parted(parts, span, chan)] + [full_spec(a.shape) for a in (vec, spec, fwd, inv)],
        (normed, vec, spec, fwd, inv),
        [wide(2 * span), wide(span), parted(parts, span, chan)],
        [
            jax.ShapeDtypeStruct((micro, parts, 2 * span, chan), f32),
            jax.ShapeDtypeStruct((micro, parts, span, chan), f32),
            jax.ShapeDtypeStruct((parts, micro * span, chan), bf16),
        ],
        [
            pltpu.VMEM((parts, span, chan), f32),
            pltpu.VMEM((2, 2 * span, chan), f32),
        ],
        1.5e10,
        "state_conv",
    )


def back_kernel(
    meta,
    grads_ref,
    normed_ref,
    drive_ref,
    mixed_ref,
    vec_ref,
    spec_ref,
    fwd_ref,
    inv_ref,
    extra_ref,
    out_ref,
    cross_ref,
    sums_ref,
    grad_mixed,
    grad_spec,
    spectrum,
):
    m = pl.program_id(0)
    blocks, span, chan = grad_mixed.shape
    gain, bias, skip = vec_ref[0:1, :], vec_ref[1:2, :], vec_ref[2:3, :]

    @pl.when(m == 0)
    def _():
        cross_ref[...] = jnp.zeros_like(cross_ref)
        sums_ref[...] = jnp.zeros_like(sums_ref)
        extra = extra_ref.shape[1]
        out_ref[:, pl.ds(out_ref.shape[1] - extra, extra), :] = extra_ref[...]

    def grad_pair(pair):
        values = []
        for k in range(2):
            block = 2 * pair + k
            normed = normed_ref[block].astype(f32)
            u = mask_of(meta, m, block, span, chan) * (normed * gain + bias)
            gm = grads_ref[block].astype(f32) * gelu_slope(mixed_ref[0, block])
            sums_ref[0:1, :] += jnp.sum(gm * u, axis=0, keepdims=True)
            grad_mixed[block] = gm
            values.append(gm)
        both = dot(fwd_ref[...], stack_split(jnp.concatenate(values, axis=1)))
        for k in range(2):
            grad_spec[2 * pair + k] = both[:, k * chan : (k + 1) * chan]

    loop(blocks // 2, grad_pair)

    def tiles_of(body):
        def one_tile(tile, carry):
            low = pl.ds(pl.multiple_of(tile * freq_tile, freq_tile), freq_tile)
            high = pl.ds(pl.multiple_of(span + tile * freq_tile, freq_tile), freq_tile)
            body(low, high)
            return carry

        lax.fori_loop(0, span // freq_tile, one_tile, 0)

    zero = jnp.zeros((freq_tile, chan), f32)

    def one_pair(index):
        for k in range(2):
            j = index * 2 + k

            def body(low, high):
                def one_term(i, acc):
                    mr, mi = grad_spec[i, low], grad_spec[i, high]
                    gr, gi = spec_ref[i - j, 0, low], spec_ref[i - j, 1, low]
                    return (acc[0] + (mr * gr + mi * gi), acc[1] + (mi * gr - mr * gi))

                acc = sum_loop(j, blocks, one_term, (zero, zero))
                spectrum[k, low] = acc[0]
                spectrum[k, high] = acc[1]

            tiles_of(body)
        both = dot(
            inv_ref[...], stack_split(jnp.concatenate([spectrum[0], spectrum[1]], axis=1))
        )
        for k in range(2):
            j = index * 2 + k
            grad_mixed[j] = both[:, k * chan : (k + 1) * chan] + skip * grad_mixed[j]

    loop(blocks // 2, one_pair)

    def finish(block):
        g = mask_of(meta, m, block, span, chan) * grad_mixed[block]
        normed = normed_ref[block].astype(f32)
        sums_ref[1:2, :] += jnp.sum(g * normed, axis=0, keepdims=True)
        sums_ref[2:3, :] += jnp.sum(g, axis=0, keepdims=True)
        out_ref[block, pl.ds(pl.multiple_of(m * span, span), span), :] = (g * gain).astype(bf16)

    loop(blocks, finish)

    def one_lag(d):
        def body(low, high):
            def one_term(j, acc):
                mr, mi = grad_spec[j + d, low], grad_spec[j + d, high]
                xr, xi = drive_ref[0, j, low], drive_ref[0, j, high]
                return (acc[0] + (mr * xr + mi * xi), acc[1] + (mi * xr - mr * xi))

            acc = sum_loop(0, blocks - d, one_term, (cross_ref[d, low], cross_ref[d, high]))
            cross_ref[d, low] = acc[0]
            cross_ref[d, high] = acc[1]

        tiles_of(body)

    loop(blocks, one_lag)


def back_call(meta, grads, normed, drive, mixed, vec, spec, fwd, inv, extra):
    parts, _, chan = normed.shape
    micro, _, span, _ = mixed.shape
    total = micro * span + extra.shape[1]
    mode = None if parts <= 8 else pl.Buffered(1)
    wide = lambda rows: pl.BlockSpec(
        (1, parts, rows, chan), lambda m, _: (m, 0, 0, 0), pipeline_mode=mode
    )
    return call(
        back_kernel,
        (micro,),
        meta,
        [parted(parts, span, chan)] * 2
        + [wide(2 * span), wide(span)]
        + [full_spec(a.shape) for a in (vec, spec, fwd, inv, extra)],
        (grads, normed, drive, mixed, vec, spec, fwd, inv, extra),
        [
            full_spec((parts, total, chan)),
            full_spec((parts, 2 * span, chan)),
            full_spec((8, chan)),
        ],
        [
            jax.ShapeDtypeStruct((parts, total, chan), bf16),
            jax.ShapeDtypeStruct((parts, 2 * span, chan), f32),
            jax.ShapeDtypeStruct((8, chan), f32),
        ],
        [
            pltpu.VMEM((parts, span, chan), f32),
            pltpu.VMEM((parts, 2 * span, chan), f32),
            pltpu.VMEM((2, 2 * span, chan), f32),
        ],
        2e10,
        "state_back",
    )


def modes_kernel(meta, cross_ref, far_re, far_im, near_re, near_im, inv_ref, out_ref, series):
    modes, span_near, chan = near_re.shape
    far_count = far_re.shape[1]
    blocks, double, _ = cross_ref.shape
    span = double // 2
    rows = lax.broadcasted_iota(jnp.int32, (span, chan), 0)
    sign = 1.0 - 2.0 * (rows & 1).astype(f32)

    def one_pair(index):
        pair = []
        for k in range(2):
            d = index * 2 + k
            real, imag = cross_ref[d, :span], cross_ref[d, span:]
            if isinstance(d, int):
                keep = 1.0 if d + 1 < blocks else 0.0
                after = min(d + 1, blocks - 1)
            else:
                keep = jnp.where(d + 1 < blocks, 1.0, 0.0)
                after = jnp.minimum(d + 1, blocks - 1)
            real = real + keep * (sign * cross_ref[after, span:])
            imag = imag - keep * (sign * cross_ref[after, :span])
            pair.append(jnp.concatenate([real, imag], axis=0))
        both = dot(inv_ref[...], stack_split(jnp.concatenate(pair, axis=1)))
        for k in range(2):
            series[pl.ds((index * 2 + k) * span, span), :] = both[:, k * chan : (k + 1) * chan]

    loop(blocks // 2, one_pair)
    group = 2

    def mode_group(index, carry):
        def one_far(i, acc):
            values = series[pl.ds(pl.multiple_of(i * span_near, span_near), span_near), :]
            result = []
            for g in range(group):
                n = index * group + g
                a = far_re[n, pl.ds(i, 1), :]
                b = far_im[n, pl.ds(i, 1), :]
                result.append((acc[g][0] + a * values, acc[g][1] + b * values))
            return tuple(result)

        zero = jnp.zeros((span_near, chan), f32)
        acc = lax.fori_loop(0, far_count, one_far, ((zero, zero),) * group, unroll=4)
        for g in range(group):
            n = index * group + g
            near_r, near_i = near_re[n], near_im[n]
            re, im = acc[g]
            out_ref[0, pl.ds(n, 1), :] = jnp.sum(re * near_r - im * near_i, axis=0, keepdims=True)
            out_ref[1, pl.ds(n, 1), :] = jnp.sum(re * near_i + im * near_r, axis=0, keepdims=True)
        return carry

    lax.fori_loop(0, modes // group, mode_group, 0)


def modes_call(meta, cross, far, near, inv):
    modes, _, chan = near[0].shape
    blocks, double, _ = cross.shape
    operands = (cross, far[0], far[1], near[0], near[1], inv)
    return call(
        modes_kernel,
        (1,),
        meta,
        [full_spec(a.shape) for a in operands],
        operands,
        full_spec((2, modes, chan)),
        jax.ShapeDtypeStruct((2, modes, chan), f32),
        [pltpu.VMEM((blocks * double // 2, chan), f32)],
        1.1e10,
        "state_modes",
    )


class Rows:
    def __init__(self, width, shard_rows, seq_size, batch_size, table):
        self.width = width
        self.shard_rows = shard_rows
        self.seq_size = seq_size
        self.batch_size = batch_size
        self.table = table
        self.piece_rows = shard_rows * seq_size
        self.by_block = shard_rows % 16 == 0

    def natural(self, meta, p, q):
        start = meta[self.table + p * self.seq_size + q] * self.shard_rows
        return pl.ds(pl.multiple_of(start, self.shard_rows), self.shard_rows)

    def order(self, meta, place):
        shape = (self.width, self.width)
        relative = lax.broadcasted_iota(jnp.int32, shape, 0)
        piece = relative // self.piece_rows
        position = (relative % self.piece_rows) // self.shard_rows
        shard = (reverse_bits(piece, bits_of(self.batch_size)) ^ meta[place + 1]) * self.seq_size
        shard = shard + (reverse_bits(position, bits_of(self.seq_size)) ^ meta[0])
        source = shard * self.shard_rows + relative % self.shard_rows
        return jnp.where(lax.broadcasted_iota(jnp.int32, shape, 1) == source, 1.0, 0.0).astype(bf16)

    def to_natural(self, meta, place, parts, target):
        if self.by_block:
            for p, part in enumerate(parts):
                for q in range(self.seq_size):
                    target[self.natural(meta, p, q), :] = part[
                        pl.ds(q * self.shard_rows, self.shard_rows), :
                    ]
        else:
            whole = jnp.concatenate([part[...] for part in parts], axis=0)
            target[...] = dot_left_t(self.order(meta, place), whole).astype(bf16)

    def to_relative(self, meta, place, value, scratch, store):
        if self.by_block:
            scratch[...] = value.astype(bf16)
        else:
            moved = dot(self.order(meta, place), value.astype(bf16))
        for p in range(self.batch_size):
            for q in range(self.seq_size):
                if self.by_block:
                    block = scratch[self.natural(meta, p, q), :]
                else:
                    start = (p * self.seq_size + q) * self.shard_rows
                    block = moved[start : start + self.shard_rows].astype(bf16)
                store(p, q, block)


def gate_kernel(pieces, order, meta, *refs):
    active_ref, x_ref, cot_ref, perm_ref, vec_ref, glu_bias_ref = refs[:6]
    weights = refs[6 : 6 + pieces]
    act_ref, resid_ref, gated_ref, norm_ref, norm_t_ref, cot_out, weight_scr = refs[6 + pieces :]
    m = pl.program_id(0)
    _, span, width = x_ref.shape
    micro = pl.num_programs(0)

    @pl.when(m == 0)
    def _():
        order.to_natural(meta, 1 + micro, weights, weight_scr)

    act = jnp.concatenate([active_ref[d] for d in range(active_ref.shape[0])], axis=1)
    act = dot_right_t(act, perm_ref[...]).astype(bf16)
    act_ref[0] = act
    gated = dot(act, weight_scr[...]) + glu_bias_ref[...]
    gated_ref[0] = gated
    residual = x_ref[0].astype(f32) + gated[:, :width] * jax.nn.sigmoid(gated[:, width:])
    resid_ref[0] = residual
    normed, _ = layer_stats(residual)
    norm_two = (normed * vec_ref[0:1, :] + vec_ref[1:2, :]).astype(bf16)
    norm_ref[...] = norm_two
    norm_t_ref[...] = norm_two.T
    rows = meta[1 + micro] + lax.broadcasted_iota(jnp.int32, (span, width), 0)
    cot_out[...] = jnp.where(rows < meta[1 + m], cot_ref[0].astype(f32), 0.0).astype(bf16)


def gate_call(meta, order, active, x, cot, perm, vec, glu_bias, weights):
    parts, _, chan = active.shape
    pieces = len(weights)
    micro, span, width = x.shape
    tokens = micro * span
    tile = lambda cols: pl.BlockSpec((1, span, cols), lambda m, _: (m, 0, 0))
    flat = pl.BlockSpec((span, width), lambda m, _: (m, 0))
    return call(
        functools.partial(gate_kernel, pieces, order),
        (micro,),
        meta,
        [parted(parts, span, chan), tile(width), tile(width)]
        + [full_spec(a.shape) for a in (perm, vec, glu_bias, *weights)],
        (active, x, cot, perm, vec, glu_bias, *weights),
        [
            tile(width),
            tile(width),
            tile(2 * width),
            flat,
            pl.BlockSpec((width, span), lambda m, _: (0, m)),
            flat,
        ],
        [
            jax.ShapeDtypeStruct((micro, span, width), bf16),
            jax.ShapeDtypeStruct((micro, span, width), f32),
            jax.ShapeDtypeStruct((micro, span, 2 * width), f32),
            jax.ShapeDtypeStruct((tokens, width), bf16),
            jax.ShapeDtypeStruct((width, tokens), bf16),
            jax.ShapeDtypeStruct((tokens, width), bf16),
        ],
        [pltpu.VMEM((width, 2 * width), bf16)],
        6 * tokens * width * width,
        "gated_unit",
    )


ff_block = 512


def ffn_kernel(pieces, batch_pieces, sub, order, out_table, place, meta, *refs):
    norm_ref, norm_t_ref, cot_ref, bias_ref = refs[:4]
    w_in = refs[4 : 4 + batch_pieces]
    w_out = refs[4 + batch_pieces : 4 + batch_pieces + pieces]
    rest = refs[4 + batch_pieces + pieces :]
    out_ref, back_ref, grad_bias = rest[:3]
    grad_out = rest[3 : 3 + pieces]
    grad_in = rest[3 + pieces : 3 + pieces + batch_pieces // 2]
    grad_in_send, in_scr, out_scr, grad_in_scr = rest[3 + pieces + batch_pieces // 2 :]
    k = pl.program_id(0)
    s = pl.program_id(1)
    order.to_natural(meta, place, w_in, in_scr)
    subs = ff_block // sub

    def sub_rows(t):
        return pl.ds(pl.multiple_of(meta[out_table + s * subs + t] * sub, sub), sub)

    for piece in range(pieces):

        @pl.when(k == piece)
        def _():
            for t in range(subs):
                out_scr[pl.ds(t * sub, sub), :] = w_out[piece][sub_rows(t), :]

    hidden = dot(norm_ref[...], in_scr[...]) + bias_ref[0]
    spread, slope = gelu_both(hidden)
    spread = spread.astype(bf16)
    grad_hidden = (dot_right_t(cot_ref[...], out_scr[...]) * slope).astype(bf16)
    grad_bias[0] = jnp.sum(grad_hidden.astype(f32), axis=0, keepdims=True)
    part_out = dot(spread, out_scr[...])
    part_back = dot_right_t(grad_hidden, in_scr[...])
    first = jnp.logical_and(k == 0, s == 0)

    @pl.when(first)
    def _():
        out_ref[...] = part_out
        back_ref[...] = part_back

    @pl.when(jnp.logical_not(first))
    def _():
        out_ref[...] += part_out
        back_ref[...] += part_back

    def store(p, q, block):
        if p < batch_pieces // 2:
            grad_in[p][q, 0] = block
        else:
            grad_in_send[p - batch_pieces // 2, q, 0] = block

    part_in = dot(norm_t_ref[...], grad_hidden)
    order.to_relative(meta, place, part_in, grad_in_scr, store)

    part = dot_left_t(spread, cot_ref[...]).astype(bf16)
    for piece in range(pieces):

        @pl.when(k == piece)
        def _():
            for t in range(subs):
                grad_out[piece][sub_rows(t), :] = part[t * sub : (t + 1) * sub, :]


def ffn_call(meta, order, out_table, place, base, column, norm, norm_t, cot, bias, w_in, w_out):
    pieces, batch_pieces = len(w_out), len(w_in)
    tokens, width = norm.shape
    piece_ff = w_out[0].shape[0]
    steps = piece_ff // ff_block
    sub = piece_ff // order.seq_size
    rows = order.piece_rows
    half = batch_pieces // 2
    block = lambda k, s, meta: meta[base + k] + s
    seq_size, low = order.seq_size, order.shard_rows
    kept = pl.BlockSpec(
        (seq_size, 1, low, ff_block), lambda k, s, meta: (0, meta[column + k], 0, s)
    )
    sent = pl.BlockSpec(
        (half, seq_size, 1, low, ff_block), lambda k, s, meta: (0, 0, meta[column + k], 0, s)
    )
    outs = call(
        functools.partial(ffn_kernel, pieces, batch_pieces, sub, order, out_table, place),
        (pieces, steps),
        meta,
        [full_spec(a.shape) for a in (norm, norm_t, cot)]
        + [pl.BlockSpec((1, 1, ff_block), lambda k, s, meta: (block(k, s, meta), 0, 0))]
        + [
            pl.BlockSpec((rows, ff_block), lambda k, s, meta: (0, block(k, s, meta)))
            for _ in w_in
        ]
        + [full_spec(a.shape) for a in w_out],
        (norm, norm_t, cot, bias, *w_in, *w_out),
        [
            full_spec((tokens, width)),
            full_spec((tokens, width)),
            pl.BlockSpec((1, 1, ff_block), lambda k, s, meta: (meta[column + k] * steps + s, 0, 0)),
        ]
        + [full_spec(a.shape) for a in w_out]
        + [kept] * half
        + [sent],
        [
            jax.ShapeDtypeStruct((tokens, width), f32),
            jax.ShapeDtypeStruct((tokens, width), f32),
            jax.ShapeDtypeStruct((pieces * steps, 1, ff_block), f32),
        ]
        + [jax.ShapeDtypeStruct(a.shape, bf16) for a in w_out]
        + [jax.ShapeDtypeStruct((seq_size, pieces, low, piece_ff), bf16)] * half
        + [jax.ShapeDtypeStruct((half, seq_size, pieces, low, piece_ff), bf16)],
        [
            pltpu.VMEM((width, ff_block), bf16),
            pltpu.VMEM((ff_block, width), bf16),
            pltpu.VMEM((width, ff_block), bf16),
        ],
        12 * tokens * width * piece_ff * pieces,
        "feed_forward",
    )
    split = 3 + pieces
    return outs[0], outs[1], outs[2], outs[3:split], outs[split:-1], outs[-1]


def gate_back_kernel(pieces, halves, order, meta, *refs):
    ffn = refs[:halves]
    back = refs[halves : 2 * halves]
    resid_ref, gated_ref, act_ref, cot_ref, perm_ref, vec_ref = refs[2 * halves : 2 * halves + 6]
    weights = refs[2 * halves + 6 : 2 * halves + 6 + pieces]
    rest = refs[2 * halves + 6 + pieces :]
    out_ref, grad_resid_ref, glu_bias_ref, sums_ref, moved_ref = rest[:5]
    grad_keep = rest[5 : 5 + pieces // 2]
    grad_send, weight_scr, gated_scr, act_scr, grad_scr = rest[5 + pieces // 2 :]
    m = pl.program_id(0)
    count = pl.num_programs(0)
    span, width = cot_ref.shape

    @pl.when(m == 0)
    def _():
        glu_bias_ref[...] = jnp.zeros_like(glu_bias_ref)
        sums_ref[...] = jnp.zeros_like(sums_ref)
        order.to_natural(meta, 1 + count, weights, weight_scr)

    residual = resid_ref[0]
    total = ffn[0][...]
    grad_norm = back[0][...]
    for h in range(1, halves):
        total = total + ffn[h][...]
        grad_norm = grad_norm + back[h][...]
    out_ref[0] = (residual + (total + vec_ref[2:3, :])).astype(bf16)
    grad_out = cot_ref[...].astype(f32)
    normed, scale = layer_stats(residual)
    sums_ref[0:1, :] += jnp.sum(grad_out, axis=0, keepdims=True)
    sums_ref[1:2, :] += jnp.sum(grad_norm * normed, axis=0, keepdims=True)
    sums_ref[2:3, :] += jnp.sum(grad_norm, axis=0, keepdims=True)
    grad_resid = grad_out + norm_back(grad_norm * vec_ref[0:1, :], normed, scale)
    grad_resid_ref[0] = grad_resid
    gated = gated_ref[0]
    gate = jax.nn.sigmoid(gated[:, width:])
    grad_left = grad_resid * gate
    grad_right = grad_left * gated[:, :width] * (1.0 - gate)
    grad_gated = jnp.concatenate([grad_left, grad_right], axis=1).astype(bf16)
    glu_bias_ref[0:1, :] += jnp.sum(grad_gated.astype(f32), axis=0, keepdims=True)
    grad_act = dot_right_t(grad_gated, weight_scr[...]).astype(bf16)
    moved = dot(grad_act, perm_ref[...]).astype(bf16)
    chan = moved_ref.shape[-1]
    for d in range(moved_ref.shape[0]):
        moved_ref[d] = moved[:, d * chan : (d + 1) * chan]
    rows = pl.ds(pl.multiple_of(m * span, span), span)
    gated_scr[rows, :] = grad_gated
    act_scr[rows, :] = act_ref[0]

    @pl.when(m == count - 1)
    def _():
        half = width // 2
        for part in range(4):
            cols = pl.ds(part * half, half)
            value = dot_left_t(act_scr[...], gated_scr[:, cols])

            def store(p, q, block):
                if p < pieces // 2:
                    grad_keep[p][q, :, cols] = block
                else:
                    grad_send[p - pieces // 2, q, :, cols] = block

            order.to_relative(meta, 1 + count, value, grad_scr, store)


def gate_back_call(meta, order, parts, ffn, back, resid, gated, act, cot, perm, vec, weights):
    halves, pieces = len(ffn), len(weights)
    micro, span, width = resid.shape
    tokens = micro * span
    chan = width // parts
    tile = lambda cols: pl.BlockSpec((1, span, cols), lambda m, _: (m, 0, 0))
    flat = pl.BlockSpec((span, width), lambda m, _: (m, 0))
    outs = call(
        functools.partial(gate_back_kernel, pieces, halves, order),
        (micro,),
        meta,
        [flat] * (2 * halves)
        + [tile(width), tile(2 * width), tile(width), flat]
        + [full_spec(a.shape) for a in (perm, vec, *weights)],
        (*ffn, *back, resid, gated, act, cot, perm, vec, *weights),
        [
            tile(width),
            tile(width),
            full_spec((8, 2 * width)),
            full_spec((8, width)),
            parted(parts, span, chan),
        ]
        + [full_spec((parts, order.shard_rows, 2 * width))] * (pieces // 2)
        + [full_spec((pieces // 2, parts, order.shard_rows, 2 * width))],
        [
            jax.ShapeDtypeStruct((micro, span, width), bf16),
            jax.ShapeDtypeStruct((micro, span, width), f32),
            jax.ShapeDtypeStruct((8, 2 * width), f32),
            jax.ShapeDtypeStruct((8, width), f32),
            jax.ShapeDtypeStruct((parts, micro * span, chan), bf16),
        ]
        + [jax.ShapeDtypeStruct((parts, order.shard_rows, 2 * width), bf16)] * (pieces // 2)
        + [jax.ShapeDtypeStruct((pieces // 2, parts, order.shard_rows, 2 * width), bf16)],
        [
            pltpu.VMEM((width, 2 * width), bf16),
            pltpu.VMEM((tokens, 2 * width), bf16),
            pltpu.VMEM((tokens, width), bf16),
            pltpu.VMEM((width, width // 2), bf16),
        ],
        10 * tokens * width * width,
        "gated_back",
    )
    return outs[:5], outs[5:-1], outs[-1]


def input_kernel(meta, moved_ref, x_ref, grad_resid_ref, perm_ref, out_ref):
    e = jnp.concatenate([moved_ref[d] for d in range(moved_ref.shape[0])], axis=1)
    e = dot_right_t(e, perm_ref[...])
    normed, scale = layer_stats(x_ref[0].astype(f32))
    out_ref[0] = (grad_resid_ref[0] + norm_back(e, normed, scale)).astype(bf16)


def input_call(meta, moved, x, grad_resid, perm):
    parts, _, chan = moved.shape
    micro, span, width = x.shape
    tile = lambda cols: pl.BlockSpec((1, span, cols), lambda m, _: (m, 0, 0))
    return call(
        input_kernel,
        (micro,),
        meta,
        [parted(parts, span, chan), tile(width), tile(width), full_spec(perm.shape)],
        (moved, x, grad_resid, perm),
        tile(width),
        jax.ShapeDtypeStruct((micro, span, width), bf16),
        [],
        2 * micro * span * width * width,
        "input_grad",
    )


def mode_tables(step_len, mode_count, length):
    order = jnp.arange(mode_count, dtype=f32)[:, None]
    rate = order * step_len

    def power(offsets):
        turns = 0.5 * rate[:, None, :] * offsets[None, :, None]
        angle = 2.0 * math.pi * (turns - jnp.round(turns))
        fading = jnp.exp(-0.5 * step_len[:, None, :] * offsets[None, :, None])
        return fading * jnp.cos(angle), fading * jnp.sin(angle)

    def outer(far, near):
        a, b = far[0][:, :, None], far[1][:, :, None]
        c, d = near[0][:, None], near[1][:, None]
        shape = (mode_count, far[0].shape[1] * near[0].shape[1], step_len.shape[-1])
        return (a * c - b * d).reshape(shape), (a * d + b * c).reshape(shape)

    ramp = jnp.arange(8, dtype=f32)
    near = outer(power(8.0 * ramp), power(ramp))
    far_count = length // near_span
    far = outer(
        power(8.0 * near_span * jnp.arange(far_count // 8, dtype=f32)), power(near_span * ramp)
    )

    def wave(scale):
        turns = scale * rate
        return 2.0 * math.pi * (turns - jnp.round(turns))

    decay = -0.5 * step_len
    turn_rate = math.pi * order
    step_im = jnp.exp(decay) * jnp.sin(wave(0.5))
    minus_one = jnp.expm1(decay) * jnp.cos(wave(0.5)) - 2.0 * jnp.sin(wave(0.25)) ** 2
    denominator = 0.25 + turn_rate**2
    input_mult = (
        (-0.5 * minus_one + step_im * turn_rate) / denominator,
        (-0.5 * step_im - minus_one * turn_rate) / denominator,
    )
    return near, far, input_mult


def cmul(a, b):
    return a[0] * b[0] - a[1] * b[1], a[0] * b[1] + a[1] * b[0]


def per_device(
    inputs,
    lengths,
    cotangent,
    norm1_gain,
    norm1_bias,
    step_size,
    state_out,
    skip_gain,
    glu_weight,
    glu_bias,
    norm2_gain,
    norm2_bias,
    ffn_in_weight,
    ffn_in_bias,
    ffn_out_weight,
    ffn_out_bias,
):
    micro, _, span, width = inputs.shape
    batch_size, seq_size = lax.axis_size("batch"), lax.axis_size("seq")
    batch_bits, seq_bits = bits_of(batch_size), bits_of(seq_size)
    devices = batch_size * seq_size
    shard_rows = width // devices
    chan = width // seq_size
    length = span * seq_size
    mode_count = state_out.shape[2]
    ff = ffn_in_weight.shape[1]
    me_b, me_s = lax.axis_index("batch"), lax.axis_index("seq")
    me = me_b * seq_size + me_s

    natural_piece = reverse_bits(jnp.arange(batch_size, dtype=jnp.int32), batch_bits) ^ me_b
    piece_of = reverse_bits(jnp.arange(batch_size, dtype=jnp.int32) ^ me_b, batch_bits)
    place = jnp.arange(devices, dtype=jnp.int32)
    of_piece = reverse_bits(place // seq_size, batch_bits) ^ me_b
    of_seq = reverse_bits(place % seq_size, seq_bits) ^ me_s
    natural = of_piece * seq_size + of_seq
    ramp = jnp.arange(seq_size, dtype=jnp.int32)
    out_place = reverse_bits(ramp ^ me_s, seq_bits)
    piece_ff = ff // batch_size
    groups = [[p for p in range(batch_size) if p % 2 == half] for half in range(2)]
    of_group = natural_piece[jnp.array(groups[0] + groups[1])]
    place_at = 1 + micro
    in_table = 8
    out_table = in_table + devices
    base_table = out_table + seq_size
    column_table = base_table + batch_size
    meta = jnp.concatenate(
        [
            me_s[None].astype(jnp.int32),
            lengths[:, 0],
            jnp.stack([me_s * span, me_b]).astype(jnp.int32),
            jnp.zeros((8 - 3 - micro,), jnp.int32),
            natural,
            out_place,
            of_group * (piece_ff // ff_block),
            of_group & (batch_size // 2 - 1),
        ]
    )
    order = Rows(width, shard_rows, seq_size, batch_size, in_table)

    x = inputs[:, 0]
    cot = cotangent[:, 0]

    top = batch_bits - 1
    half = batch_size // 2

    def over_low(pieces):
        for bit in reversed(range(top)):
            pieces = pieces + swap_batch(pieces, bit)
        return pieces

    def weave(low, high):
        return [piece for pair in zip(low, high) for piece in pair]

    def join(*parts):
        return jnp.concatenate(parts, axis=0)

    def near_swap(value):
        return swap(value, "seq", 1)

    def middle_swap(value):
        return swap(value, "seq", 2)

    def last_swap(value):
        return swap(value, "seq", seq_size // 2)

    def top_swap(value):
        return swap(value, "batch", 1 << top)

    counts = [2 * shard_rows, shard_rows, shard_rows, shard_rows, 4 * shard_rows]
    starts = [sum(counts[:k]) for k in range(len(counts))]
    small_size = sum(counts)
    small = jnp.concatenate(
        [
            glu_bias,
            norm2_gain,
            norm2_bias,
            ffn_out_bias,
            ffn_in_bias,
            jnp.zeros((16 * chan - small_size,), bf16),
        ]
    )
    glu_1 = gather_direct(glu_weight)
    in_1 = gather_first(ffn_in_weight)
    normed, perm = norm_call(
        me_b[None].astype(jnp.int32),
        x,
        small.reshape(16, chan),
        batch_bits,
        shard_rows,
        seq_size,
    )
    normed, glu_1, in_1, ffn_out_weight, one, coefs = together(
        (
            normed,
            glu_1,
            in_1,
            ffn_out_weight,
            jnp.concatenate([norm1_gain, norm1_bias, skip_gain, step_size]),
            state_out,
        )
    )

    normed = exchange(normed)
    glu_w = gather_more(join(glu_weight[None], *glu_1), 1)
    glu_2 = near_swap(glu_w)
    in_w = gather_more(join(ffn_in_weight[None], in_1), 2)
    in_2 = middle_swap(in_w)
    out_1 = gather_first(ffn_out_weight)
    one, coefs = gather_batch(one), gather_batch(coefs)
    one = jnp.stack(one).reshape(batch_size, 4, shard_rows).astype(f32)
    one = jnp.moveaxis(one, 0, 1).reshape(4, chan)
    vec_one = jnp.concatenate([one[:3], jnp.zeros((5, chan), f32)], axis=0)
    coefs = jnp.concatenate(coefs, axis=1)
    coefs = jnp.swapaxes(coefs, 1, 2).astype(f32)
    near, far, input_mult = mode_tables(one[3:4], mode_count, length)
    joint = cmul(coefs, input_mult)
    lift = cmul((joint[0][:, None], joint[1][:, None]), far)
    fwd_np, inv_np = transform_tables(span)
    fwd, inv = jnp.asarray(fwd_np), jnp.asarray(inv_np)
    spec = kernel_call(meta, lift, near, fwd, seq_size, span)
    normed, glu_2, in_2, out_1, spec = together((normed, glu_2, in_2, out_1, spec))

    glu_w = join(glu_w, glu_2).reshape(-1, 2 * width)
    glu_top = top_swap(glu_w)
    in_w = join(in_w, in_2)
    in_3 = near_swap(in_w)
    out_w = gather_more(join(ffn_out_weight[None], out_1), 2)
    out_2 = middle_swap(out_w)
    drive_spec, mixed, active = conv_call(
        meta, micro, normed, vec_one, after(spec, glu_w, in_w, out_w), fwd, inv
    )
    active, glu_top, in_3, out_2 = together((active, glu_top, in_3, out_2))

    small_seq = after(normed, active)[:, micro * span :, :].reshape(seq_size, -1)[:, :small_size]
    active = exchange(active)
    (small_top,) = swap_batch([small_seq], top)
    in_w = join(in_w, in_3).reshape(-1, ff)
    in_top = top_swap(after(in_w, small_top))
    out_w = join(out_w, out_2)
    out_3 = near_swap(out_w)
    glu_parts = weave(over_low([glu_w]), over_low([glu_top]))
    small_all = jnp.stack(weave(over_low([small_seq]), over_low([small_top])))
    small_all = jnp.take(small_all, piece_of, axis=0).reshape(devices, -1).astype(f32)
    glu_bias_all, gain_two, bias_two, out_bias, in_bias = [
        small_all[:, s : s + c].reshape(-1) for s, c in zip(starts, counts)
    ]
    vec_two = jnp.concatenate(
        [gain_two[None], bias_two[None], out_bias[None], jnp.zeros((5, width), f32)]
    )
    in_low = over_low([after(in_w, vec_two, glu_bias_all, in_bias, glu_parts)])
    active, in_top, out_3, in_low = together((active, in_top, out_3, in_low))

    out_w = join(out_w, out_3).reshape(-1, width)
    out_top = top_swap(out_w)
    out_low = over_low([out_w])
    in_parts = weave(in_low, over_low([in_top]))
    act, resid, gated, norm_two, norm_two_t, cot_out = gate_call(
        meta, order, after(active, out_w), x, cot, perm, vec_two, glu_bias_all[None], glu_parts
    )

    in_bias_blocks = in_bias.reshape(ff // ff_block, 1, ff_block)

    def ffn_half(which, norm_two, weights):
        return ffn_call(
            meta,
            order,
            out_table,
            place_at,
            base_table + which * half,
            column_table + which * half,
            norm_two,
            norm_two_t,
            cot_out,
            in_bias_blocks,
            in_parts,
            weights,
        )

    def low_rest(values):
        for bit in range(1, top):
            keep, send = values[: len(values) // 2], values[len(values) // 2 :]
            came = swap(jnp.stack([Sum(*v).total().astype(bf16) for v in send]), "batch", 1 << bit)
            values = [v + [came[i]] for i, v in enumerate(keep)]
        return values

    def low_sum(keep, came):
        return low_rest([[v, came[i]] for i, v in enumerate(keep)])

    def out_send(parts):
        return parts[half // 2][None] if half == 2 else jnp.stack(parts[half // 2 :])

    def rounded(terms):
        return Sum(*terms).total().astype(bf16)

    out_a, back_a, bias_a, grad_out_a, keep_in_a, send_in_a = ffn_half(0, norm_two, out_low)
    out_top = after(out_top, out_a)
    in_a_came = swap(send_in_a, "batch", 1)
    out_a_came = swap(out_send(grad_out_a), "batch", 1)
    out_b, back_b, bias_b, grad_out_b, keep_in_b, send_in_b = ffn_half(
        1, after(norm_two, out_a), over_low([out_top])
    )
    in_a_came, out_a_came = after((in_a_came, out_a_came), out_b)

    in_b_came = swap(send_in_b, "batch", 1)
    out_b_came = swap(out_send(grad_out_b), "batch", 1)
    in_a_own, in_a_other = low_sum(keep_in_a, in_a_came)
    in_a_other = rounded(in_a_other)
    in_b_top = top_swap(in_a_other)
    (output, grad_resid, grad_glu_bias, sums, moved), keep_glu, send_glu = gate_back_call(
        meta,
        order,
        seq_size,
        [out_a, out_b],
        [back_a, back_b],
        after(resid, in_a_other),
        gated,
        act,
        cot_out,
        perm,
        vec_two,
        glu_parts,
    )
    moved, in_b_came, out_b_came, in_b_top = together((moved, in_b_came, out_b_came, in_b_top))

    grads_in = exchange(moved)
    glu_came = swap(send_glu, "batch", 1)
    (out_b_sum,) = low_sum(grad_out_b[: half // 2], out_b_came)
    out_b_sum = rounded(out_b_sum)
    out_a_top = top_swap(out_b_sum)
    in_b_own, in_b_other = low_sum(keep_in_b, in_b_came)
    in_b_other = rounded([after(in_b_other[0], out_b_sum), *in_b_other[1:]])
    in_a_top = top_swap(in_b_other)
    sum_in_b = Sum(*in_b_own, in_b_top)
    in_b_near = near_swap(sum_in_b.upper())

    lower = (me_b >> top) == 0

    def halves(a, b, axis):
        return jnp.concatenate([jnp.where(lower, a, b), jnp.where(lower, b, a)], axis=axis)

    in_bias_sums = halves(bias_a.reshape(-1), bias_b.reshape(-1), 0)
    small_grads = jnp.concatenate(
        [
            value.reshape(devices, -1)
            for value in (grad_glu_bias[0], sums[1], sums[2], sums[0], in_bias_sums)
        ],
        axis=1,
    )
    small_grads = small_grads.reshape(batch_size, seq_size, -1)
    small_grads = jnp.moveaxis(small_grads, 1, 0).reshape(seq_size, -1)
    high = lax.reduce_precision(small_grads, 8, 7)
    rest = (small_grads - high).astype(bf16)
    extra_rows = -(-2 * small_grads.shape[1] // (16 * chan)) * 16
    blank = jnp.zeros((seq_size, extra_rows * chan - 2 * small_grads.shape[1]), bf16)
    extra = jnp.concatenate([high.astype(bf16), rest, blank], axis=1)
    extra = extra.reshape(seq_size, extra_rows, chan)
    grads_in, glu_came, in_b_near, extra = together((grads_in, glu_came, in_b_near, extra))

    sum_in_b.keep(in_b_near)
    in_b_middle = sum_in_b.upper()
    moved_back, cross, state_sums = back_call(
        meta,
        after(grads_in, in_b_middle),
        normed,
        drive_spec,
        mixed,
        vec_one,
        spec,
        fwd,
        inv,
        extra,
    )
    in_b_middle = middle_swap(in_b_middle)
    moved_back, cross, in_b_middle, out_a_top, in_a_top = together(
        (moved_back, cross, in_b_middle, out_a_top, in_a_top)
    )

    moved_back = exchange(moved_back)
    (out_a_sum,) = low_sum(grad_out_a[: half // 2], out_a_came)
    sum_out = Sum(*[v.reshape(seq_size, -1, width) for v in (*out_a_sum, out_a_top)])
    out_near = sum_out.upper()
    out_near_came = near_swap(out_near)
    glu_own, glu_other = low_sum(keep_glu, glu_came)
    glu_other = rounded([after(glu_other[0], out_near), *glu_other[1:]])
    glu_top_came = top_swap(glu_other)
    sum_in_a = Sum(*in_a_own, after(in_a_top, glu_other))
    in_a_near = near_swap(sum_in_a.upper())
    sum_in_b.keep(in_b_middle)
    sum_in_b.middle()
    in_b_last = last_swap(sum_in_b.upper())
    moved_back, out_near_came, glu_top_came, in_a_near, in_b_last = together(
        (moved_back, out_near_came, glu_top_came, in_a_near, in_b_last)
    )

    sum_out.keep(out_near_came)
    out_middle = sum_out.upper()
    sum_in_a.keep(in_a_near)
    in_a_middle = sum_in_a.upper()
    sum_glu = Sum(*glu_own, glu_top_came)
    glu_near = sum_glu.upper()
    input_grad = input_call(
        meta, after(moved_back, out_middle, in_a_middle, glu_near), x, grad_resid, perm
    )
    out_middle, in_a_middle = middle_swap(out_middle), middle_swap(in_a_middle)
    glu_near = near_swap(glu_near)
    input_grad, out_middle, in_a_middle, glu_near = together(
        (input_grad, out_middle, in_a_middle, glu_near)
    )

    sum_out.keep(out_middle)
    sum_out.middle()
    out_last = sum_out.upper()
    sum_in_a.keep(in_a_middle)
    sum_in_a.middle()
    in_a_last = sum_in_a.upper()
    sum_glu.keep(glu_near)
    glu_middle = sum_glu.upper()
    raw_modes = modes_call(
        meta, after(cross, input_grad, out_last, in_a_last, glu_middle), far, near, inv
    )
    out_last, in_a_last = last_swap(out_last), last_swap(in_a_last)
    glu_middle = middle_swap(glu_middle)
    raw_modes, out_last, in_a_last, glu_middle = together(
        (raw_modes, out_last, in_a_last, glu_middle)
    )
    sum_glu.keep(glu_middle)
    sum_glu.middle()
    glu_last = last_swap(sum_glu.upper())

    def finish(value, came):
        value.keep(came)
        return value.total()[0]

    z = cmul((raw_modes[0], raw_modes[1]), input_mult)
    state_grads = jnp.concatenate([z[0], -z[1], state_sums[:3]], axis=0).T
    state_grads = reduce_batch(state_grads.reshape(batch_size, shard_rows, -1))
    grad_state = jnp.stack([state_grads[:, :mode_count], state_grads[:, mode_count : 2 * mode_count]])
    grad_out_total = finish(sum_out, out_last)
    far_in = halves(finish(sum_in_a, in_a_last), finish(sum_in_b, in_b_last), 0)
    grad_in_total = jnp.concatenate([far_in[b] for b in range(batch_size)], axis=1)
    grad_glu_total = finish(sum_glu, glu_last)

    small_came = moved_back[:, micro * span :, :].reshape(seq_size, -1).astype(f32)
    small_came = jnp.sum(small_came, axis=0)
    size = batch_size * small_size
    small_came = (small_came[:size] + small_came[size : 2 * size]).reshape(batch_size, -1)
    own = reduce_batch(jnp.take(small_came, natural_piece, axis=0))
    grad_glu_bias_own, grad_gain_two, grad_bias_two, grad_out_bias, grad_in_bias_own = [
        own[s : s + c] for s, c in zip(starts, counts)
    ]

    return (
        output[:, None],
        input_grad[:, None],
        state_grads[:, 2 * mode_count + 1],
        state_grads[:, 2 * mode_count + 2],
        grad_state,
        state_grads[:, 2 * mode_count],
        grad_glu_total,
        grad_glu_bias_own,
        grad_gain_two,
        grad_bias_two,
        grad_in_total,
        grad_in_bias_own,
        grad_out_total,
        grad_out_bias,
    )


def solution(mesh):
    both = ("batch", "seq")
    rows = P(None, "batch", "seq", None)
    vector = P(both)
    matrix = P(both, None)
    state = P(None, both, None)
    return jax.shard_map(
        per_device,
        mesh=mesh,
        in_specs=(
            rows,
            P(None, "batch"),
            rows,
            vector,
            vector,
            vector,
            state,
            vector,
            matrix,
            vector,
            vector,
            vector,
            matrix,
            vector,
            matrix,
            vector,
        ),
        out_specs=(
            rows,
            rows,
            vector,
            vector,
            state,
            vector,
            matrix,
            vector,
            vector,
            vector,
            matrix,
            vector,
            matrix,
            vector,
        ),
        check_vma=False,
    )
```

time: 2910 us -> 528 us (0.18)
  matrix products: 1030 us -> 0 us
  waiting for transfers between devices: 1120 us -> 131 us
  local copies, waits for them, and re-layouts: 325 us -> 36.6 us
  blocking collectives: 223 us -> 0 us
  Pallas kernels: 0 us -> 210 us
  starting transfers between devices: 1.16 us -> 74.9 us
  other arithmetic: 142 us -> 69.2 us
  loops' own time: 40.2 us -> 0 us
    dot_general x187 -> x0, matrix products: 1030 us -> none  [the longest x36 203 us: project_block(): inner_im = jnp.einsum('ijh,jnh->inh', folded, near_im, precision=highest)]
    reduce_scatter x3 -> x0, waiting for transfers between devices: 587 us -> none  [the longest x1 360 us: per_device(): lax.psum_scatter(local_sums[10], ('batch', 'seq'), scatter_dimension=0, t...]
    all_gather x17 -> x0, waiting for transfers between devices: 517 us -> none  [the longest x14 517 us: prefix(): gathered = jax.tree.map(lambda a: lax.all_gather(a, axis), part)]
    pallas_call x0 -> x10, Pallas kernels: none -> 210 us  [call(): pl.pallas_call(kernel, grid_spec=pltpu.PrefetchScalarGridSpec(num_scalar_...]
    all_gather x2 -> x0, blocking collectives: 136 us -> none  [the longest x1 72.5 us: per_device(): lax.all_gather(weight_shards[3], ('batch', 'seq'), axis=1, tiled=True)]
    ppermute x0 -> x53, waiting for transfers between devices: none -> 128 us  [swap(): return lax.ppermute(value, axis, [(i, i ^ bit) for i in range(size)])]
    reshape x60 -> x1, local copies, waits for them, and re-layouts: 87.7 us -> 0.09 us  [per_device(): small_grads = jnp.moveaxis(small_grads, 1, 0).reshape(seq_size, -1)]
    unnamed x2 -> x0, blocking collectives: 87.1 us -> none
  transfers between devices with their start and end apart: 21 -> 57, of which waited for: 14 -> 14; matrix products, arithmetic and copies ran while one was open for 27% -> 15% of each run, Pallas kernels for 0% -> 40%
where the time goes in v1:
time: 528 us; the launch traced here: 523 us
  Pallas kernels  210 us (40%)
  waiting for transfers between devices  131 us (25%)
  starting transfers between devices  74.9 us (14%)
  other arithmetic  69.2 us (13%)
  local copies, waits for them, and re-layouts  36.6 us (7%)
    pallas_call x10, Pallas kernels, call(): pl.pallas_call(kernel, grid_spec=pltpu.PrefetchScalarGridSpec(num_scalar_...  210 us
    ppermute x53, waiting for transfers between devices, swap(): return lax.ppermute(value, axis, [(i, i ^ bit) for i in range(size)])  128 us
    ppermute x53, starting transfers between devices, swap(): return lax.ppermute(value, axis, [(i, i ^ bit) for i in range(size)])  52 us
    all_to_all x4, starting transfers between devices, exchange(): return lax.all_to_all(parts, 'seq', 0, 0)  22.9 us
    convert_element_type x12, other arithmetic, upper(): return self.total(self.terms[0].shape[0] // 2).astype(bf16)  18.9 us
    concatenate x7, other arithmetic, join(): return jnp.concatenate(parts, axis=0)  11.8 us
    convert_element_type x4, other arithmetic, rounded(): return Sum(*terms).total().astype(bf16)  10.8 us
    unnamed x109, local copies, waits for them, and re-layouts  10.6 us
  transfers between devices with their start and end apart: 57, of which 14 were waited for; matrix products, arithmetic and copies ran while one was open for 15% of the time, Pallas kernels for 40%

profile of v1, /device:TPU:0, one launch (start us, length us, event | category | flops | bytes accessed | tf_op | source)
XLA Modules:
  0.0 523.3 jit_solution(8540030458783754924)
XLA Ops:
  0.7 4.1 collective-permute-start
  13.0 4.0 concatenate.76
  18.2 5.6 %norm_one.1 = (bf16[8,784,128]{2,1,0:T(8,128)(2,1)}, bf16[1024,1024]{1,0:T(8,128)(2,1)}) custom-call(s32[1]{0:T(128)} %bitcast.3.meta, bf16[3,256,1024]{2,1,0:T(8,128)(2,1)} %bitcast.228, bf16[16,128]{1,0:T(8,128)(2,1)} %bitcast.265), custom_call_target="tpu_custom_call" | custom-call | flops 32212254 | bytes 80530 | tf_op jit(solution)/shard_map/norm_one/pallas_call | solution.py:207
  24.4 3.7 collective-permute-done.3
  33.9 5.2 all-to-all-start
  53.0 3.6 cosine_multiply_fusion.1
  62.2 16.8 %state_kernel.1.spec_ref = f32[8,2,256,128]{3,2,1,0:T(8,128)} custom-call(s32[56]{0:T(128)} %concatenate.75.meta, f32[64,32,128]{2,1,0:T(8,128)} %get-tuple-element.255.lift_re, f32[64,32,128]{2,1,0:T(8,128)} %get-tuple-element.254.lift_im, f32[64,64,128]{2,1,0:T(8,128)} %get-tuple-element.253.near_re, f32[64,64,128]{2,1,0:T(8,128)} %get-tuple-element.252.near_im, ...), custom_call_target="tpu_custom_call" | custom-call | flops 220000000 | bytes 550000 | tf_op jit(solution)/shard_map/state_kernel/pallas_call | solution.py:207
  79.0 9.3 %collective-permute-done.6 = bf16[1,128,1024]{2,1,0:T(8,128)(2,1)} collective-permute-done((bf16[1,128,1024]{2,1,0:T(8,128)(2,1)S(1)}, bf16[1,128,1024]{2,1,0:T(8,128)(2,1)}, u32[]{:S(2)}, u32[]{:S(2)}) %collective-permute-start.6) | collective-permute-done | bytes 262176 | tf_op jit(solution)/shard_map/ppermute | solution.py:44
  97.5 20.2 %state_conv.1 = (f32[3,8,512,128]{3,2,1,0:T(8,128)}, f32[3,8,256,128]{3,2,1,0:T(8,128)}, bf16[8,768,128]{2,1,0:T(8,128)(2,1)}) custom-call(s32[56]{0:T(128)} %concatenate.75.meta, bf16[8,784,128]{2,1,0:T(8,128)(2,1)} %copy-done.1, f32[8,128]{1,0:T(8,128)} %concatenate.81.vec_ref, f32[8,2,256,128]{3,2,1,0:T(8,128)} %state_kernel.1.spec_ref, ...), custom_call_target="tpu_custom_call" | custom-call | flops 300000000 | bytes 750000 | tf_op jit(solution)/shard_map/state_conv/pallas_call | solution.py:207
  120.5 5.1 all-to-all-start.1
  133.5 34.5 %collective-permute-done.18 = bf16[4,128,1024]{2,1,0:T(8,128)(2,1)S(1)} collective-permute-done((bf16[4,128,1024]{2,1,0:T(8,128)(2,1)S(1)}, bf16[4,128,1024]{2,1,0:T(8,128)(2,1)S(1)}, u32[]{:S(2)}, u32[]{:S(2)}) %collective-permute-start.18) | collective-permute-done | bytes 1048608 | tf_op jit(solution)/shard_map/ppermute | solution.py:44
  169.0 6.7 %collective-permute-done.17.refs_5_ = bf16[256,4096]{1,0:T(8,128)(2,1)} collective-permute-done((bf16[256,4096]{1,0:T(8,128)(2,1)S(1)}, bf16[256,4096]{1,0:T(8,128)(2,1)}, u32[]{:S(2)}, u32[]{:S(2)}) %collective-permute-start.17) | collective-permute-done | bytes 2097184 | tf_op jit(solution)/shard_map/ppermute | solution.py:44
  181.0 13.6 %gated_unit.1 = (bf16[3,256,1024]{2,1,0:T(8,128)(2,1)}, f32[3,256,1024]{2,1,0:T(8,128)}, f32[3,256,2048]{2,1,0:T(8,128)}, bf16[768,1024]{1,0:T(8,128)(2,1)}, bf1...) custom-call(s32[56]{0:T(128)} %concatenate.75.meta, bf16[8,768,128]{2,1,0:T(8,128)(2,1)} %all-to-all-done.1.refs_0_, ...), custom_call_target="tpu_custom_call" | custom-call | flops 96636768 | bytes 241591 | tf_op jit(solution)/shard_map/gated_unit/pallas_call | solution.py:207
  196.1 35.2 %feed_forward.2 = (f32[768,1024]{1,0:T(8,128)}, f32[768,1024]{1,0:T(8,128)}, f32[4,1,512]{2,1,0:T(1,128)}, bf16[1024,1024]{1,0:T(8,128)(2,1)}, bf16[1024,1024]{1...) custom-call(s32[56]{0:T(128)} %concatenate.75.meta, ...), custom_call_target="tpu_custom_call" | custom-call | flops 386547072 | bytes 966367 | tf_op jit(solution)/shard_map/feed_forward/pallas_call | solution.py:207
  231.9 6.1 %collective-permute-done.27.refs_9_ = bf16[1024,1024]{1,0:T(8,128)(2,1)} collective-permute-done((bf16[1024,1024]{1,0:T(8,128)(2,1)}, bf16[1024,1024]{1,0:T(8,128)(2,1)}, u32[]{:S(2)}, u32[]{:S(2)}) %collective-permute-start.27) | collective-permute-done | bytes 2097184 | tf_op jit(solution)/shard_map/ppermute | solution.py:44
  238.0 35.3 %feed_forward.3 = (f32[768,1024]{1,0:T(8,128)}, f32[768,1024]{1,0:T(8,128)}, f32[4,1,512]{2,1,0:T(1,128)}, bf16[1024,1024]{1,0:T(8,128)(2,1)}, bf16[1024,1024]{1...) custom-call(s32[56]{0:T(128)} %concatenate.75.meta, ...), custom_call_target="tpu_custom_call" | custom-call | flops 386547072 | bytes 966367 | tf_op jit(solution)/shard_map/feed_forward/pallas_call | solution.py:207
  276.9 24.4 %gated_back.1 = (bf16[3,256,1024]{2,1,0:T(8,128)(2,1)}, f32[3,256,1024]{2,1,0:T(8,128)}, f32[8,2048]{1,0:T(8,128)}, f32[8,1024]{1,0:T(8,128)}, bf16[8,768,128]{2...) custom-call(s32[56]{0:T(128)} %concatenate.75.meta, ...), custom_call_target="tpu_custom_call" | custom-call | flops 161061280 | bytes 402653 | tf_op jit(solution)/shard_map/gated_back/pallas_call | solution.py:207
  301.4 6.3 %all-to-all-start.2 = ((bf16[8,768,128]{2,1,0:T(8,128)(2,1)}), bf16[8,768,128]{2,1,0:T(8,128)(2,1)S(1)}, u32[]{:S(2)}, u32[]{:S(2)}) async-start(bf16[8,768,128]{2,1,0:T(8,128)(2,1)} %get-tuple-element.166), calls=%async_computation.2 | async-start | bytes 3145728 | tf_op jit(solution)/shard_map/all_to_all | solution.py:106
  308.4 4.5 fusion
  316.2 3.0 fusion.3
  324.4 17.4 %collective-permute-done.33 = bf16[4,2,32,1024]{3,2,1,0:T(8,128)(2,1)S(1)} collective-permute-done((bf16[4,2,32,1024]{3,2,1,0:T(8,128)(2,1)S(1)}, bf16[4,2,32,1024]{3,2,1,0:T(8,128)(2,1)S(1)}, u32[]{:S(2)}, u32[]{:S(2)}) %collective-permute-start.33) | collective-permute-done | bytes 524320 | tf_op jit(solution)/shard_map/ppermute | solution.py:44
  341.8 3.0 all-to-all-done.2.grads_ref
  347.1 32.0 %state_back.1 = (bf16[8,800,128]{2,1,0:T(8,128)(2,1)}, f32[8,512,128]{2,1,0:T(8,128)}, f32[8,128]{1,0:T(8,128)}) custom-call(s32[56]{0:T(128)} %concatenate.75.meta, bf16[8,768,128]{2,1,0:T(8,128)(2,1)} %copy-done.4, bf16[8,784,128]{2,1,0:T(8,128)(2,1)} %copy-done.1, f32[3,8,512,128]{3,2,1,0:T(8,128)} %get-tuple-element.178.drive_ref, ...), custom_call_target="tpu_custom_call" | custom-call | flops 400000000 | bytes 1000000 | tf_op jit(solution)/shard_map/state_back/pallas_call | solution.py:207
  379.2 4.1 collective-permute-done.36
  383.3 6.3 %all-to-all-start.3 = ((bf16[8,800,128]{2,1,0:T(8,128)(2,1)}), bf16[8,800,128]{2,1,0:T(8,128)(2,1)S(1)}, u32[]{:S(2)}, u32[]{:S(2)}) async-start(bf16[8,800,128]{2,1,0:T(8,128)(2,1)} %get-tuple-element.187), calls=%async_computation.3 | async-start | bytes 3276800 | tf_op jit(solution)/shard_map/all_to_all | solution.py:106
  410.1 22.9 %collective-permute-done.41 = bf16[1,2,32,1024]{3,2,1,0:T(8,128)(2,1)S(1)} collective-permute-done((bf16[1,2,32,1024]{3,2,1,0:T(8,128)(2,1)S(1)}, bf16[1,2,32,1024]{3,2,1,0:T(8,128)(2,1)S(1)}, u32[]{:S(2)}, u32[]{:S(2)}) %collective-permute-start.41) | collective-permute-done | bytes 131104 | tf_op jit(solution)/shard_map/ppermute | solution.py:44
  433.0 10.0 %collective-permute-done.40 = bf16[4,2,32,1024]{3,2,1,0:T(8,128)(2,1)S(1)} collective-permute-done((bf16[4,2,32,1024]{3,2,1,0:T(8,128)(2,1)S(1)}, bf16[4,2,32,1024]{3,2,1,0:T(8,128)(2,1)S(1)}, u32[]{:S(2)}, u32[]{:S(2)}) %collective-permute-start.40) | collective-permute-done | bytes 524320 | tf_op jit(solution)/shard_map/ppermute | solution.py:44
  455.3 7.7 %input_grad.1 = bf16[3,256,1024]{2,1,0:T(8,128)(2,1)} custom-call(s32[56]{0:T(128)} %concatenate.75.meta, bf16[8,800,128]{2,1,0:T(8,128)(2,1)} %copy-done.3, bf16[3,256,1024]{2,1,0:T(8,128)(2,1)} %bitcast.230, f32[3,256,1024]{2,1,0:T(8,128)} %get-tuple-element.205.grad_resid_ref, bf16[1024,1024]{1,0:T(8,128)(2,1)} %get-tuple-element.142.refs_3_.refs_8_.perm_ref), custom_call_target="tpu_custom_call" | custom-call | flops 32212254 | bytes 80530 | tf_op jit(solution)/shard_map/input_grad/pallas_call | solution.py:207
  464.2 7.9 %collective-permute-done.43 = bf16[2,2,32,1024]{3,2,1,0:T(8,128)(2,1)S(1)} collective-permute-done((bf16[2,2,32,1024]{3,2,1,0:T(8,128)(2,1)}, bf16[2,2,32,1024]{3,2,1,0:T(8,128)(2,1)S(1)}, u32[]{:S(2)}, u32[]{:S(2)}) %collective-permute-start.43) | collective-permute-done | bytes 262176 | tf_op jit(solution)/shard_map/ppermute | solution.py:44
  478.0 3.6 collective-permute-start.45
  483.3 18.6 %state_modes.1 = f32[2,64,128]{2,1,0:T(8,128)} custom-call(s32[56]{0:T(128)} %concatenate.75.meta, f32[8,512,128]{2,1,0:T(8,128)} %get-tuple-element.211.cross_ref, f32[64,32,128]{2,1,0:T(8,128)} %get-tuple-element.257.far_re, f32[64,32,128]{2,1,0:T(8,128)} %get-tuple-element.256.far_im, f32[64,64,128]{2,1,0:T(8,128)} %get-tuple-element.253.near_re, ...), custom_call_target="tpu_custom_call" | custom-call | flops 220000000 | bytes 550000 | tf_op jit(solution)/shard_map/state_modes/pallas_call | solution.py:207
  516.5 4.7 collective-permute-done.50
  (336 shorter events, 135.8 us)
Async XLA Ops:
  0.7 23.7 %collective-permute-start = (bf16[1,32,2048]{2,1,0:T(8,128)(2,1)}, bf16[1,32,2048]{2,1,0:T(8,128)(2,1)S(1)}, u32[]{:S(2)}, u32[]{:S(2)}) collective-permute-start(bf16[1,32,2048]{2,1,0:T(8,128)(2,1)} %bitcast.251), channel_id=1, source_target_pairs={{0,4},{1,5},{2,6},{3,7},{4,0},{5,1},{6,2},{7,3},{8,12},{9,13},{10,... | collective-permute-start | bytes 393224 | tf_op jit(solution)/shard_map/ppermute | solution.py:44
  6.4 21.8 %collective-permute-start.3 = (bf16[1,32,4096]{2,1,0:T(8,128)(2,1)}, bf16[1,32,4096]{2,1,0:T(8,128)(2,1)S(1)}, u32[]{:S(2)}, u32[]{:S(2)}) collective-permute-start(bf16[1,32,4096]{2,1,0:T(8,128)(2,1)} %bitcast.238), channel_id=1, source_target_pairs={{0,4},{1,5},{2,6},{3,7},{4,0},{5,1},{6,2},{7,3},{8,12},{9,13},{10,... | collective-permute-start | bytes 786440 | tf_op jit(solution)/shard_map/ppermute | solution.py:44
  30.3 21.1 %collective-permute-start.8 = (bf16[2,32,64]{1,2,0:T(8,128)(2,1)S(1)}, bf16[2,32,64]{1,2,0:T(8,128)(2,1)S(1)}, u32[]{:S(2)}, u32[]{:S(2)}) collective-permute-start(bf16[2,32,64]{1,2,0:T(8,128)(2,1)S(1)} %copy.48), channel_id=1, source_target_pairs={{0,8},{8,0},{16,24},{24,16},{1,9},{9,1},{17,25},{25,17},{2,10},{10... | collective-permute-start | bytes 24584 | tf_op jit(solution)/shard_map/ppermute | solution.py:44
  31.4 56.9 %collective-permute-start.4 = (bf16[4,32,2048]{2,1,0:T(8,128)(2,1)}, bf16[4,32,2048]{2,1,0:T(8,128)(2,1)}, u32[]{:S(2)}, u32[]{:S(2)}) collective-permute-start(bf16[4,32,2048]{2,1,0:T(8,128)(2,1)} %pad_maximum_fusion.4), channel_id=1, source_target_pairs={{0,1},{1,0},{2,3},{3,2},{4,5},{5,4},{6,7},{7,6},{8,9},{9,8},{10,11... | collective-permute-start | bytes 1572872 | tf_op jit(solution)/shard_map/ppermute | solution.py:44
  33.9 54.4 %all-to-all-start = ((bf16[8,784,128]{2,1,0:T(8,128)(2,1)}), bf16[8,784,128]{2,1,0:T(8,128)(2,1)S(1)}, u32[]{:S(2)}, u32[]{:S(2)}) async-start(bf16[8,784,128]{2,1,0:T(8,128)(2,1)} %get-tuple-element.117), calls=%async_computation | async-start | bytes 3211264 | tf_op jit(solution)/shard_map/all_to_all | solution.py:106
  42.1 46.2 %collective-permute-start.5 = (bf16[2,32,4096]{2,1,0:T(8,128)(2,1)}, bf16[2,32,4096]{2,1,0:T(8,128)(2,1)}, u32[]{:S(2)}, u32[]{:S(2)}) collective-permute-start(bf16[2,32,4096]{2,1,0:T(8,128)(2,1)} %pad_maximum_fusion.5), channel_id=1, source_target_pairs={{0,2},{1,3},{2,0},{3,1},{4,6},{5,7},{6,4},{7,5},{8,10},{9,11},{10,... | collective-permute-start | bytes 1572872 | tf_op jit(solution)/shard_map/ppermute | solution.py:44
  45.4 42.8 %collective-permute-start.6 = (bf16[1,128,1024]{2,1,0:T(8,128)(2,1)S(1)}, bf16[1,128,1024]{2,1,0:T(8,128)(2,1)}, u32[]{:S(2)}, u32[]{:S(2)}) collective-permute-start(bf16[1,128,1024]{2,1,0:T(8,128)(2,1)S(1)} %bitcast.243), channel_id=1, source_target_pairs={{0,4},{1,5},{2,6},{3,7},{4,0},{5,1},{6,2},{7,3},{8,12},{9,13},{10,... | collective-permute-start | bytes 786440 | tf_op jit(solution)/shard_map/ppermute | solution.py:44
  90.8 26.9 %collective-permute-start.14 = (bf16[4,32,4096]{2,1,0:T(8,128)(2,1)}, bf16[4,32,4096]{2,1,0:T(8,128)(2,1)}, u32[]{:S(2)}, u32[]{:S(2)}) collective-permute-start(bf16[4,32,4096]{2,1,0:T(8,128)(2,1)} %pad_maximum_fusion.2), channel_id=1, source_target_pairs={{0,1},{1,0},{2,3},{3,2},{4,5},{5,4},{6,7},{7,6},{8,9},{9,8},{10,11... | collective-permute-start | bytes 3145736 | tf_op jit(solution)/shard_map/ppermute | solution.py:44
  93.4 24.3 %collective-permute-start.13 = (bf16[256,2048]{1,0:T(8,128)(2,1)S(1)}, bf16[256,2048]{1,0:T(8,128)(2,1)}, u32[]{:S(2)}, u32[]{:S(2)}) collective-permute-start(bf16[256,2048]{1,0:T(8,128)(2,1)S(1)} %bitcast.231), channel_id=1, source_target_pairs={{0,16},{8,24},{16,0},{24,8},{1,17},{9,25},{17,1},{25,9},{2,18},{10... | collective-permute-start | bytes 3145736 | tf_op jit(solution)/shard_map/ppermute | solution.py:44
  96.7 21.0 %collective-permute-start.15 = (bf16[2,128,1024]{2,1,0:T(8,128)(2,1)}, bf16[2,128,1024]{2,1,0:T(8,128)(2,1)}, u32[]{:S(2)}, u32[]{:S(2)}) collective-permute-start(bf16[2,128,1024]{2,1,0:T(8,128)(2,1)} %pad_maximum_fusion.6), channel_id=1, source_target_pairs={{0,2},{1,3},{2,0},{3,1},{4,6},{5,7},{6,4},{7,5},{8,10},{9,11},{10,... | collective-permute-start | bytes 1572872 | tf_op jit(solution)/shard_map/ppermute | solution.py:44
  120.5 55.1 %all-to-all-start.1 = ((bf16[8,768,128]{2,1,0:T(8,128)(2,1)}), bf16[8,768,128]{2,1,0:T(8,128)(2,1)}, u32[]{:S(2)}, u32[]{:S(2)}) async-start(bf16[8,768,128]{2,1,0:T(8,128)(2,1)} %get-tuple-element.132), calls=%async_computation.1 | async-start | bytes 3145728 | tf_op jit(solution)/shard_map/all_to_all | solution.py:106
  127.8 47.8 %collective-permute-start.17 = (bf16[256,4096]{1,0:T(8,128)(2,1)S(1)}, bf16[256,4096]{1,0:T(8,128)(2,1)}, u32[]{:S(2)}, u32[]{:S(2)}) collective-permute-start(bf16[256,4096]{1,0:T(8,128)(2,1)S(1)} %bitcast.224), channel_id=1, source_target_pairs={{0,16},{8,24},{16,0},{24,8},{1,17},{9,25},{17,1},{25,9},{2,18},{10... | collective-permute-start | bytes 6291464 | tf_op jit(solution)/shard_map/ppermute | solution.py:44
  130.2 45.5 %collective-permute-start.23 = (bf16[256,4096]{1,0:T(8,128)(2,1)S(1)}, bf16[256,4096]{1,0:T(8,128)(2,1)}, u32[]{:S(2)}, u32[]{:S(2)}) collective-permute-start(bf16[256,4096]{1,0:T(8,128)(2,1)S(1)} %bitcast.225), channel_id=1, source_target_pairs={{0,8},{8,0},{16,24},{24,16},{1,9},{9,1},{17,25},{25,17},{2,10},{10... | collective-permute-start | bytes 6291464 | tf_op jit(solution)/shard_map/ppermute | solution.py:44
  131.5 36.5 %collective-permute-start.18 = (bf16[4,128,1024]{2,1,0:T(8,128)(2,1)S(1)}, bf16[4,128,1024]{2,1,0:T(8,128)(2,1)S(1)}, u32[]{:S(2)}, u32[]{:S(2)}) collective-permute-start(bf16[4,128,1024]{2,1,0:T(8,128)(2,1)S(1)} %pad_maximum_fusion.3), channel_id=1, source_target_pairs={{0,1},{1,0},{2,3},{3,2},{4,5},{5,4},{6,7},{7,6},{8,9},{9,8},{10,11... | collective-permute-start | bytes 3145736 | tf_op jit(solution)/shard_map/ppermute | solution.py:44
  179.1 52.2 %collective-permute-start.26 = (bf16[1024,1024]{1,0:T(8,128)(2,1)}, bf16[1024,1024]{1,0:T(8,128)(2,1)}, u32[]{:S(2)}, u32[]{:S(2)}) collective-permute-start(bf16[1024,1024]{1,0:T(8,128)(2,1)} %bitcast.25.refs_8_), channel_id=1, source_target_pairs={{0,16},{8,24},{16,0},{24,8},{1,17},{9,25},{17,1},{25,9},{2,18},{10... | collective-permute-start | bytes 6291464 | tf_op jit(solution)/shard_map/ppermute | solution.py:44
  231.4 42.4 %collective-permute-start.28 = (bf16[2,8,2,32,1024]{4,3,2,1,0:T(8,128)(2,1)}, bf16[2,8,2,32,1024]{4,3,2,1,0:T(8,128)(2,1)S(1)}, u32[]{:S(2)}, u32[]{:S(2)}) collective-permute-start(bf16[2,8,2,32,1024]{4,3,2,1,0:T(8,128)(2,1)} %get-tuple-element.157), channel_id=1, source_target_pairs={{0,8},{8,0},{16,24},{24,16},{1,9},{9,1},{17,25},{25,17},{2,10},{10... | collective-permute-start | bytes 6291464 | tf_op jit(solution)/shard_map/ppermute | solution.py:44
  273.2 28.2 %collective-permute-start.29 = (bf16[2,8,2,32,1024]{4,3,2,1,0:T(8,128)(2,1)}, bf16[2,8,2,32,1024]{4,3,2,1,0:T(8,128)(2,1)}, u32[]{:S(2)}, u32[]{:S(2)}) collective-permute-start(bf16[2,8,2,32,1024]{4,3,2,1,0:T(8,128)(2,1)} %get-tuple-element.164), channel_id=1, source_target_pairs={{0,8},{8,0},{16,24},{24,16},{1,9},{9,1},{17,25},{25,17},{2,10},{10... | collective-permute-start | bytes 6291464 | tf_op jit(solution)/shard_map/ppermute | solution.py:44
  273.5 27.9 %collective-permute-start.30 = (bf16[1,1024,1024]{2,1,0:T(8,128)(2,1)}, bf16[1,1024,1024]{2,1,0:T(8,128)(2,1)}, u32[]{:S(2)}, u32[]{:S(2)}) collective-permute-start(bf16[1,1024,1024]{2,1,0:T(8,128)(2,1)} %bitcast.271), channel_id=1, source_target_pairs={{0,8},{8,0},{16,24},{24,16},{1,9},{9,1},{17,25},{25,17},{2,10},{10... | collective-permute-start | bytes 6291464 | tf_op jit(solution)/shard_map/ppermute | solution.py:44
  275.4 26.0 %collective-permute-start.31 = (bf16[8,2,32,1024]{3,2,1,0:T(8,128)(2,1)}, bf16[8,2,32,1024]{3,2,1,0:T(8,128)(2,1)S(1)}, u32[]{:S(2)}, u32[]{:S(2)}) collective-permute-start(bf16[8,2,32,1024]{3,2,1,0:T(8,128)(2,1)} %fusion.4), channel_id=1, source_target_pairs={{0,16},{8,24},{16,0},{24,8},{1,17},{9,25},{17,1},{25,9},{2,18},{10... | collective-permute-start | bytes 3145736 | tf_op jit(solution)/shard_map/ppermute | solution.py:44
  301.4 43.4 %all-to-all-start.2 = ((bf16[8,768,128]{2,1,0:T(8,128)(2,1)}), bf16[8,768,128]{2,1,0:T(8,128)(2,1)S(1)}, u32[]{:S(2)}, u32[]{:S(2)}) async-start(bf16[8,768,128]{2,1,0:T(8,128)(2,1)} %get-tuple-element.166), calls=%async_computation.2 | async-start | bytes 3145728 | tf_op jit(solution)/shard_map/all_to_all | solution.py:106
  307.8 83.2 %collective-permute-start.37 = (bf16[1,1024,1024]{2,1,0:T(8,128)(2,1)}, bf16[1,1024,1024]{2,1,0:T(8,128)(2,1)}, u32[]{:S(2)}, u32[]{:S(2)}) collective-permute-start(bf16[1,1024,1024]{2,1,0:T(8,128)(2,1)} %bitcast.270), channel_id=1, source_target_pairs={{0,8},{8,0},{16,24},{24,16},{1,9},{9,1},{17,25},{25,17},{2,10},{10... | collective-permute-start | bytes 6291464 | tf_op jit(solution)/shard_map/ppermute | solution.py:44
  312.9 70.4 %collective-permute-start.35 = (bf16[1024,1024]{1,0:T(8,128)(2,1)}, bf16[1024,1024]{1,0:T(8,128)(2,1)}, u32[]{:S(2)}, u32[]{:S(2)}) collective-permute-start(bf16[1024,1024]{1,0:T(8,128)(2,1)} %fusion), channel_id=1, source_target_pairs={{0,16},{8,24},{16,0},{24,8},{1,17},{9,25},{17,1},{25,9},{2,18},{10... | collective-permute-start | bytes 6291464 | tf_op jit(solution)/shard_map/ppermute | solution.py:44
  319.3 64.0 %collective-permute-start.36 = (bf16[8,2,32,1024]{3,2,1,0:T(8,128)(2,1)}, bf16[8,2,32,1024]{3,2,1,0:T(8,128)(2,1)}, u32[]{:S(2)}, u32[]{:S(2)}) collective-permute-start(bf16[8,2,32,1024]{3,2,1,0:T(8,128)(2,1)} %fusion.3), channel_id=1, source_target_pairs={{0,16},{8,24},{16,0},{24,8},{1,17},{9,25},{17,1},{25,9},{2,18},{10... | collective-permute-start | bytes 3145736 | tf_op jit(solution)/shard_map/ppermute | solution.py:44
  346.4 36.9 %collective-permute-start.34 = (bf16[2,2,32,1024]{3,2,1,0:T(8,128)(2,1)S(1)}, bf16[2,2,32,1024]{3,2,1,0:T(8,128)(2,1)S(1)}, u32[]{:S(2)}, u32[]{:S(2)}) collective-permute-start(bf16[2,2,32,1024]{3,2,1,0:T(8,128)(2,1)S(1)} %fusion.32), channel_id=1, source_target_pairs={{0,2},{1,3},{2,0},{3,1},{4,6},{5,7},{6,4},{7,5},{8,10},{9,11},{10,... | collective-permute-start | bytes 786440 | tf_op jit(solution)/shard_map/ppermute | solution.py:44
  383.3 61.4 %all-to-all-start.3 = ((bf16[8,800,128]{2,1,0:T(8,128)(2,1)}), bf16[8,800,128]{2,1,0:T(8,128)(2,1)S(1)}, u32[]{:S(2)}, u32[]{:S(2)}) async-start(bf16[8,800,128]{2,1,0:T(8,128)(2,1)} %get-tuple-element.187), calls=%async_computation.3 | async-start | bytes 3276800 | tf_op jit(solution)/shard_map/all_to_all | solution.py:106
  396.4 46.6 %collective-permute-start.39 = (bf16[8,32,2048]{2,1,0:T(8,128)(2,1)S(1)}, bf16[8,32,2048]{2,1,0:T(8,128)(2,1)S(1)}, u32[]{:S(2)}, u32[]{:S(2)}) collective-permute-start(bf16[8,32,2048]{2,1,0:T(8,128)(2,1)S(1)} %fusion.1), channel_id=1, source_target_pairs={{0,16},{8,24},{16,0},{24,8},{1,17},{9,25},{17,1},{25,9},{2,18},{10... | collective-permute-start | bytes 3145736 | tf_op jit(solution)/shard_map/ppermute | solution.py:44
  397.5 47.2 %collective-permute-start.38 = (bf16[4,128,1024]{2,1,0:T(8,128)(2,1)S(1)}, bf16[4,128,1024]{2,1,0:T(8,128)(2,1)}, u32[]{:S(2)}, u32[]{:S(2)}) collective-permute-start(bf16[4,128,1024]{2,1,0:T(8,128)(2,1)S(1)} %fusion.2), channel_id=1, source_target_pairs={{0,1},{1,0},{2,3},{3,2},{4,5},{5,4},{6,7},{7,6},{8,9},{9,8},{10,11... | collective-permute-start | bytes 3145736 | tf_op jit(solution)/shard_map/ppermute | solution.py:44
  401.0 42.0 %collective-permute-start.40 = (bf16[4,2,32,1024]{3,2,1,0:T(8,128)(2,1)S(1)}, bf16[4,2,32,1024]{3,2,1,0:T(8,128)(2,1)S(1)}, u32[]{:S(2)}, u32[]{:S(2)}) collective-permute-start(bf16[4,2,32,1024]{3,2,1,0:T(8,128)(2,1)S(1)} %fusion.10), channel_id=1, source_target_pairs={{0,1},{1,0},{2,3},{3,2},{4,5},{5,4},{6,7},{7,6},{8,9},{9,8},{10,11... | collective-permute-start | bytes 1572872 | tf_op jit(solution)/shard_map/ppermute | solution.py:44
  402.2 30.8 %collective-permute-start.41 = (bf16[1,2,32,1024]{3,2,1,0:T(8,128)(2,1)S(1)}, bf16[1,2,32,1024]{3,2,1,0:T(8,128)(2,1)S(1)}, u32[]{:S(2)}, u32[]{:S(2)}) collective-permute-start(bf16[1,2,32,1024]{3,2,1,0:T(8,128)(2,1)S(1)} %fusion.60), channel_id=1, source_target_pairs={{0,4},{1,5},{2,6},{3,7},{4,0},{5,1},{6,2},{7,3},{8,12},{9,13},{10,... | collective-permute-start | bytes 393224 | tf_op jit(solution)/shard_map/ppermute | solution.py:44
  449.8 22.3 %collective-permute-start.44 = (bf16[4,32,2048]{2,1,0:T(8,128)(2,1)}, bf16[4,32,2048]{2,1,0:T(8,128)(2,1)}, u32[]{:S(2)}, u32[]{:S(2)}) collective-permute-start(bf16[4,32,2048]{2,1,0:T(8,128)(2,1)} %fusion.6), channel_id=1, source_target_pairs={{0,1},{1,0},{2,3},{3,2},{4,5},{5,4},{6,7},{7,6},{8,9},{9,8},{10,11... | collective-permute-start | bytes 1572872 | tf_op jit(solution)/shard_map/ppermute | solution.py:44
  476.3 25.6 %collective-permute-start.47 = (bf16[2,32,2048]{2,1,0:T(8,128)(2,1)}, bf16[2,32,2048]{2,1,0:T(8,128)(2,1)}, u32[]{:S(2)}, u32[]{:S(2)}) collective-permute-start(bf16[2,32,2048]{2,1,0:T(8,128)(2,1)} %fusion.21), channel_id=1, source_target_pairs={{0,2},{1,3},{2,0},{3,1},{4,6},{5,7},{6,4},{7,5},{8,10},{9,11},{10,... | collective-permute-start | bytes 786440 | tf_op jit(solution)/shard_map/ppermute | solution.py:44
  478.0 24.6 %collective-permute-start.45 = (bf16[1,128,1024]{2,1,0:T(8,128)(2,1)}, bf16[1,128,1024]{2,1,0:T(8,128)(2,1)}, u32[]{:S(2)}, u32[]{:S(2)}) collective-permute-start(bf16[1,128,1024]{2,1,0:T(8,128)(2,1)} %fusion.26), channel_id=1, source_target_pairs={{0,4},{1,5},{2,6},{3,7},{4,0},{5,1},{6,2},{7,3},{8,12},{9,13},{10,... | collective-permute-start | bytes 786440 | tf_op jit(solution)/shard_map/ppermute | solution.py:44
  (76 other events, 996.5 us)

commit v2 on v1

--- a/solution.py
+++ b/solution.py
@@ -108,28 +108,23 @@
 
 def gelu_parts(values):
     square = values * values
-    tanh = jnp.tanh(gelu_scale * values * (1.0 + gelu_cubic * square))
-    half = 0.5 * (1.0 + tanh)
-    return tanh, square, half
+    half = 0.5 * jnp.tanh(values * (gelu_scale + gelu_scale * gelu_cubic * square)) + 0.5
+    return square, half
 
 
 def gelu_value(values):
-    return values * gelu_parts(values)[2]
+    return values * gelu_parts(values)[1]
+
+
+def gelu_both(values):
+    square, half = gelu_parts(values)
+    value = values * half
+    inner = 2.0 * gelu_scale + 6.0 * gelu_scale * gelu_cubic * square
+    return value, half + value * (1.0 - half) * inner
 
 
 def gelu_slope(values):
-    tanh, square, half = gelu_parts(values)
-    return half + 0.5 * values * (1.0 - tanh * tanh) * (
-        gelu_scale * (1.0 + 3.0 * gelu_cubic * square)
-    )
-
-
-def gelu_both(values):
-    tanh, square, half = gelu_parts(values)
-    slope = half + 0.5 * values * (1.0 - tanh * tanh) * (
-        gelu_scale * (1.0 + 3.0 * gelu_cubic * square)
-    )
-    return values * half, slope
+    return gelu_both(values)[1]
 
 
 def layer_stats(values):
@@ -238,9 +233,7 @@
         row = lax.broadcasted_iota(jnp.int32, (width, width), 0)
         perm_ref[...] = jnp.where(row == source, 1.0, 0.0).astype(bf16)
         for d in range(out_ref.shape[0]):
-            out_ref[d, pl.ds(out_ref.shape[1] - extra_ref.shape[0], extra_ref.shape[0]), :] = (
-                extra_ref[...]
-            )
+            out_ref[d, pl.ds(out_ref.shape[1] - 16, 16), :] = extra_ref[...]
 
     span = x_ref.shape[1]
     rows = pl.ds(pl.multiple_of(pl.program_id(0) * span, span), span)
@@ -257,11 +250,12 @@
         functools.partial(norm_kernel, batch_bits, shard_rows, parts),
         (micro,),
         meta,
-        [pl.BlockSpec((1, span, width), lambda m, _: (m, 0, 0)), full_spec(extra.shape)],
+        [pl.BlockSpec((1, span, width), lambda m, _: (m, 0, 0))]
+        + [full_spec(extra.shape)],
         (x, extra),
-        [full_spec((parts, micro * span + extra.shape[0], chan)), full_spec((width, width))],
+        [full_spec((parts, micro * span + 16, chan)), full_spec((width, width))],
         [
-            jax.ShapeDtypeStruct((parts, micro * span + extra.shape[0], chan), bf16),
+            jax.ShapeDtypeStruct((parts, micro * span + 16, chan), bf16),
             jax.ShapeDtypeStruct((width, width), bf16),
         ],
         [],
@@ -395,7 +389,7 @@
                 spectrum[k, high] = acc[1]
                 return carry
 
-            lax.fori_loop(0, span // freq_tile, one_tile, 0)
+            lax.fori_loop(0, span // freq_tile, one_tile, 0, unroll=True)
         both = dot(
             inv_ref[...], stack_split(jnp.concatenate([spectrum[0], spectrum[1]], axis=1))
         )
@@ -485,7 +479,7 @@
             body(low, high)
             return carry
 
-        lax.fori_loop(0, span // freq_tile, one_tile, 0)
+        lax.fori_loop(0, span // freq_tile, one_tile, 0, unroll=True)
 
     zero = jnp.zeros((freq_tile, chan), f32)
 
@@ -646,7 +640,7 @@
 
 
 class Rows:
-    def __init__(self, width, shard_rows, seq_size, batch_size, table):
+    def __init__(self, width, shard_rows, seq_size, batch_size, table, by_channel=False):
         self.width = width
         self.shard_rows = shard_rows
         self.seq_size = seq_size
@@ -654,6 +648,7 @@
         self.table = table
         self.piece_rows = shard_rows * seq_size
         self.by_block = shard_rows % 16 == 0
+        self.by_channel = by_channel
 
     def natural(self, meta, p, q):
         start = meta[self.table + p * self.seq_size + q] * self.shard_rows
@@ -664,8 +659,12 @@
         relative = lax.broadcasted_iota(jnp.int32, shape, 0)
         piece = relative // self.piece_rows
         position = (relative % self.piece_rows) // self.shard_rows
-        shard = (reverse_bits(piece, bits_of(self.batch_size)) ^ meta[place + 1]) * self.seq_size
-        shard = shard + (reverse_bits(position, bits_of(self.seq_size)) ^ meta[0])
+        seq = reverse_bits(position, bits_of(self.seq_size)) ^ meta[0]
+        if self.by_channel:
+            shard = seq * self.batch_size + piece
+        else:
+            batch = reverse_bits(piece, bits_of(self.batch_size)) ^ meta[place + 1]
+            shard = batch * self.seq_size + seq
         source = shard * self.shard_rows + relative % self.shard_rows
         return jnp.where(lax.broadcasted_iota(jnp.int32, shape, 1) == source, 1.0, 0.0).astype(bf16)
 
@@ -696,9 +695,9 @@
 
 
 def gate_kernel(pieces, order, meta, *refs):
-    active_ref, x_ref, cot_ref, perm_ref, vec_ref, glu_bias_ref = refs[:6]
-    weights = refs[6 : 6 + pieces]
-    act_ref, resid_ref, gated_ref, norm_ref, norm_t_ref, cot_out, weight_scr = refs[6 + pieces :]
+    active_ref, x_ref, cot_ref, vec_ref, glu_bias_ref = refs[:5]
+    weights = refs[5 : 5 + pieces]
+    act_ref, resid_ref, gated_ref, norm_ref, norm_t_ref, cot_out, weight_scr = refs[5 + pieces :]
     m = pl.program_id(0)
     _, span, width = x_ref.shape
     micro = pl.num_programs(0)
@@ -708,8 +707,7 @@
         order.to_natural(meta, 1 + micro, weights, weight_scr)
 
     act = jnp.concatenate([active_ref[d] for d in range(active_ref.shape[0])], axis=1)
-    act = dot_right_t(act, perm_ref[...]).astype(bf16)
-    act_ref[0] = act
+    act_ref[...] = act
     gated = dot(act, weight_scr[...]) + glu_bias_ref[...]
     gated_ref[0] = gated
     residual = x_ref[0].astype(f32) + gated[:, :width] * jax.nn.sigmoid(gated[:, width:])
@@ -722,7 +720,7 @@
     cot_out[...] = jnp.where(rows < meta[1 + m], cot_ref[0].astype(f32), 0.0).astype(bf16)
 
 
-def gate_call(meta, order, active, x, cot, perm, vec, glu_bias, weights):
+def gate_call(meta, order, active, x, cot, vec, glu_bias, weights):
     parts, _, chan = active.shape
     pieces = len(weights)
     micro, span, width = x.shape
@@ -734,10 +732,10 @@
         (micro,),
         meta,
         [parted(parts, span, chan), tile(width), tile(width)]
-        + [full_spec(a.shape) for a in (perm, vec, glu_bias, *weights)],
-        (active, x, cot, perm, vec, glu_bias, *weights),
+        + [full_spec(a.shape) for a in (vec, glu_bias, *weights)],
+        (active, x, cot, vec, glu_bias, *weights),
         [
-            tile(width),
+            flat,
             tile(width),
             tile(2 * width),
             flat,
@@ -745,7 +743,7 @@
             flat,
         ],
         [
-            jax.ShapeDtypeStruct((micro, span, width), bf16),
+            jax.ShapeDtypeStruct((tokens, width), bf16),
             jax.ShapeDtypeStruct((micro, span, width), f32),
             jax.ShapeDtypeStruct((micro, span, 2 * width), f32),
             jax.ShapeDtypeStruct((tokens, width), bf16),
@@ -758,22 +756,41 @@
     )
 
 
-ff_block = 512
-
-
-def ffn_kernel(pieces, batch_pieces, sub, order, out_table, place, meta, *refs):
-    norm_ref, norm_t_ref, cot_ref, bias_ref = refs[:4]
-    w_in = refs[4 : 4 + batch_pieces]
-    w_out = refs[4 + batch_pieces : 4 + batch_pieces + pieces]
-    rest = refs[4 + batch_pieces + pieces :]
-    out_ref, back_ref, grad_bias = rest[:3]
-    grad_out = rest[3 : 3 + pieces]
-    grad_in = rest[3 + pieces : 3 + pieces + batch_pieces // 2]
-    grad_in_send, in_scr, out_scr, grad_in_scr = rest[3 + pieces + batch_pieces // 2 :]
+def ff_block_of(piece_ff):
+    return min(1024, piece_ff)
+
+
+def ffn_kernel(pieces, batch_pieces, sub, order, out_table, place, first, second, meta, *refs):
+    refs = list(refs)
+    take = lambda count: [refs.pop(0) for _ in range(count)]
+    half = batch_pieces // 2
+    (cot_ref,) = take(1)
+    w_out = take(pieces)
+    if first:
+        norm_ref, bias_ref = take(2)
+        w_in = take(batch_pieces)
+    else:
+        spread_ref, hidden_ref = take(2)
+    if second:
+        (norm_t_ref,) = take(1)
+    if first:
+        back_ref, grad_bias = take(2)
+        if not second:
+            spread_ref, hidden_ref = take(2)
+    if second:
+        (out_ref,) = take(1)
+        grad_out, grad_in = take(pieces), take(half)
+        (grad_in_send,) = take(1)
+    (out_scr,) = take(1)
+    if first:
+        (in_scr,) = take(1)
+    if second:
+        (grad_in_scr,) = take(1)
     k = pl.program_id(0)
     s = pl.program_id(1)
-    order.to_natural(meta, place, w_in, in_scr)
+    ff_block = out_scr.shape[0]
     subs = ff_block // sub
+    start = jnp.logical_and(k == 0, s == 0)
 
     def sub_rows(t):
         return pl.ds(pl.multiple_of(meta[out_table + s * subs + t] * sub, sub), sub)
@@ -785,111 +802,132 @@
             for t in range(subs):
                 out_scr[pl.ds(t * sub, sub), :] = w_out[piece][sub_rows(t), :]
 
-    hidden = dot(norm_ref[...], in_scr[...]) + bias_ref[0]
-    spread, slope = gelu_both(hidden)
-    spread = spread.astype(bf16)
-    grad_hidden = (dot_right_t(cot_ref[...], out_scr[...]) * slope).astype(bf16)
-    grad_bias[0] = jnp.sum(grad_hidden.astype(f32), axis=0, keepdims=True)
-    part_out = dot(spread, out_scr[...])
-    part_back = dot_right_t(grad_hidden, in_scr[...])
-    first = jnp.logical_and(k == 0, s == 0)
-
-    @pl.when(first)
-    def _():
-        out_ref[...] = part_out
-        back_ref[...] = part_back
-
-    @pl.when(jnp.logical_not(first))
-    def _():
-        out_ref[...] += part_out
-        back_ref[...] += part_back
-
-    def store(p, q, block):
-        if p < batch_pieces // 2:
-            grad_in[p][q, 0] = block
-        else:
-            grad_in_send[p - batch_pieces // 2, q, 0] = block
-
-    part_in = dot(norm_t_ref[...], grad_hidden)
-    order.to_relative(meta, place, part_in, grad_in_scr, store)
-
-    part = dot_left_t(spread, cot_ref[...]).astype(bf16)
-    for piece in range(pieces):
-
-        @pl.when(k == piece)
+    def accumulate(ref, part):
+        @pl.when(start)
         def _():
-            for t in range(subs):
-                grad_out[piece][sub_rows(t), :] = part[t * sub : (t + 1) * sub, :]
-
-
-def ffn_call(meta, order, out_table, place, base, column, norm, norm_t, cot, bias, w_in, w_out):
-    pieces, batch_pieces = len(w_out), len(w_in)
-    tokens, width = norm.shape
+            ref[...] = part
+
+        @pl.when(jnp.logical_not(start))
+        def _():
+            ref[...] += part
+
+    if first:
+        order.to_natural(meta, place, w_in, in_scr)
+        hidden = dot(norm_ref[...], in_scr[...]) + bias_ref[0]
+        spread, slope = gelu_both(hidden)
+        spread = spread.astype(bf16)
+        grad_hidden = (dot_right_t(cot_ref[...], out_scr[...]) * slope).astype(bf16)
+        grad_bias[0] = jnp.sum(grad_hidden.astype(f32), axis=0, keepdims=True)
+        if not second:
+            spread_ref[...] = spread
+            hidden_ref[...] = grad_hidden
+        accumulate(back_ref, dot_right_t(grad_hidden, in_scr[...]))
+    else:
+        spread, grad_hidden = spread_ref[...], hidden_ref[...]
+
+    if second:
+        accumulate(out_ref, dot(spread, out_scr[...]))
+
+        def store(p, q, block):
+            if p < half:
+                grad_in[p][q, 0] = block
+            else:
+                grad_in_send[p - half, q, 0] = block
+
+        order.to_relative(meta, place, dot(norm_t_ref[...], grad_hidden), grad_in_scr, store)
+        part = dot_left_t(spread, cot_ref[...]).astype(bf16)
+        for piece in range(pieces):
+
+            @pl.when(k == piece)
+            def _():
+                for t in range(subs):
+                    grad_out[piece][sub_rows(t), :] = part[t * sub : (t + 1) * sub, :]
+
+
+def ffn_call(meta, order, out_table, place, base, column, cot, w_out, norm=None, bias=None, w_in=None, norm_t=None, kept=None):
+    first, second = norm is not None, norm_t is not None
+    pieces, batch_pieces = len(w_out), order.batch_size
+    tokens, width = cot.shape
     piece_ff = w_out[0].shape[0]
+    ff_block = ff_block_of(piece_ff)
     steps = piece_ff // ff_block
     sub = piece_ff // order.seq_size
     rows = order.piece_rows
     half = batch_pieces // 2
+    seq_size, low = order.seq_size, order.shard_rows
     block = lambda k, s, meta: meta[base + k] + s
-    seq_size, low = order.seq_size, order.shard_rows
-    kept = pl.BlockSpec(
-        (seq_size, 1, low, ff_block), lambda k, s, meta: (0, meta[column + k], 0, s)
-    )
-    sent = pl.BlockSpec(
-        (half, seq_size, 1, low, ff_block), lambda k, s, meta: (0, 0, meta[column + k], 0, s)
-    )
-    outs = call(
-        functools.partial(ffn_kernel, pieces, batch_pieces, sub, order, out_table, place),
-        (pieces, steps),
-        meta,
-        [full_spec(a.shape) for a in (norm, norm_t, cot)]
-        + [pl.BlockSpec((1, 1, ff_block), lambda k, s, meta: (block(k, s, meta), 0, 0))]
-        + [
+    wide = full_spec((tokens, width))
+    step_columns = pl.BlockSpec((tokens, ff_block), lambda k, s, meta: (0, k * steps + s))
+    activations = jax.ShapeDtypeStruct((tokens, pieces * piece_ff), bf16)
+    total = jax.ShapeDtypeStruct((tokens, width), f32)
+    operands = [cot, *w_out]
+    in_specs = [wide] + [full_spec(a.shape) for a in w_out]
+    outs, out_specs, scratch = [], [], [pltpu.VMEM((ff_block, width), bf16)]
+    if first:
+        operands += [norm, bias, *w_in]
+        in_specs += [wide]
+        in_specs += [pl.BlockSpec((1, 1, ff_block), lambda k, s, meta: (block(k, s, meta), 0, 0))]
+        in_specs += [
             pl.BlockSpec((rows, ff_block), lambda k, s, meta: (0, block(k, s, meta)))
             for _ in w_in
         ]
-        + [full_spec(a.shape) for a in w_out],
-        (norm, norm_t, cot, bias, *w_in, *w_out),
-        [
-            full_spec((tokens, width)),
-            full_spec((tokens, width)),
-            pl.BlockSpec((1, 1, ff_block), lambda k, s, meta: (meta[column + k] * steps + s, 0, 0)),
+        outs += [total, jax.ShapeDtypeStruct((pieces * steps, 1, ff_block), f32)]
+        out_specs += [wide]
+        out_specs += [
+            pl.BlockSpec((1, 1, ff_block), lambda k, s, meta: (meta[column + k] * steps + s, 0, 0))
         ]
-        + [full_spec(a.shape) for a in w_out]
-        + [kept] * half
-        + [sent],
-        [
-            jax.ShapeDtypeStruct((tokens, width), f32),
-            jax.ShapeDtypeStruct((tokens, width), f32),
-            jax.ShapeDtypeStruct((pieces * steps, 1, ff_block), f32),
+        scratch += [pltpu.VMEM((width, ff_block), bf16)]
+        if not second:
+            outs += [activations] * 2
+            out_specs += [step_columns] * 2
+    else:
+        operands += kept
+        in_specs += [step_columns] * 2
+    if second:
+        operands += [norm_t]
+        in_specs += [full_spec(norm_t.shape)]
+        outs += [total] + [jax.ShapeDtypeStruct(a.shape, bf16) for a in w_out]
+        outs += [jax.ShapeDtypeStruct((seq_size, pieces, low, piece_ff), bf16)] * half
+        outs += [jax.ShapeDtypeStruct((half, seq_size, pieces, low, piece_ff), bf16)]
+        out_specs += [wide] + [full_spec(a.shape) for a in w_out]
+        out_specs += [
+            pl.BlockSpec((seq_size, 1, low, ff_block), lambda k, s, meta: (0, meta[column + k], 0, s))
+        ] * half
+        out_specs += [
+            pl.BlockSpec(
+                (half, seq_size, 1, low, ff_block),
+                lambda k, s, meta: (0, 0, meta[column + k], 0, s),
+            )
         ]
-        + [jax.ShapeDtypeStruct(a.shape, bf16) for a in w_out]
-        + [jax.ShapeDtypeStruct((seq_size, pieces, low, piece_ff), bf16)] * half
-        + [jax.ShapeDtypeStruct((half, seq_size, pieces, low, piece_ff), bf16)],
-        [
-            pltpu.VMEM((width, ff_block), bf16),
-            pltpu.VMEM((ff_block, width), bf16),
-            pltpu.VMEM((width, ff_block), bf16),
-        ],
-        12 * tokens * width * piece_ff * pieces,
+        scratch += [pltpu.VMEM((width, ff_block), bf16)]
+    results = call(
+        functools.partial(
+            ffn_kernel, pieces, batch_pieces, sub, order, out_table, place, first, second
+        ),
+        (pieces, steps),
+        meta,
+        in_specs,
+        operands,
+        out_specs,
+        outs,
+        scratch,
+        6 * (first + second) * tokens * width * piece_ff * pieces,
         "feed_forward",
     )
-    split = 3 + pieces
-    return outs[0], outs[1], outs[2], outs[3:split], outs[split:-1], outs[-1]
+    head = results[: 2 * first + 2 * (first and not second)]
+    tail = results[len(head) :]
+    return head, tail[:1], tail[1 : 1 + pieces], tail[1 + pieces : -1], tail[-1:]
 
 
 def gate_back_kernel(pieces, halves, order, meta, *refs):
-    ffn = refs[:halves]
-    back = refs[halves : 2 * halves]
-    resid_ref, gated_ref, act_ref, cot_ref, perm_ref, vec_ref = refs[2 * halves : 2 * halves + 6]
-    weights = refs[2 * halves + 6 : 2 * halves + 6 + pieces]
-    rest = refs[2 * halves + 6 + pieces :]
-    out_ref, grad_resid_ref, glu_bias_ref, sums_ref, moved_ref = rest[:5]
-    grad_keep = rest[5 : 5 + pieces // 2]
-    grad_send, weight_scr, gated_scr, act_scr, grad_scr = rest[5 + pieces // 2 :]
+    back = refs[:halves]
+    resid_ref, gated_ref, cot_ref, vec_ref = refs[halves : halves + 4]
+    weights = refs[halves + 4 : halves + 4 + pieces]
+    rest = refs[halves + 4 + pieces :]
+    grad_resid_ref, grad_gated_ref, glu_bias_ref, sums_ref, moved_ref, weight_scr = rest
     m = pl.program_id(0)
     count = pl.num_programs(0)
-    span, width = cot_ref.shape
+    width = cot_ref.shape[1]
 
     @pl.when(m == 0)
     def _():
@@ -898,12 +936,9 @@
         order.to_natural(meta, 1 + count, weights, weight_scr)
 
     residual = resid_ref[0]
-    total = ffn[0][...]
     grad_norm = back[0][...]
     for h in range(1, halves):
-        total = total + ffn[h][...]
         grad_norm = grad_norm + back[h][...]
-    out_ref[0] = (residual + (total + vec_ref[2:3, :])).astype(bf16)
     grad_out = cot_ref[...].astype(f32)
     normed, scale = layer_stats(residual)
     sums_ref[0:1, :] += jnp.sum(grad_out, axis=0, keepdims=True)
@@ -916,75 +951,80 @@
     grad_left = grad_resid * gate
     grad_right = grad_left * gated[:, :width] * (1.0 - gate)
     grad_gated = jnp.concatenate([grad_left, grad_right], axis=1).astype(bf16)
+    grad_gated_ref[...] = grad_gated
     glu_bias_ref[0:1, :] += jnp.sum(grad_gated.astype(f32), axis=0, keepdims=True)
-    grad_act = dot_right_t(grad_gated, weight_scr[...]).astype(bf16)
-    moved = dot(grad_act, perm_ref[...]).astype(bf16)
+    moved = dot_right_t(grad_gated, weight_scr[...]).astype(bf16)
     chan = moved_ref.shape[-1]
     for d in range(moved_ref.shape[0]):
         moved_ref[d] = moved[:, d * chan : (d + 1) * chan]
-    rows = pl.ds(pl.multiple_of(m * span, span), span)
-    gated_scr[rows, :] = grad_gated
-    act_scr[rows, :] = act_ref[0]
-
-    @pl.when(m == count - 1)
-    def _():
-        half = width // 2
-        for part in range(4):
-            cols = pl.ds(part * half, half)
-            value = dot_left_t(act_scr[...], gated_scr[:, cols])
-
-            def store(p, q, block):
-                if p < pieces // 2:
-                    grad_keep[p][q, :, cols] = block
-                else:
-                    grad_send[p - pieces // 2, q, :, cols] = block
-
-            order.to_relative(meta, 1 + count, value, grad_scr, store)
-
-
-def gate_back_call(meta, order, parts, ffn, back, resid, gated, act, cot, perm, vec, weights):
-    halves, pieces = len(ffn), len(weights)
+
+
+def gate_back_call(meta, order, parts, back, resid, gated, cot, vec, weights):
+    halves, pieces = len(back), len(weights)
     micro, span, width = resid.shape
     tokens = micro * span
     chan = width // parts
     tile = lambda cols: pl.BlockSpec((1, span, cols), lambda m, _: (m, 0, 0))
-    flat = pl.BlockSpec((span, width), lambda m, _: (m, 0))
-    outs = call(
+    flat = lambda cols: pl.BlockSpec((span, cols), lambda m, _: (m, 0))
+    return call(
         functools.partial(gate_back_kernel, pieces, halves, order),
         (micro,),
         meta,
-        [flat] * (2 * halves)
-        + [tile(width), tile(2 * width), tile(width), flat]
-        + [full_spec(a.shape) for a in (perm, vec, *weights)],
-        (*ffn, *back, resid, gated, act, cot, perm, vec, *weights),
+        [flat(width)] * halves
+        + [tile(width), tile(2 * width), flat(width)]
+        + [full_spec(a.shape) for a in (vec, *weights)],
+        (*back, resid, gated, cot, vec, *weights),
         [
             tile(width),
-            tile(width),
+            flat(2 * width),
             full_spec((8, 2 * width)),
             full_spec((8, width)),
             parted(parts, span, chan),
-        ]
-        + [full_spec((parts, order.shard_rows, 2 * width))] * (pieces // 2)
-        + [full_spec((pieces // 2, parts, order.shard_rows, 2 * width))],
+        ],
         [
-            jax.ShapeDtypeStruct((micro, span, width), bf16),
             jax.ShapeDtypeStruct((micro, span, width), f32),
+            jax.ShapeDtypeStruct((tokens, 2 * width), bf16),
             jax.ShapeDtypeStruct((8, 2 * width), f32),
             jax.ShapeDtypeStruct((8, width), f32),
             jax.ShapeDtypeStruct((parts, micro * span, chan), bf16),
-        ]
-        + [jax.ShapeDtypeStruct((parts, order.shard_rows, 2 * width), bf16)] * (pieces // 2)
-        + [jax.ShapeDtypeStruct((pieces // 2, parts, order.shard_rows, 2 * width), bf16)],
-        [
-            pltpu.VMEM((width, 2 * width), bf16),
-            pltpu.VMEM((tokens, 2 * width), bf16),
-            pltpu.VMEM((tokens, width), bf16),
-            pltpu.VMEM((width, width // 2), bf16),
         ],
-        10 * tokens * width * width,
+        [pltpu.VMEM((width, 2 * width), bf16)],
+        4 * tokens * width * width,
         "gated_back",
     )
-    return outs[:5], outs[5:-1], outs[-1]
+
+
+def gate_weight_kernel(pieces, order, place, meta, act_ref, grad_ref, *refs):
+    grad_keep, grad_send, scratch = refs[: pieces // 2], refs[-2], refs[-1]
+
+    def store(p, q, block):
+        if p < pieces // 2:
+            grad_keep[p][q] = block
+        else:
+            grad_send[p - pieces // 2, q] = block
+
+    order.to_relative(meta, place, dot_left_t(act_ref[...], grad_ref[...]), scratch, store)
+
+
+def gate_weight_call(meta, order, place, act, grad_gated):
+    tokens, width = act.shape
+    pieces, parts, low = order.batch_size, order.seq_size, order.shard_rows
+    cols = width // 2
+    outs = call(
+        functools.partial(gate_weight_kernel, pieces, order, place),
+        (4,),
+        meta,
+        [full_spec(act.shape), pl.BlockSpec((tokens, cols), lambda c, _: (0, c))],
+        (act, grad_gated),
+        [pl.BlockSpec((parts, low, cols), lambda c, _: (0, 0, c))] * (pieces // 2)
+        + [pl.BlockSpec((pieces // 2, parts, low, cols), lambda c, _: (0, 0, 0, c))],
+        [jax.ShapeDtypeStruct((parts, low, 2 * width), bf16)] * (pieces // 2)
+        + [jax.ShapeDtypeStruct((pieces // 2, parts, low, 2 * width), bf16)],
+        [pltpu.VMEM((width, cols), bf16)],
+        4 * tokens * width * width,
+        "gated_weight",
+    )
+    return outs[:-1], outs[-1]
 
 
 def input_kernel(meta, moved_ref, x_ref, grad_resid_ref, perm_ref, out_ref):
@@ -1085,35 +1125,39 @@
     me_b, me_s = lax.axis_index("batch"), lax.axis_index("seq")
     me = me_b * seq_size + me_s
 
-    natural_piece = reverse_bits(jnp.arange(batch_size, dtype=jnp.int32), batch_bits) ^ me_b
-    piece_of = reverse_bits(jnp.arange(batch_size, dtype=jnp.int32) ^ me_b, batch_bits)
-    place = jnp.arange(devices, dtype=jnp.int32)
-    of_piece = reverse_bits(place // seq_size, batch_bits) ^ me_b
-    of_seq = reverse_bits(place % seq_size, seq_bits) ^ me_s
-    natural = of_piece * seq_size + of_seq
-    ramp = jnp.arange(seq_size, dtype=jnp.int32)
-    out_place = reverse_bits(ramp ^ me_s, seq_bits)
     piece_ff = ff // batch_size
-    groups = [[p for p in range(batch_size) if p % 2 == half] for half in range(2)]
-    of_group = natural_piece[jnp.array(groups[0] + groups[1])]
     place_at = 1 + micro
     in_table = 8
     out_table = in_table + devices
     base_table = out_table + seq_size
     column_table = base_table + batch_size
-    meta = jnp.concatenate(
-        [
-            me_s[None].astype(jnp.int32),
-            lengths[:, 0],
-            jnp.stack([me_s * span, me_b]).astype(jnp.int32),
-            jnp.zeros((8 - 3 - micro,), jnp.int32),
-            natural,
-            out_place,
-            of_group * (piece_ff // ff_block),
-            of_group & (batch_size // 2 - 1),
-        ]
-    )
+    chan_table = column_table + batch_size
+    pieces = np.arange(batch_size)
+    natural_piece = reverse_bits(pieces, batch_bits) ^ me_b
+    piece_of = reverse_bits(jnp.arange(batch_size, dtype=jnp.int32) ^ me_b, batch_bits)
+
+    def meta_of(parts):
+        lengths, me_b, me_s = parts
+        place = np.arange(devices)
+        of_piece = reverse_bits(place // seq_size, batch_bits) ^ me_b
+        of_seq = reverse_bits(place % seq_size, seq_bits) ^ me_s
+        halves = np.concatenate([pieces[pieces % 2 == 0], pieces[pieces % 2 == 1]])
+        of_group = reverse_bits(halves, batch_bits) ^ me_b
+        table = jnp.concatenate(
+            [
+                of_piece * seq_size + of_seq,
+                reverse_bits(np.arange(seq_size) ^ me_s, seq_bits),
+                of_group * (piece_ff // ff_block_of(piece_ff)),
+                of_group & (batch_size // 2 - 1),
+                of_seq * batch_size + place // seq_size,
+            ]
+        )
+        head = jnp.stack([me_s, *lengths[:, 0], me_s * span, me_b])
+        blank = jnp.zeros((8 - head.shape[0],), jnp.int32)
+        return jnp.concatenate([head, blank, table]).astype(jnp.int32)
+
     order = Rows(width, shard_rows, seq_size, batch_size, in_table)
+    chan_order = Rows(width, shard_rows, seq_size, batch_size, chan_table, by_channel=True)
 
     x = inputs[:, 0]
     cot = cotangent[:, 0]
@@ -1147,46 +1191,26 @@
     counts = [2 * shard_rows, shard_rows, shard_rows, shard_rows, 4 * shard_rows]
     starts = [sum(counts[:k]) for k in range(len(counts))]
     small_size = sum(counts)
-    small = jnp.concatenate(
-        [
-            glu_bias,
-            norm2_gain,
-            norm2_bias,
-            ffn_out_bias,
-            ffn_in_bias,
-            jnp.zeros((16 * chan - small_size,), bf16),
-        ]
-    )
-    glu_1 = gather_direct(glu_weight)
     in_1 = gather_first(ffn_in_weight)
+    vectors = (norm1_gain, norm1_bias, skip_gain, step_size)
+    vectors = vectors + (glu_bias, norm2_gain, norm2_bias, ffn_out_bias, ffn_in_bias)
+    vectors = jnp.concatenate([v.reshape(-1, shard_rows) for v in vectors], axis=0)
+    vectors = jnp.concatenate(gather_batch(vectors), axis=1)
+    coefs = gather_batch(state_out)
     normed, perm = norm_call(
         me_b[None].astype(jnp.int32),
         x,
-        small.reshape(16, chan),
+        jnp.pad(vectors[4:], ((0, 20 - vectors.shape[0]), (0, 0))),
         batch_bits,
         shard_rows,
         seq_size,
     )
-    normed, glu_1, in_1, ffn_out_weight, one, coefs = together(
-        (
-            normed,
-            glu_1,
-            in_1,
-            ffn_out_weight,
-            jnp.concatenate([norm1_gain, norm1_bias, skip_gain, step_size]),
-            state_out,
-        )
-    )
-
-    normed = exchange(normed)
-    glu_w = gather_more(join(glu_weight[None], *glu_1), 1)
-    glu_2 = near_swap(glu_w)
+    normed, in_1, one, coefs = together((normed, in_1, vectors[:4], coefs))
     in_w = gather_more(join(ffn_in_weight[None], in_1), 2)
     in_2 = middle_swap(in_w)
-    out_1 = gather_first(ffn_out_weight)
-    one, coefs = gather_batch(one), gather_batch(coefs)
-    one = jnp.stack(one).reshape(batch_size, 4, shard_rows).astype(f32)
-    one = jnp.moveaxis(one, 0, 1).reshape(4, chan)
+    glu_1 = gather_first(after(glu_weight, in_w))
+    meta = meta_of(after((lengths, me_b, me_s), in_w))
+    one = one.astype(f32)
     vec_one = jnp.concatenate([one[:3], jnp.zeros((5, chan), f32)], axis=0)
     coefs = jnp.concatenate(coefs, axis=1)
     coefs = jnp.swapaxes(coefs, 1, 2).astype(f32)
@@ -1195,50 +1219,57 @@
     lift = cmul((joint[0][:, None], joint[1][:, None]), far)
     fwd_np, inv_np = transform_tables(span)
     fwd, inv = jnp.asarray(fwd_np), jnp.asarray(inv_np)
-    spec = kernel_call(meta, lift, near, fwd, seq_size, span)
-    normed, glu_2, in_2, out_1, spec = together((normed, glu_2, in_2, out_1, spec))
-
-    glu_w = join(glu_w, glu_2).reshape(-1, 2 * width)
-    glu_top = top_swap(glu_w)
+    normed, in_2, glu_1, lift, near = together((normed, in_2, glu_1, lift, near))
+
+    normed = exchange(normed)
     in_w = join(in_w, in_2)
     in_3 = near_swap(in_w)
-    out_w = gather_more(join(ffn_out_weight[None], out_1), 2)
-    out_2 = middle_swap(out_w)
-    drive_spec, mixed, active = conv_call(
-        meta, micro, normed, vec_one, after(spec, glu_w, in_w, out_w), fwd, inv
-    )
-    active, glu_top, in_3, out_2 = together((active, glu_top, in_3, out_2))
-
-    small_seq = after(normed, active)[:, micro * span :, :].reshape(seq_size, -1)[:, :small_size]
-    active = exchange(active)
-    (small_top,) = swap_batch([small_seq], top)
-    in_w = join(in_w, in_3).reshape(-1, ff)
-    in_top = top_swap(after(in_w, small_top))
-    out_w = join(out_w, out_2)
-    out_3 = near_swap(out_w)
-    glu_parts = weave(over_low([glu_w]), over_low([glu_top]))
-    small_all = jnp.stack(weave(over_low([small_seq]), over_low([small_top])))
-    small_all = jnp.take(small_all, piece_of, axis=0).reshape(devices, -1).astype(f32)
+    glu_w = gather_more(join(glu_weight[None], glu_1), 2)
+    glu_2 = middle_swap(glu_w)
+    spec = kernel_call(meta, after(lift, in_w, glu_w), near, fwd, seq_size, span)
+    small_all = normed[:, micro * span :, :].astype(f32)
+    small_all = small_all.reshape(seq_size, 16, batch_size, shard_rows)
+    small_all = jnp.take(jnp.transpose(small_all, (2, 0, 1, 3)), piece_of, axis=0)
     glu_bias_all, gain_two, bias_two, out_bias, in_bias = [
-        small_all[:, s : s + c].reshape(-1) for s, c in zip(starts, counts)
+        small_all[:, :, s : s + c].reshape(-1) for s, c in ((0, 2), (2, 1), (3, 1), (4, 1), (5, 4))
     ]
     vec_two = jnp.concatenate(
         [gain_two[None], bias_two[None], out_bias[None], jnp.zeros((5, width), f32)]
     )
-    in_low = over_low([after(in_w, vec_two, glu_bias_all, in_bias, glu_parts)])
-    active, in_top, out_3, in_low = together((active, in_top, out_3, in_low))
-
+    normed, in_3, glu_2, spec, ffn_out_weight, vec_two, glu_bias_all, in_bias = together(
+        (normed, in_3, glu_2, spec, ffn_out_weight, vec_two, glu_bias_all, in_bias)
+    )
+
+    in_w = join(in_w, in_3).reshape(-1, ff)
+    in_top = top_swap(in_w)
+    glu_w = join(glu_w, glu_2)
+    glu_3 = near_swap(glu_w)
+    out_1 = gather_direct(ffn_out_weight)
+    drive_spec, mixed, active_own = conv_call(
+        meta, micro, normed, vec_one, after(spec, glu_w, in_w), fwd, inv
+    )
+    active_own, glu_3, out_1 = together((active_own, glu_3, out_1))
+
+    active = exchange(active_own)
+    out_w = gather_more(join(ffn_out_weight[None], *out_1), 1)
+    out_3 = near_swap(out_w)
+    glu_w = join(glu_w, after(glu_3, out_w)).reshape(-1, 2 * width)
+    glu_top = top_swap(after(glu_w, in_top))
+    in_parts = weave(over_low([in_w]), over_low([in_top]))
+    glu_parts = weave(over_low([glu_w]), over_low([glu_top]))
+    active, out_3, glu_parts = together((active, out_3, glu_parts))
     out_w = join(out_w, out_3).reshape(-1, width)
     out_top = top_swap(out_w)
     out_low = over_low([out_w])
-    in_parts = weave(in_low, over_low([in_top]))
+    active = after(active, out_w)
+
     act, resid, gated, norm_two, norm_two_t, cot_out = gate_call(
-        meta, order, after(active, out_w), x, cot, perm, vec_two, glu_bias_all[None], glu_parts
-    )
-
-    in_bias_blocks = in_bias.reshape(ff // ff_block, 1, ff_block)
-
-    def ffn_half(which, norm_two, weights):
+        meta, chan_order, active, x, cot, vec_two, glu_bias_all[None], glu_parts
+    )
+
+    in_bias_blocks = in_bias.reshape(-1, 1, ff_block_of(piece_ff))
+
+    def ffn_half(which, weights, **parts):
         return ffn_call(
             meta,
             order,
@@ -1246,12 +1277,9 @@
             place_at,
             base_table + which * half,
             column_table + which * half,
-            norm_two,
-            norm_two_t,
             cot_out,
-            in_bias_blocks,
-            in_parts,
             weights,
+            **parts,
         )
 
     def low_rest(values):
@@ -1270,46 +1298,53 @@
     def rounded(terms):
         return Sum(*terms).total().astype(bf16)
 
-    out_a, back_a, bias_a, grad_out_a, keep_in_a, send_in_a = ffn_half(0, norm_two, out_low)
-    out_top = after(out_top, out_a)
+    (back_a, bias_a), (out_a,), grad_out_a, keep_in_a, (send_in_a,) = ffn_half(
+        0, out_low, norm=norm_two, bias=in_bias_blocks, w_in=in_parts, norm_t=norm_two_t
+    )
+    out_high = over_low([after(out_top, back_a)])
     in_a_came = swap(send_in_a, "batch", 1)
     out_a_came = swap(out_send(grad_out_a), "batch", 1)
-    out_b, back_b, bias_b, grad_out_b, keep_in_b, send_in_b = ffn_half(
-        1, after(norm_two, out_a), over_low([out_top])
-    )
-    in_a_came, out_a_came = after((in_a_came, out_a_came), out_b)
-
-    in_b_came = swap(send_in_b, "batch", 1)
-    out_b_came = swap(out_send(grad_out_b), "batch", 1)
     in_a_own, in_a_other = low_sum(keep_in_a, in_a_came)
     in_a_other = rounded(in_a_other)
     in_b_top = top_swap(in_a_other)
-    (output, grad_resid, grad_glu_bias, sums, moved), keep_glu, send_glu = gate_back_call(
+    (back_b, bias_b), (out_b,), grad_out_b, keep_in_b, (send_in_b,) = ffn_half(
+        1,
+        out_high,
+        norm=after(norm_two, back_a, in_a_other),
+        bias=in_bias_blocks,
+        w_in=in_parts,
+        norm_t=norm_two_t,
+    )
+    back_b, in_b_top, out_a_came = together((back_b, in_b_top, out_a_came))
+
+    grad_resid, grad_gated, grad_glu_bias, sums, moved = gate_back_call(
         meta,
-        order,
+        chan_order,
         seq_size,
-        [out_a, out_b],
         [back_a, back_b],
-        after(resid, in_a_other),
+        resid,
         gated,
-        act,
         cot_out,
-        perm,
         vec_two,
         glu_parts,
     )
-    moved, in_b_came, out_b_came, in_b_top = together((moved, in_b_came, out_b_came, in_b_top))
+    grad_out_b, send_in_b = after((grad_out_b, send_in_b), moved)
+    out_b_came = swap(out_send(grad_out_b), "batch", 1)
+    in_b_came = swap(send_in_b, "batch", 1)
 
     grads_in = exchange(moved)
-    glu_came = swap(send_glu, "batch", 1)
     (out_b_sum,) = low_sum(grad_out_b[: half // 2], out_b_came)
     out_b_sum = rounded(out_b_sum)
     out_a_top = top_swap(out_b_sum)
+    keep_glu, send_glu = gate_weight_call(
+        meta, chan_order, place_at, act, after(grad_gated, out_b_sum)
+    )
     in_b_own, in_b_other = low_sum(keep_in_b, in_b_came)
-    in_b_other = rounded([after(in_b_other[0], out_b_sum), *in_b_other[1:]])
+    in_b_other = rounded([after(in_b_other[0], send_glu), *in_b_other[1:]])
     in_a_top = top_swap(in_b_other)
     sum_in_b = Sum(*in_b_own, in_b_top)
-    in_b_near = near_swap(sum_in_b.upper())
+    in_b_near = sum_in_b.upper()
+    in_b_near_came = near_swap(in_b_near)
 
     lower = (me_b >> top) == 0
 
@@ -1332,13 +1367,15 @@
     blank = jnp.zeros((seq_size, extra_rows * chan - 2 * small_grads.shape[1]), bf16)
     extra = jnp.concatenate([high.astype(bf16), rest, blank], axis=1)
     extra = extra.reshape(seq_size, extra_rows, chan)
-    grads_in, glu_came, in_b_near, extra = together((grads_in, glu_came, in_b_near, extra))
-
-    sum_in_b.keep(in_b_near)
-    in_b_middle = sum_in_b.upper()
+    (out_a_sum,) = low_sum(grad_out_a[: half // 2], out_a_came)
+    out_a_sum = [v.reshape(seq_size, -1, width) for v in out_a_sum]
+    grads_in, extra, out_a_sum, in_a_own, near, far, input_mult = together(
+        (grads_in, extra, out_a_sum, in_a_own, near, far, input_mult)
+    )
+
     moved_back, cross, state_sums = back_call(
         meta,
-        after(grads_in, in_b_middle),
+        after(grads_in, in_b_other, in_b_near),
         normed,
         drive_spec,
         mixed,
@@ -1348,62 +1385,68 @@
         inv,
         extra,
     )
-    in_b_middle = middle_swap(in_b_middle)
-    moved_back, cross, in_b_middle, out_a_top, in_a_top = together(
-        (moved_back, cross, in_b_middle, out_a_top, in_a_top)
+    moved_back, cross, in_b_near_came, out_a_top = together(
+        (moved_back, cross, in_b_near_came, out_a_top)
     )
 
     moved_back = exchange(moved_back)
-    (out_a_sum,) = low_sum(grad_out_a[: half // 2], out_a_came)
-    sum_out = Sum(*[v.reshape(seq_size, -1, width) for v in (*out_a_sum, out_a_top)])
+    glu_came = swap(after(send_glu, cross), "batch", 1)
+    sum_out = Sum(*out_a_sum, out_a_top.reshape(seq_size, -1, width))
     out_near = sum_out.upper()
     out_near_came = near_swap(out_near)
-    glu_own, glu_other = low_sum(keep_glu, glu_came)
-    glu_other = rounded([after(glu_other[0], out_near), *glu_other[1:]])
+    sum_in_b.keep(after(in_b_near_came, out_near))
+    in_b_middle = sum_in_b.upper()
+    in_b_middle_came = middle_swap(in_b_middle)
+    glu_own, glu_other = low_sum(keep_glu, after(glu_came, in_b_middle))
+    glu_other = rounded(glu_other)
     glu_top_came = top_swap(glu_other)
     sum_in_a = Sum(*in_a_own, after(in_a_top, glu_other))
-    in_a_near = near_swap(sum_in_a.upper())
-    sum_in_b.keep(in_b_middle)
+    in_a_near = sum_in_a.upper()
+    in_a_near_came = near_swap(in_a_near)
+    raw_modes = modes_call(meta, after(cross, in_a_near), far, near, inv)
+    in_b_middle_came, in_a_near_came, out_near_came, glu_top_came = after(
+        (in_b_middle_came, in_a_near_came, out_near_came, glu_top_came), raw_modes
+    )
+    sum_in_b.keep(in_b_middle_came)
     sum_in_b.middle()
-    in_b_last = last_swap(sum_in_b.upper())
-    moved_back, out_near_came, glu_top_came, in_a_near, in_b_last = together(
-        (moved_back, out_near_came, glu_top_came, in_a_near, in_b_last)
-    )
-
-    sum_out.keep(out_near_came)
+    in_b_last = sum_in_b.upper()
+    in_b_last_came = last_swap(in_b_last)
+    sum_in_a.keep(after(in_a_near_came, in_b_last))
+    in_a_middle = sum_in_a.upper()
+    in_a_middle_came = middle_swap(in_a_middle)
+    sum_glu = Sum(*glu_own, after(glu_top_came, in_a_middle))
+    glu_near = sum_glu.upper()
+    glu_near_came = near_swap(glu_near)
+    sum_out.keep(after(out_near_came, glu_near))
     out_middle = sum_out.upper()
-    sum_in_a.keep(in_a_near)
-    in_a_middle = sum_in_a.upper()
-    sum_glu = Sum(*glu_own, glu_top_came)
-    glu_near = sum_glu.upper()
-    input_grad = input_call(
-        meta, after(moved_back, out_middle, in_a_middle, glu_near), x, grad_resid, perm
-    )
-    out_middle, in_a_middle = middle_swap(out_middle), middle_swap(in_a_middle)
-    glu_near = near_swap(glu_near)
-    input_grad, out_middle, in_a_middle, glu_near = together(
-        (input_grad, out_middle, in_a_middle, glu_near)
-    )
-
-    sum_out.keep(out_middle)
+    out_middle_came = middle_swap(out_middle)
+
+    input_grad = input_call(meta, after(moved_back, out_middle), x, grad_resid, perm)
+    input_grad, in_a_middle_came, glu_near_came, out_middle_came = together(
+        (input_grad, in_a_middle_came, glu_near_came, out_middle_came)
+    )
+    sum_glu.keep(glu_near_came)
+    glu_middle = sum_glu.upper()
+    glu_middle_came = middle_swap(glu_middle)
+    sum_in_a.keep(after(in_a_middle_came, glu_middle))
+    sum_in_a.middle()
+    in_a_last = sum_in_a.upper()
+    in_a_last_came = last_swap(in_a_last)
+    sum_out.keep(after(out_middle_came, in_a_last))
     sum_out.middle()
     out_last = sum_out.upper()
-    sum_in_a.keep(in_a_middle)
-    sum_in_a.middle()
-    in_a_last = sum_in_a.upper()
-    sum_glu.keep(glu_near)
-    glu_middle = sum_glu.upper()
-    raw_modes = modes_call(
-        meta, after(cross, input_grad, out_last, in_a_last, glu_middle), far, near, inv
-    )
-    out_last, in_a_last = last_swap(out_last), last_swap(in_a_last)
-    glu_middle = middle_swap(glu_middle)
-    raw_modes, out_last, in_a_last, glu_middle = together(
-        (raw_modes, out_last, in_a_last, glu_middle)
-    )
-    sum_glu.keep(glu_middle)
+    out_last_came = last_swap(out_last)
+    sum_glu.keep(after(glu_middle_came, out_last))
     sum_glu.middle()
-    glu_last = last_swap(sum_glu.upper())
+    glu_last = sum_glu.upper()
+    glu_last_came = last_swap(glu_last)
+    out_a, out_b, resid = after((out_a, out_b, resid), glu_last)
+    output = resid + (out_a + out_b + vec_two[2:3]).reshape(resid.shape)
+    output = output.astype(bf16)
+    in_a_last_came, out_last_came, in_b_last_came = after(
+        (in_a_last_came, out_last_came, in_b_last_came), output
+    )
+    raw_modes, state_sums = after((raw_modes, state_sums), input_grad)
 
     def finish(value, came):
         value.keep(came)
@@ -1413,10 +1456,10 @@
     state_grads = jnp.concatenate([z[0], -z[1], state_sums[:3]], axis=0).T
     state_grads = reduce_batch(state_grads.reshape(batch_size, shard_rows, -1))
     grad_state = jnp.stack([state_grads[:, :mode_count], state_grads[:, mode_count : 2 * mode_count]])
-    grad_out_total = finish(sum_out, out_last)
-    far_in = halves(finish(sum_in_a, in_a_last), finish(sum_in_b, in_b_last), 0)
+    grad_out_total = finish(sum_out, out_last_came)
+    far_in = halves(finish(sum_in_a, in_a_last_came), finish(sum_in_b, in_b_last_came), 0)
     grad_in_total = jnp.concatenate([far_in[b] for b in range(batch_size)], axis=1)
-    grad_glu_total = finish(sum_glu, glu_last)
+    grad_glu_total = finish(sum_glu, glu_last_came)
 
     small_came = moved_back[:, micro * span :, :].reshape(seq_size, -1).astype(f32)
     small_came = jnp.sum(small_came, axis=0)

time: 528 us -> 474 us (0.90)
  waiting for transfers between devices: 131 us -> 101 us
  Pallas kernels: 210 us -> 186 us
    ppermute x53 -> x50, waiting for transfers between devices: 128 us -> 78.6 us  [swap(): return lax.ppermute(value, axis, [(i, i ^ bit) for i in range(size)])]
    pallas_call x10 -> x11, Pallas kernels: 210 us -> 186 us  [call(): pl.pallas_call(kernel, grid_spec=pltpu.PrefetchScalarGridSpec(num_scalar_...]
    all_to_all x4, waiting for transfers between devices: 3 us -> 22.5 us  [exchange(): return lax.all_to_all(parts, 'seq', 0, 0)]
    unnamed x109 -> x118, local copies, waits for them, and re-layouts: 10.6 us -> 9.17 us
    ppermute x53 -> x50, starting transfers between devices: 52 us -> 53.1 us  [swap(): return lax.ppermute(value, axis, [(i, i ^ bit) for i in range(size)])]
  transfers between devices with their start and end apart: 57 -> 54, of which waited for: 14 -> 18; matrix products, arithmetic and copies ran while one was open for 15% -> 18% of each run, Pallas kernels for 40% -> 37%
where the time goes in v2:
time: 474 us; the launch traced here: 467 us
  Pallas kernels  186 us (39%)
  waiting for transfers between devices  101 us (21%)
  starting transfers between devices  76 us (16%)
  other arithmetic  68.4 us (14%)
  local copies, waits for them, and re-layouts  33.1 us (7%)
    pallas_call x11, Pallas kernels, call(): pl.pallas_call(kernel, grid_spec=pltpu.PrefetchScalarGridSpec(num_scalar_...  186 us
    ppermute x50, waiting for transfers between devices, swap(): return lax.ppermute(value, axis, [(i, i ^ bit) for i in range(size)])  78.6 us
    ppermute x50, starting transfers between devices, swap(): return lax.ppermute(value, axis, [(i, i ^ bit) for i in range(size)])  53.1 us
    all_to_all x4, starting transfers between devices, exchange(): return lax.all_to_all(parts, 'seq', 0, 0)  22.9 us
    all_to_all x4, waiting for transfers between devices, exchange(): return lax.all_to_all(parts, 'seq', 0, 0)  22.5 us
    convert_element_type x12, other arithmetic, upper(): return self.total(self.terms[0].shape[0] // 2).astype(bf16)  21.3 us
    convert_element_type x4, other arithmetic, rounded(): return Sum(*terms).total().astype(bf16)  12.9 us
  transfers between devices with their start and end apart: 54, of which 18 were waited for; matrix products, arithmetic and copies ran while one was open for 18% of the time, Pallas kernels for 37%

profile of v2, /device:TPU:0, one launch (start us, length us, event | category | flops | bytes accessed | tf_op | source)
XLA Modules:
  0.0 466.6 jit_solution(16297347162124087120)
XLA Ops:
  3.6 3.0 collective-permute-start
  13.1 5.6 %norm_one.1 = (bf16[8,784,128]{2,1,0:T(8,128)(2,1)}, bf16[1024,1024]{1,0:T(8,128)(2,1)}) custom-call(s32[1]{0:T(128)} %bitcast.1.meta, bf16[3,256,1024]{2,1,0:T(8,128)(2,1)} %bitcast.207, bf16[16,128]{1,0:T(8,128)(2,1)} %pad.5.extra_ref), custom_call_target="tpu_custom_call" | custom-call | flops 32212254 | bytes 80530 | tf_op jit(solution)/shard_map/norm_one/pallas_call | solution.py:202
  18.7 4.7 %collective-permute-done.3 = bf16[1,32,4096]{2,1,0:T(8,128)(2,1)S(1)} collective-permute-done((bf16[1,32,4096]{2,1,0:T(8,128)(2,1)}, bf16[1,32,4096]{2,1,0:T(8,128)(2,1)S(1)}, u32[]{:S(2)}, u32[]{:S(2)}) %collective-permute-start.3) | collective-permute-done | bytes 262176 | tf_op jit(solution)/shard_map/ppermute | solution.py:44
  26.1 3.3 collective-permute-start.8
  41.6 6.4 %all-to-all-start = ((bf16[8,784,128]{2,1,0:T(8,128)(2,1)}), bf16[8,784,128]{2,1,0:T(8,128)(2,1)S(1)}, u32[]{:S(2)}, u32[]{:S(2)}) async-start(bf16[8,784,128]{2,1,0:T(8,128)(2,1)} %get-tuple-element.162), calls=%async_computation | async-start | bytes 3211264 | tf_op jit(solution)/shard_map/all_to_all | solution.py:106
  56.7 16.8 %state_kernel.1.spec_ref = f32[8,2,256,128]{3,2,1,0:T(8,128)} custom-call(s32[88]{0:T(128)} %concatenate.77.meta, f32[64,32,128]{2,1,0:T(8,128)} %get-tuple-element.166.lift_re, f32[64,32,128]{2,1,0:T(8,128)} %get-tuple-element.168.lift_im, f32[64,64,128]{2,1,0:T(8,128)} %get-tuple-element.253.near_re, f32[64,64,128]{2,1,0:T(8,128)} %get-tuple-element.254.near_im, ...), custom_call_target="tpu_custom_call" | custom-call | flops 220000000 | bytes 550000 | tf_op jit(solution)/shard_map/state_kernel/pallas_call | solution.py:202
  73.5 11.6 %all-to-all-done.normed_ref = bf16[8,784,128]{2,1,0:T(8,128)(2,1)S(1)} async-done(((bf16[8,784,128]{2,1,0:T(8,128)(2,1)}), bf16[8,784,128]{2,1,0:T(8,128)(2,1)S(1)}, u32[]{:S(2)}, u32[]{:S(2)}) %all-to-all-start) | async-done | bytes 1605664 | tf_op jit(solution)/shard_map/all_to_all | solution.py:106
  101.6 12.9 %state_conv.1 = (f32[3,8,512,128]{3,2,1,0:T(8,128)}, f32[3,8,256,128]{3,2,1,0:T(8,128)}, bf16[8,768,128]{2,1,0:T(8,128)(2,1)}) custom-call(s32[88]{0:T(128)} %concatenate.77.meta, bf16[8,784,128]{2,1,0:T(8,128)(2,1)} %copy-done.1, f32[8,128]{1,0:T(8,128)} %concatenate.82.vec_ref, f32[8,2,256,128]{3,2,1,0:T(8,128)} %state_kernel.1.spec_ref, ...), custom_call_target="tpu_custom_call" | custom-call | flops 300000000 | bytes 750000 | tf_op jit(solution)/shard_map/state_conv/pallas_call | solution.py:202
  115.6 8.1 %all-to-all-start.1 = ((bf16[8,768,128]{2,1,0:T(8,128)(2,1)}), bf16[8,768,128]{2,1,0:T(8,128)(2,1)}, u32[]{:S(2)}, u32[]{:S(2)}) async-start(bf16[8,768,128]{2,1,0:T(8,128)(2,1)} %get-tuple-element.178), calls=%async_computation.1 | async-start | bytes 3145728 | tf_op jit(solution)/shard_map/all_to_all | solution.py:106
  126.1 11.9 %collective-permute-done.16.refs_6_ = bf16[256,4096]{1,0:T(8,128)(2,1)} collective-permute-done((bf16[256,4096]{1,0:T(8,128)(2,1)S(1)}, bf16[256,4096]{1,0:T(8,128)(2,1)}, u32[]{:S(2)}, u32[]{:S(2)}) %collective-permute-start.16) | collective-permute-done | bytes 2097184 | tf_op jit(solution)/shard_map/ppermute | solution.py:44
  141.5 19.2 %collective-permute-done.17.refs_6_.refs_7_ = bf16[256,2048]{1,0:T(8,128)(2,1)} collective-permute-done((bf16[256,2048]{1,0:T(8,128)(2,1)S(1)}, bf16[256,2048]{1,0:T(8,128)(2,1)}, u32[]{:S(2)}, u32[]{:S(2)}) %collective-permute-start.17) | collective-permute-done | bytes 1048608 | tf_op jit(solution)/shard_map/ppermute | solution.py:44
  163.7 7.0 %collective-permute-done.15 = bf16[4,128,1024]{2,1,0:T(8,128)(2,1)} collective-permute-done((bf16[4,128,1024]{2,1,0:T(8,128)(2,1)S(1)}, bf16[4,128,1024]{2,1,0:T(8,128)(2,1)}, u32[]{:S(2)}, u32[]{:S(2)}) %collective-permute-start.15) | collective-permute-done | bytes 1048608 | tf_op jit(solution)/shard_map/ppermute | solution.py:44
  173.6 11.9 %gated_unit.1 = (bf16[768,1024]{1,0:T(8,128)(2,1)}, f32[3,256,1024]{2,1,0:T(8,128)}, f32[3,256,2048]{2,1,0:T(8,128)}, bf16[768,1024]{1,0:T(8,128)(2,1)}, bf16[10...) custom-call(s32[88]{0:T(128)} %concatenate.77.meta, bf16[8,768,128]{2,1,0:T(8,128)(2,1)} %all-to-all-done.1.refs_0_, ...), custom_call_target="tpu_custom_call" | custom-call | flops 96636768 | bytes 241591 | tf_op jit(solution)/shard_map/gated_unit/pallas_call | solution.py:202
  185.5 34.5 %feed_forward.2 = (f32[768,1024]{1,0:T(8,128)}, f32[2,1,1024]{2,1,0:T(1,128)}, f32[768,1024]{1,0:T(8,128)}, bf16[1024,1024]{1,0:T(8,128)(2,1)}, bf16[1024,1024]{...) custom-call(s32[88]{0:T(128)} %concatenate.77.meta, ...), custom_call_target="tpu_custom_call" | custom-call | flops 386547072 | bytes 966367 | tf_op jit(solution)/shard_map/feed_forward/pallas_call | solution.py:202
  224.5 3.3 fusion.4
  231.8 34.1 %feed_forward.3 = (f32[768,1024]{1,0:T(8,128)}, f32[2,1,1024]{2,1,0:T(1,128)}, f32[768,1024]{1,0:T(8,128)}, bf16[1024,1024]{1,0:T(8,128)(2,1)}, bf16[1024,1024]{...) custom-call(s32[88]{0:T(128)} %concatenate.77.meta, ...), custom_call_target="tpu_custom_call" | custom-call | flops 386547072 | bytes 966367 | tf_op jit(solution)/shard_map/feed_forward/pallas_call | solution.py:202
  265.9 14.8 %gated_back.1 = (f32[3,256,1024]{2,1,0:T(8,128)}, bf16[768,2048]{1,0:T(8,128)(2,1)}, f32[8,2048]{1,0:T(8,128)}, f32[8,1024]{1,0:T(8,128)}, bf16[8,768,128]{2,1,0:T(8,128)(2,1)}) custom-call(s32[88]{0:T(128)} %concatenate.77.meta, f32[768,1024]{1,0:T(8,128)} %get-tuple-element.200.refs_0_, f32[768,1024]{1,0:T(8,128)} %get-tuple-element.207.refs_1_, ...), custom_call_target="tpu_custom_call" | custom-call | flops 64424508 | bytes 161061 | tf_op jit(solution)/shard_map/gated_back/pallas_call | solution.py:202
  281.4 4.3 all-to-all-start.2
  288.1 3.9 fusion
  301.1 8.2 %gated_weight.1 = (bf16[8,32,2048]{2,1,0:T(8,128)(2,1)}, bf16[8,32,2048]{2,1,0:T(8,128)(2,1)}, bf16[2,8,32,2048]{3,2,1,0:T(8,128)(2,1)}) custom-call(s32[88]{0:T(128)} %concatenate.77.meta, bf16[768,1024]{1,0:T(8,128)(2,1)} %get-tuple-element.195.act_ref, bf16[768,2048]{1,0:T(8,128)(2,1)} %get-tuple-element.215.grad_ref), custom_call_target="tpu_custom_call" | custom-call | flops 64424508 | bytes 161061 | tf_op jit(solution)/shard_map/gated_weight/pallas_call | solution.py:202
  309.3 3.0 fusion.3
  312.3 10.9 %all-to-all-done.2.grads_ref = bf16[8,768,128]{2,1,0:T(8,128)(2,1)S(1)} async-done(((bf16[8,768,128]{2,1,0:T(8,128)(2,1)}), bf16[8,768,128]{2,1,0:T(8,128)(2,1)S(1)}, u32[]{:S(2)}, u32[]{:S(2)}) %all-to-all-start.2) | async-done | bytes 1572896 | tf_op jit(solution)/shard_map/all_to_all | solution.py:106
  324.3 21.0 %state_back.1 = (bf16[8,800,128]{2,1,0:T(8,128)(2,1)}, f32[8,512,128]{2,1,0:T(8,128)}, f32[8,128]{1,0:T(8,128)}) custom-call(s32[88]{0:T(128)} %concatenate.77.meta, bf16[8,768,128]{2,1,0:T(8,128)(2,1)} %copy-done.5, bf16[8,784,128]{2,1,0:T(8,128)(2,1)} %copy-done.1, f32[3,8,512,128]{3,2,1,0:T(8,128)} %get-tuple-element.233.drive_ref, ...), custom_call_target="tpu_custom_call" | custom-call | flops 400000000 | bytes 1000000 | tf_op jit(solution)/shard_map/state_back/pallas_call | solution.py:202
  346.1 4.0 all-to-all-start.3
  354.9 3.0 fusion.2
  365.3 10.8 %collective-permute-done.34 = bf16[8,2,32,1024]{3,2,1,0:T(8,128)(2,1)S(1)} collective-permute-done((bf16[8,2,32,1024]{3,2,1,0:T(8,128)(2,1)}, bf16[8,2,32,1024]{3,2,1,0:T(8,128)(2,1)S(1)}, u32[]{:S(2)}, u32[]{:S(2)}) %collective-permute-start.34) | collective-permute-done | bytes 1048608 | tf_op jit(solution)/shard_map/ppermute | solution.py:44
  380.4 18.4 %state_modes.1 = f32[2,64,128]{2,1,0:T(8,128)} custom-call(s32[88]{0:T(128)} %concatenate.77.meta, f32[8,512,128]{2,1,0:T(8,128)} %get-tuple-element.250.cross_ref, f32[64,32,128]{2,1,0:T(8,128)} %get-tuple-element.251.far_re, f32[64,32,128]{2,1,0:T(8,128)} %get-tuple-element.252.far_im, f32[64,64,128]{2,1,0:T(8,128)} %get-tuple-element.253.near_re, ...), custom_call_target="tpu_custom_call" | custom-call | flops 220000000 | bytes 550000 | tf_op jit(solution)/shard_map/state_modes/pallas_call | solution.py:202
  415.4 7.7 %input_grad.1 = bf16[3,256,1024]{2,1,0:T(8,128)(2,1)} custom-call(s32[88]{0:T(128)} %concatenate.77.meta, bf16[8,800,128]{2,1,0:T(8,128)(2,1)} %copy-done.4, bf16[3,256,1024]{2,1,0:T(8,128)(2,1)} %bitcast.209, f32[3,256,1024]{2,1,0:T(8,128)} %get-tuple-element.264.grad_resid_ref, bf16[1024,1024]{1,0:T(8,128)(2,1)} %get-tuple-element.265.perm_ref), custom_call_target="tpu_custom_call" | custom-call | flops 32212254 | bytes 80530 | tf_op jit(solution)/shard_map/input_grad/pallas_call | solution.py:202
  423.1 4.8 %collective-permute-done.40 = bf16[2,128,1024]{2,1,0:T(8,128)(2,1)S(1)} collective-permute-done((bf16[2,128,1024]{2,1,0:T(8,128)(2,1)S(1)}, bf16[2,128,1024]{2,1,0:T(8,128)(2,1)S(1)}, u32[]{:S(2)}, u32[]{:S(2)}) %collective-permute-start.40) | collective-permute-done | bytes 524320 | tf_op jit(solution)/shard_map/ppermute | solution.py:44
  432.0 4.0 collective-permute-start.47
  443.9 4.0 add_add_fusion
  449.6 7.8 %collective-permute-done.49 = bf16[1,128,1024]{2,1,0:T(8,128)(2,1)S(1)} collective-permute-done((bf16[1,128,1024]{2,1,0:T(8,128)(2,1)S(1)}, bf16[1,128,1024]{2,1,0:T(8,128)(2,1)S(1)}, u32[]{:S(2)}, u32[]{:S(2)}) %collective-permute-start.49) | collective-permute-done | bytes 262176 | tf_op jit(solution)/shard_map/ppermute | solution.py:44
  (336 shorter events, 139.4 us)
Async XLA Ops:
  41.6 43.5 %all-to-all-start = ((bf16[8,784,128]{2,1,0:T(8,128)(2,1)}), bf16[8,784,128]{2,1,0:T(8,128)(2,1)S(1)}, u32[]{:S(2)}, u32[]{:S(2)}) async-start(bf16[8,784,128]{2,1,0:T(8,128)(2,1)} %get-tuple-element.162), calls=%async_computation | async-start | bytes 3211264 | tf_op jit(solution)/shard_map/all_to_all | solution.py:106
  52.5 37.8 %collective-permute-start.9 = (bf16[4,32,4096]{2,1,0:T(8,128)(2,1)}, bf16[4,32,4096]{2,1,0:T(8,128)(2,1)}, u32[]{:S(2)}, u32[]{:S(2)}) collective-permute-start(bf16[4,32,4096]{2,1,0:T(8,128)(2,1)} %pad_maximum_fusion.1), channel_id=1, source_target_pairs={{0,1},{1,0},{2,3},{3,2},{4,5},{5,4},{6,7},{7,6},{8,9},{9,8},{10,11... | collective-permute-start | bytes 3145736 | tf_op jit(solution)/shard_map/ppermute | solution.py:44
  55.2 35.1 %collective-permute-start.10 = (bf16[2,32,2048]{2,1,0:T(8,128)(2,1)}, bf16[2,32,2048]{2,1,0:T(8,128)(2,1)}, u32[]{:S(2)}, u32[]{:S(2)}) collective-permute-start(bf16[2,32,2048]{2,1,0:T(8,128)(2,1)} %pad_maximum_fusion.7), channel_id=1, source_target_pairs={{0,2},{1,3},{2,0},{3,1},{4,6},{5,7},{6,4},{7,5},{8,10},{9,11},{10,... | collective-permute-start | bytes 786440 | tf_op jit(solution)/shard_map/ppermute | solution.py:44
  91.8 46.2 %collective-permute-start.16 = (bf16[256,4096]{1,0:T(8,128)(2,1)S(1)}, bf16[256,4096]{1,0:T(8,128)(2,1)}, u32[]{:S(2)}, u32[]{:S(2)}) collective-permute-start(bf16[256,4096]{1,0:T(8,128)(2,1)S(1)} %bitcast.203), channel_id=1, source_target_pairs={{0,16},{8,24},{16,0},{24,8},{1,17},{9,25},{17,1},{25,9},{2,18},{10... | collective-permute-start | bytes 6291464 | tf_op jit(solution)/shard_map/ppermute | solution.py:44
  95.2 20.5 %collective-permute-start.11 = (bf16[4,32,2048]{2,1,0:T(8,128)(2,1)}, bf16[4,32,2048]{2,1,0:T(8,128)(2,1)}, u32[]{:S(2)}, u32[]{:S(2)}) collective-permute-start(bf16[4,32,2048]{2,1,0:T(8,128)(2,1)} %pad_maximum_fusion.5), channel_id=1, source_target_pairs={{0,1},{1,0},{2,3},{3,2},{4,5},{5,4},{6,7},{7,6},{8,9},{9,8},{10,11... | collective-permute-start | bytes 1572872 | tf_op jit(solution)/shard_map/ppermute | solution.py:44
  96.6 17.9 %collective-permute-start.12 = (bf16[1,128,1024]{2,1,0:T(8,128)(2,1)S(1)}, bf16[1,128,1024]{2,1,0:T(8,128)(2,1)S(1)}, u32[]{:S(2)}, u32[]{:S(2)}) collective-permute-start(bf16[1,128,1024]{2,1,0:T(8,128)(2,1)S(1)} %bitcast.236), channel_id=1, source_target_pairs={{0,4},{1,5},{2,6},{3,7},{4,0},{5,1},{6,2},{7,3},{8,12},{9,13},{10,... | collective-permute-start | bytes 786440 | tf_op jit(solution)/shard_map/ppermute | solution.py:44
  97.2 18.4 %collective-permute-start.13 = (bf16[1,128,1024]{2,1,0:T(8,128)(2,1)S(1)}, bf16[1,128,1024]{2,1,0:T(8,128)(2,1)S(1)}, u32[]{:S(2)}, u32[]{:S(2)}) collective-permute-start(bf16[1,128,1024]{2,1,0:T(8,128)(2,1)S(1)} %bitcast.237), channel_id=1, source_target_pairs={{0,2},{1,3},{2,0},{3,1},{4,6},{5,7},{6,4},{7,5},{8,10},{9,11},{10,... | collective-permute-start | bytes 786440 | tf_op jit(solution)/shard_map/ppermute | solution.py:44
  98.8 16.9 %collective-permute-start.14 = (bf16[1,128,1024]{2,1,0:T(8,128)(2,1)S(1)}, bf16[1,128,1024]{2,1,0:T(8,128)(2,1)S(1)}, u32[]{:S(2)}, u32[]{:S(2)}) collective-permute-start(bf16[1,128,1024]{2,1,0:T(8,128)(2,1)S(1)} %bitcast.238), channel_id=1, source_target_pairs={{0,6},{1,7},{2,4},{3,5},{4,2},{5,3},{6,0},{7,1},{8,14},{9,15},{10,... | collective-permute-start | bytes 786440 | tf_op jit(solution)/shard_map/ppermute | solution.py:44
  115.6 55.1 %all-to-all-start.1 = ((bf16[8,768,128]{2,1,0:T(8,128)(2,1)}), bf16[8,768,128]{2,1,0:T(8,128)(2,1)}, u32[]{:S(2)}, u32[]{:S(2)}) async-start(bf16[8,768,128]{2,1,0:T(8,128)(2,1)} %get-tuple-element.178), calls=%async_computation.1 | async-start | bytes 3145728 | tf_op jit(solution)/shard_map/all_to_all | solution.py:106
  138.0 22.7 %collective-permute-start.17 = (bf16[256,2048]{1,0:T(8,128)(2,1)S(1)}, bf16[256,2048]{1,0:T(8,128)(2,1)}, u32[]{:S(2)}, u32[]{:S(2)}) collective-permute-start(bf16[256,2048]{1,0:T(8,128)(2,1)S(1)} %bitcast.211), channel_id=1, source_target_pairs={{0,16},{8,24},{16,0},{24,8},{1,17},{9,25},{17,1},{25,9},{2,18},{10... | collective-permute-start | bytes 3145736 | tf_op jit(solution)/shard_map/ppermute | solution.py:44
  139.5 22.0 %collective-permute-start.18 = (bf16[256,2048]{1,0:T(8,128)(2,1)S(1)}, bf16[256,2048]{1,0:T(8,128)(2,1)S(1)}, u32[]{:S(2)}, u32[]{:S(2)}) collective-permute-start(bf16[256,2048]{1,0:T(8,128)(2,1)S(1)} %bitcast.212), channel_id=1, source_target_pairs={{0,8},{8,0},{16,24},{24,16},{1,9},{9,1},{17,25},{25,17},{2,10},{10... | collective-permute-start | bytes 3145736 | tf_op jit(solution)/shard_map/ppermute | solution.py:44
  139.5 31.2 %collective-permute-start.15 = (bf16[4,128,1024]{2,1,0:T(8,128)(2,1)S(1)}, bf16[4,128,1024]{2,1,0:T(8,128)(2,1)}, u32[]{:S(2)}, u32[]{:S(2)}) collective-permute-start(bf16[4,128,1024]{2,1,0:T(8,128)(2,1)S(1)} %pad_maximum_fusion.2), channel_id=1, source_target_pairs={{0,1},{1,0},{2,3},{3,2},{4,5},{5,4},{6,7},{7,6},{8,9},{9,8},{10,11... | collective-permute-start | bytes 3145736 | tf_op jit(solution)/shard_map/ppermute | solution.py:44
  160.7 24.8 %collective-permute-start.21 = (bf16[256,4096]{1,0:T(8,128)(2,1)S(1)}, bf16[256,4096]{1,0:T(8,128)(2,1)}, u32[]{:S(2)}, u32[]{:S(2)}) collective-permute-start(bf16[256,4096]{1,0:T(8,128)(2,1)S(1)} %bitcast.204), channel_id=1, source_target_pairs={{0,8},{8,0},{16,24},{24,16},{1,9},{9,1},{17,25},{25,17},{2,10},{10... | collective-permute-start | bytes 6291464 | tf_op jit(solution)/shard_map/ppermute | solution.py:44
  161.4 24.1 %collective-permute-start.22 = (bf16[256,4096]{1,0:T(8,128)(2,1)}, bf16[256,4096]{1,0:T(8,128)(2,1)}, u32[]{:S(2)}, u32[]{:S(2)}) collective-permute-start(bf16[256,4096]{1,0:T(8,128)(2,1)} %collective-permute-done.16.refs_6_), channel_id=1, source_target_pairs={{0,8},{8,0},{16,24},{24,16},{1,9},{9,1},{17,25},{25,17},{2,10},{10... | collective-permute-start | bytes 6291464 | tf_op jit(solution)/shard_map/ppermute | solution.py:44
  173.0 48.4 %collective-permute-start.23 = (bf16[1024,1024]{1,0:T(8,128)(2,1)}, bf16[1024,1024]{1,0:T(8,128)(2,1)}, u32[]{:S(2)}, u32[]{:S(2)}) collective-permute-start(bf16[1024,1024]{1,0:T(8,128)(2,1)} %bitcast.217), channel_id=1, source_target_pairs={{0,16},{8,24},{16,0},{24,8},{1,17},{9,25},{17,1},{25,9},{2,18},{10... | collective-permute-start | bytes 6291464 | tf_op jit(solution)/shard_map/ppermute | solution.py:44
  221.3 44.6 %collective-permute-start.27 = (bf16[1,1024,1024]{2,1,0:T(8,128)(2,1)}, bf16[1,1024,1024]{2,1,0:T(8,128)(2,1)}, u32[]{:S(2)}, u32[]{:S(2)}) collective-permute-start(bf16[1,1024,1024]{2,1,0:T(8,128)(2,1)} %bitcast.257), channel_id=1, source_target_pairs={{0,8},{8,0},{16,24},{24,16},{1,9},{9,1},{17,25},{25,17},{2,10},{10... | collective-permute-start | bytes 6291464 | tf_op jit(solution)/shard_map/ppermute | solution.py:44
  227.8 38.1 %collective-permute-start.26 = (bf16[8,2,32,1024]{3,2,1,0:T(8,128)(2,1)}, bf16[8,2,32,1024]{3,2,1,0:T(8,128)(2,1)S(1)}, u32[]{:S(2)}, u32[]{:S(2)}) collective-permute-start(bf16[8,2,32,1024]{3,2,1,0:T(8,128)(2,1)} %fusion.4), channel_id=1, source_target_pairs={{0,16},{8,24},{16,0},{24,8},{1,17},{9,25},{17,1},{25,9},{2,18},{10... | collective-permute-start | bytes 3145736 | tf_op jit(solution)/shard_map/ppermute | solution.py:44
  281.4 41.8 %all-to-all-start.2 = ((bf16[8,768,128]{2,1,0:T(8,128)(2,1)}), bf16[8,768,128]{2,1,0:T(8,128)(2,1)S(1)}, u32[]{:S(2)}, u32[]{:S(2)}) async-start(bf16[8,768,128]{2,1,0:T(8,128)(2,1)} %get-tuple-element.211), calls=%async_computation.2 | async-start | bytes 3145728 | tf_op jit(solution)/shard_map/all_to_all | solution.py:106
  292.0 53.3 %collective-permute-start.31 = (bf16[1024,1024]{1,0:T(8,128)(2,1)}, bf16[1024,1024]{1,0:T(8,128)(2,1)}, u32[]{:S(2)}, u32[]{:S(2)}) collective-permute-start(bf16[1024,1024]{1,0:T(8,128)(2,1)} %fusion), channel_id=1, source_target_pairs={{0,16},{8,24},{16,0},{24,8},{1,17},{9,25},{17,1},{25,9},{2,18},{10... | collective-permute-start | bytes 6291464 | tf_op jit(solution)/shard_map/ppermute | solution.py:44
  298.4 46.9 %collective-permute-start.30 = (bf16[4,2,32,1024]{3,2,1,0:T(8,128)(2,1)}, bf16[4,2,32,1024]{3,2,1,0:T(8,128)(2,1)S(1)}, u32[]{:S(2)}, u32[]{:S(2)}) collective-permute-start(bf16[4,2,32,1024]{3,2,1,0:T(8,128)(2,1)} %fusion.10), channel_id=1, source_target_pairs={{0,1},{1,0},{2,3},{3,2},{4,5},{5,4},{6,7},{7,6},{8,9},{9,8},{10,11... | collective-permute-start | bytes 1572872 | tf_op jit(solution)/shard_map/ppermute | solution.py:44
  345.3 17.4 %collective-permute-start.32 = (bf16[2,8,32,2048]{3,2,1,0:T(8,128)(2,1)}, bf16[2,8,32,2048]{3,2,1,0:T(8,128)(2,1)}, u32[]{:S(2)}, u32[]{:S(2)}) collective-permute-start(bf16[2,8,32,2048]{3,2,1,0:T(8,128)(2,1)} %get-tuple-element.239), channel_id=1, source_target_pairs={{0,8},{8,0},{16,24},{24,16},{1,9},{9,1},{17,25},{25,17},{2,10},{10... | collective-permute-start | bytes 6291464 | tf_op jit(solution)/shard_map/ppermute | solution.py:44
  346.1 52.7 %all-to-all-start.3 = ((bf16[8,800,128]{2,1,0:T(8,128)(2,1)}), bf16[8,800,128]{2,1,0:T(8,128)(2,1)S(1)}, u32[]{:S(2)}, u32[]{:S(2)}) async-start(bf16[8,800,128]{2,1,0:T(8,128)(2,1)} %get-tuple-element.260), calls=%async_computation.3 | async-start | bytes 3276800 | tf_op jit(solution)/shard_map/all_to_all | solution.py:106
  351.0 25.0 %collective-permute-start.34 = (bf16[8,2,32,1024]{3,2,1,0:T(8,128)(2,1)}, bf16[8,2,32,1024]{3,2,1,0:T(8,128)(2,1)S(1)}, u32[]{:S(2)}, u32[]{:S(2)}) collective-permute-start(bf16[8,2,32,1024]{3,2,1,0:T(8,128)(2,1)} %fusion.3), channel_id=1, source_target_pairs={{0,16},{8,24},{16,0},{24,8},{1,17},{9,25},{17,1},{25,9},{2,18},{10... | collective-permute-start | bytes 3145736 | tf_op jit(solution)/shard_map/ppermute | solution.py:44
  357.8 43.7 %collective-permute-start.37 = (bf16[4,128,1024]{2,1,0:T(8,128)(2,1)}, bf16[4,128,1024]{2,1,0:T(8,128)(2,1)}, u32[]{:S(2)}, u32[]{:S(2)}) collective-permute-start(bf16[4,128,1024]{2,1,0:T(8,128)(2,1)} %fusion.2), channel_id=1, source_target_pairs={{0,1},{1,0},{2,3},{3,2},{4,5},{5,4},{6,7},{7,6},{8,9},{9,8},{10,11... | collective-permute-start | bytes 3145736 | tf_op jit(solution)/shard_map/ppermute | solution.py:44
  361.2 37.7 %collective-permute-start.36 = (bf16[2,2,32,1024]{3,2,1,0:T(8,128)(2,1)S(1)}, bf16[2,2,32,1024]{3,2,1,0:T(8,128)(2,1)S(1)}, u32[]{:S(2)}, u32[]{:S(2)}) collective-permute-start(bf16[2,2,32,1024]{3,2,1,0:T(8,128)(2,1)S(1)} %fusion.23), channel_id=1, source_target_pairs={{0,2},{1,3},{2,0},{3,1},{4,6},{5,7},{6,4},{7,5},{8,10},{9,11},{10,... | collective-permute-start | bytes 786440 | tf_op jit(solution)/shard_map/ppermute | solution.py:44
  377.2 27.4 %collective-permute-start.35 = (bf16[4,2,32,1024]{3,2,1,0:T(8,128)(2,1)}, bf16[4,2,32,1024]{3,2,1,0:T(8,128)(2,1)}, u32[]{:S(2)}, u32[]{:S(2)}) collective-permute-start(bf16[4,2,32,1024]{3,2,1,0:T(8,128)(2,1)} %add_convert_fusion.1), channel_id=1, source_target_pairs={{0,1},{1,0},{2,3},{3,2},{4,5},{5,4},{6,7},{7,6},{8,9},{9,8},{10,11... | collective-permute-start | bytes 1572872 | tf_op jit(solution)/shard_map/ppermute | solution.py:44
  378.9 29.4 %collective-permute-start.33 = (bf16[8,32,2048]{2,1,0:T(8,128)(2,1)}, bf16[8,32,2048]{2,1,0:T(8,128)(2,1)}, u32[]{:S(2)}, u32[]{:S(2)}) collective-permute-start(bf16[8,32,2048]{2,1,0:T(8,128)(2,1)} %fusion.1), channel_id=1, source_target_pairs={{0,16},{8,24},{16,0},{24,8},{1,17},{9,25},{17,1},{25,9},{2,18},{10... | collective-permute-start | bytes 3145736 | tf_op jit(solution)/shard_map/ppermute | solution.py:44
  401.5 55.9 %collective-permute-start.48 = (bf16[1,2,32,1024]{3,2,1,0:T(8,128)(2,1)}, bf16[1,2,32,1024]{3,2,1,0:T(8,128)(2,1)}, u32[]{:S(2)}, u32[]{:S(2)}) collective-permute-start(bf16[1,2,32,1024]{3,2,1,0:T(8,128)(2,1)} %fusion.39), channel_id=1, source_target_pairs={{0,4},{1,5},{2,6},{3,7},{4,0},{5,1},{6,2},{7,3},{8,12},{9,13},{10,... | collective-permute-start | bytes 393224 | tf_op jit(solution)/shard_map/ppermute | solution.py:44
  410.6 17.3 %collective-permute-start.39 = (bf16[4,32,2048]{2,1,0:T(8,128)(2,1)}, bf16[4,32,2048]{2,1,0:T(8,128)(2,1)}, u32[]{:S(2)}, u32[]{:S(2)}) collective-permute-start(bf16[4,32,2048]{2,1,0:T(8,128)(2,1)} %fusion.6), channel_id=1, source_target_pairs={{0,1},{1,0},{2,3},{3,2},{4,5},{5,4},{6,7},{7,6},{8,9},{9,8},{10,11... | collective-permute-start | bytes 1572872 | tf_op jit(solution)/shard_map/ppermute | solution.py:44
  432.0 25.4 %collective-permute-start.47 = (bf16[1,2,32,1024]{3,2,1,0:T(8,128)(2,1)}, bf16[1,2,32,1024]{3,2,1,0:T(8,128)(2,1)S(1)}, u32[]{:S(2)}, u32[]{:S(2)}) collective-permute-start(bf16[1,2,32,1024]{3,2,1,0:T(8,128)(2,1)} %add_convert_fusion.3), channel_id=1, source_target_pairs={{0,4},{1,5},{2,6},{3,7},{4,0},{5,1},{6,2},{7,3},{8,12},{9,13},{10,... | collective-permute-start | bytes 393224 | tf_op jit(solution)/shard_map/ppermute | solution.py:44
  438.2 19.2 %collective-permute-start.49 = (bf16[1,128,1024]{2,1,0:T(8,128)(2,1)S(1)}, bf16[1,128,1024]{2,1,0:T(8,128)(2,1)S(1)}, u32[]{:S(2)}, u32[]{:S(2)}) collective-permute-start(bf16[1,128,1024]{2,1,0:T(8,128)(2,1)S(1)} %fusion.17), channel_id=1, source_target_pairs={{0,4},{1,5},{2,6},{3,7},{4,0},{5,1},{6,2},{7,3},{8,12},{9,13},{10,... | collective-permute-start | bytes 786440 | tf_op jit(solution)/shard_map/ppermute | solution.py:44
  442.8 21.5 %collective-permute-start.44 = (bf16[1,32,2048]{2,1,0:T(8,128)(2,1)S(1)}, bf16[1,32,2048]{2,1,0:T(8,128)(2,1)S(1)}, u32[]{:S(2)}, u32[]{:S(2)}) collective-permute-start(bf16[1,32,2048]{2,1,0:T(8,128)(2,1)S(1)} %fusion.43), channel_id=1, source_target_pairs={{0,4},{1,5},{2,6},{3,7},{4,0},{5,1},{6,2},{7,3},{8,12},{9,13},{10,... | collective-permute-start | bytes 393224 | tf_op jit(solution)/shard_map/ppermute | solution.py:44
  (78 other events, 839.2 us)

commit v3 on v2

--- a/solution.py
+++ b/solution.py
@@ -1219,7 +1219,7 @@
     lift = cmul((joint[0][:, None], joint[1][:, None]), far)
     fwd_np, inv_np = transform_tables(span)
     fwd, inv = jnp.asarray(fwd_np), jnp.asarray(inv_np)
-    normed, in_2, glu_1, lift, near = together((normed, in_2, glu_1, lift, near))
+    in_2, glu_1, lift, near = together((in_2, glu_1, lift, near))
 
     normed = exchange(normed)
     in_w = join(in_w, in_2)
@@ -1425,18 +1425,18 @@
     input_grad, in_a_middle_came, glu_near_came, out_middle_came = together(
         (input_grad, in_a_middle_came, glu_near_came, out_middle_came)
     )
-    sum_glu.keep(glu_near_came)
+    sum_out.keep(out_middle_came)
+    sum_out.middle()
+    out_last = sum_out.upper()
+    out_last_came = last_swap(out_last)
+    sum_glu.keep(after(glu_near_came, out_last))
     glu_middle = sum_glu.upper()
     glu_middle_came = middle_swap(glu_middle)
     sum_in_a.keep(after(in_a_middle_came, glu_middle))
     sum_in_a.middle()
     in_a_last = sum_in_a.upper()
     in_a_last_came = last_swap(in_a_last)
-    sum_out.keep(after(out_middle_came, in_a_last))
-    sum_out.middle()
-    out_last = sum_out.upper()
-    out_last_came = last_swap(out_last)
-    sum_glu.keep(after(glu_middle_came, out_last))
+    sum_glu.keep(after(glu_middle_came, in_a_last))
     sum_glu.middle()
     glu_last = sum_glu.upper()
     glu_last_came = last_swap(glu_last)

time: 474 us -> 461 us (0.973)
  starting transfers between devices: 76 us -> 70.4 us
  waiting for transfers between devices: 101 us -> 95.5 us
    all_to_all x4, waiting for transfers between devices: 22.5 us -> 14.5 us  [exchange(): return lax.all_to_all(parts, 'seq', 0, 0)]
  transfers between devices with their start and end apart: 54 -> 54, of which waited for: 18 -> 17; matrix products, arithmetic and copies ran while one was open for 18% -> 19% of each run, Pallas kernels for 37% -> 37%
where the time goes in v3:
time: 461 us; the launch traced here: 457 us
  Pallas kernels  186 us (40%)
  waiting for transfers between devices  95.5 us (21%)
  other arithmetic  71.9 us (16%)
  starting transfers between devices  70.4 us (15%)
  local copies, waits for them, and re-layouts  31.4 us (7%)
    pallas_call x11, Pallas kernels, call(): pl.pallas_call(kernel, grid_spec=pltpu.PrefetchScalarGridSpec(num_scalar_...  186 us
    ppermute x50, waiting for transfers between devices, swap(): return lax.ppermute(value, axis, [(i, i ^ bit) for i in range(size)])  81.1 us
    ppermute x50, starting transfers between devices, swap(): return lax.ppermute(value, axis, [(i, i ^ bit) for i in range(size)])  49.7 us
    all_to_all x4, starting transfers between devices, exchange(): return lax.all_to_all(parts, 'seq', 0, 0)  20.7 us
    convert_element_type x12, other arithmetic, upper(): return self.total(self.terms[0].shape[0] // 2).astype(bf16)  20.6 us
    all_to_all x4, waiting for transfers between devices, exchange(): return lax.all_to_all(parts, 'seq', 0, 0)  14.5 us
    convert_element_type x4, other arithmetic, rounded(): return Sum(*terms).total().astype(bf16)  12.8 us
    concatenate x7, other arithmetic, join(): return jnp.concatenate(parts, axis=0)  9.43 us
  transfers between devices with their start and end apart: 54, of which 17 were waited for; matrix products, arithmetic and copies ran while one was open for 19% of the time, Pallas kernels for 37%

profile of v3, /device:TPU:0, one launch (start us, length us, event | category | flops | bytes accessed | tf_op | source)
XLA Modules:
  0.0 457.0 jit_solution(7855562063561464338)
XLA Ops:
  3.6 3.0 collective-permute-start
  14.3 5.6 %norm_one.1 = (bf16[8,784,128]{2,1,0:T(8,128)(2,1)}, bf16[1024,1024]{1,0:T(8,128)(2,1)}) custom-call(s32[1]{0:T(128)} %bitcast.1.meta, bf16[3,256,1024]{2,1,0:T(8,128)(2,1)} %bitcast.207, bf16[16,128]{1,0:T(8,128)(2,1)} %pad.5.extra_ref), custom_call_target="tpu_custom_call" | custom-call | flops 32212254 | bytes 80530 | tf_op jit(solution)/shard_map/norm_one/pallas_call | solution.py:202
  19.9 3.5 collective-permute-done.3
  26.2 3.3 collective-permute-start.8
  29.5 4.1 all-to-all-start
  53.8 16.8 %state_kernel.1.spec_ref = f32[8,2,256,128]{3,2,1,0:T(8,128)} custom-call(s32[88]{0:T(128)} %concatenate.77.meta, f32[64,32,128]{2,1,0:T(8,128)} %get-tuple-element.164.lift_re, f32[64,32,128]{2,1,0:T(8,128)} %get-tuple-element.166.lift_im, f32[64,64,128]{2,1,0:T(8,128)} %get-tuple-element.251.near_re, f32[64,64,128]{2,1,0:T(8,128)} %get-tuple-element.252.near_im, ...), custom_call_target="tpu_custom_call" | custom-call | flops 220000000 | bytes 550000 | tf_op jit(solution)/shard_map/state_kernel/pallas_call | solution.py:202
  70.6 3.4 all-to-all-done.normed_ref
  86.3 3.3 collective-permute-start.12
  92.5 12.9 %state_conv.1 = (f32[3,8,512,128]{3,2,1,0:T(8,128)}, f32[3,8,256,128]{3,2,1,0:T(8,128)}, bf16[8,768,128]{2,1,0:T(8,128)(2,1)}) custom-call(s32[88]{0:T(128)} %concatenate.77.meta, bf16[8,784,128]{2,1,0:T(8,128)(2,1)} %copy-done.1, f32[8,128]{1,0:T(8,128)} %concatenate.82.vec_ref, f32[8,2,256,128]{3,2,1,0:T(8,128)} %state_kernel.1.spec_ref, ...), custom_call_target="tpu_custom_call" | custom-call | flops 300000000 | bytes 750000 | tf_op jit(solution)/shard_map/state_conv/pallas_call | solution.py:202
  107.3 7.7 %all-to-all-start.1 = ((bf16[8,768,128]{2,1,0:T(8,128)(2,1)}), bf16[8,768,128]{2,1,0:T(8,128)(2,1)}, u32[]{:S(2)}, u32[]{:S(2)}) async-start(bf16[8,768,128]{2,1,0:T(8,128)(2,1)} %get-tuple-element.176), calls=%async_computation.1 | async-start | bytes 3145728 | tf_op jit(solution)/shard_map/all_to_all | solution.py:106
  116.5 13.4 %collective-permute-done.16.refs_6_ = bf16[256,4096]{1,0:T(8,128)(2,1)} collective-permute-done((bf16[256,4096]{1,0:T(8,128)(2,1)S(1)}, bf16[256,4096]{1,0:T(8,128)(2,1)}, u32[]{:S(2)}, u32[]{:S(2)}) %collective-permute-start.16) | collective-permute-done | bytes 2097184 | tf_op jit(solution)/shard_map/ppermute | solution.py:44
  131.4 22.1 %collective-permute-done.17.refs_6_.refs_7_ = bf16[256,2048]{1,0:T(8,128)(2,1)} collective-permute-done((bf16[256,2048]{1,0:T(8,128)(2,1)S(1)}, bf16[256,2048]{1,0:T(8,128)(2,1)}, u32[]{:S(2)}, u32[]{:S(2)}) %collective-permute-start.17) | collective-permute-done | bytes 1048608 | tf_op jit(solution)/shard_map/ppermute | solution.py:44
  156.4 4.5 collective-permute-done.15
  164.0 11.9 %gated_unit.1 = (bf16[768,1024]{1,0:T(8,128)(2,1)}, f32[3,256,1024]{2,1,0:T(8,128)}, f32[3,256,2048]{2,1,0:T(8,128)}, bf16[768,1024]{1,0:T(8,128)(2,1)}, bf16[10...) custom-call(s32[88]{0:T(128)} %concatenate.77.meta, bf16[8,768,128]{2,1,0:T(8,128)(2,1)} %all-to-all-done.1.refs_0_, ...), custom_call_target="tpu_custom_call" | custom-call | flops 96636768 | bytes 241591 | tf_op jit(solution)/shard_map/gated_unit/pallas_call | solution.py:202
  176.0 34.1 %feed_forward.2 = (f32[768,1024]{1,0:T(8,128)}, f32[2,1,1024]{2,1,0:T(1,128)}, f32[768,1024]{1,0:T(8,128)}, bf16[1024,1024]{1,0:T(8,128)(2,1)}, bf16[1024,1024]{...) custom-call(s32[88]{0:T(128)} %concatenate.77.meta, ...), custom_call_target="tpu_custom_call" | custom-call | flops 386547072 | bytes 966367 | tf_op jit(solution)/shard_map/feed_forward/pallas_call | solution.py:202
  214.5 3.3 fusion.4
  221.8 34.2 %feed_forward.3 = (f32[768,1024]{1,0:T(8,128)}, f32[2,1,1024]{2,1,0:T(1,128)}, f32[768,1024]{1,0:T(8,128)}, bf16[1024,1024]{1,0:T(8,128)(2,1)}, bf16[1024,1024]{...) custom-call(s32[88]{0:T(128)} %concatenate.77.meta, ...), custom_call_target="tpu_custom_call" | custom-call | flops 386547072 | bytes 966367 | tf_op jit(solution)/shard_map/feed_forward/pallas_call | solution.py:202
  256.0 15.0 %gated_back.1 = (f32[3,256,1024]{2,1,0:T(8,128)}, bf16[768,2048]{1,0:T(8,128)(2,1)}, f32[8,2048]{1,0:T(8,128)}, f32[8,1024]{1,0:T(8,128)}, bf16[8,768,128]{2,1,0:T(8,128)(2,1)}) custom-call(s32[88]{0:T(128)} %concatenate.77.meta, f32[768,1024]{1,0:T(8,128)} %get-tuple-element.198.refs_0_, f32[768,1024]{1,0:T(8,128)} %get-tuple-element.205.refs_1_, ...), custom_call_target="tpu_custom_call" | custom-call | flops 64424508 | bytes 161061 | tf_op jit(solution)/shard_map/gated_back/pallas_call | solution.py:202
  271.7 5.0 %all-to-all-start.2 = ((bf16[8,768,128]{2,1,0:T(8,128)(2,1)}), bf16[8,768,128]{2,1,0:T(8,128)(2,1)S(1)}, u32[]{:S(2)}, u32[]{:S(2)}) async-start(bf16[8,768,128]{2,1,0:T(8,128)(2,1)} %get-tuple-element.209), calls=%async_computation.2 | async-start | bytes 3145728 | tf_op jit(solution)/shard_map/all_to_all | solution.py:106
  279.1 3.9 fusion
  292.0 8.1 %gated_weight.1 = (bf16[8,32,2048]{2,1,0:T(8,128)(2,1)}, bf16[8,32,2048]{2,1,0:T(8,128)(2,1)}, bf16[2,8,32,2048]{3,2,1,0:T(8,128)(2,1)}) custom-call(s32[88]{0:T(128)} %concatenate.77.meta, bf16[768,1024]{1,0:T(8,128)(2,1)} %get-tuple-element.193.act_ref, bf16[768,2048]{1,0:T(8,128)(2,1)} %get-tuple-element.213.grad_ref), custom_call_target="tpu_custom_call" | custom-call | flops 64424508 | bytes 161061 | tf_op jit(solution)/shard_map/gated_weight/pallas_call | solution.py:202
  300.1 3.0 fusion.3
  303.1 11.0 %all-to-all-done.2.grads_ref = bf16[8,768,128]{2,1,0:T(8,128)(2,1)S(1)} async-done(((bf16[8,768,128]{2,1,0:T(8,128)(2,1)}), bf16[8,768,128]{2,1,0:T(8,128)(2,1)S(1)}, u32[]{:S(2)}, u32[]{:S(2)}) %all-to-all-start.2) | async-done | bytes 1572896 | tf_op jit(solution)/shard_map/all_to_all | solution.py:106
  315.3 21.0 %state_back.1 = (bf16[8,800,128]{2,1,0:T(8,128)(2,1)}, f32[8,512,128]{2,1,0:T(8,128)}, f32[8,128]{1,0:T(8,128)}) custom-call(s32[88]{0:T(128)} %concatenate.77.meta, bf16[8,768,128]{2,1,0:T(8,128)(2,1)} %copy-done.5, bf16[8,784,128]{2,1,0:T(8,128)(2,1)} %copy-done.1, f32[3,8,512,128]{3,2,1,0:T(8,128)} %get-tuple-element.231.drive_ref, ...), custom_call_target="tpu_custom_call" | custom-call | flops 400000000 | bytes 1000000 | tf_op jit(solution)/shard_map/state_back/pallas_call | solution.py:202
  337.1 3.9 all-to-all-start.3
  345.8 3.0 fusion.2
  356.1 10.8 %collective-permute-done.34 = bf16[8,2,32,1024]{3,2,1,0:T(8,128)(2,1)S(1)} collective-permute-done((bf16[8,2,32,1024]{3,2,1,0:T(8,128)(2,1)}, bf16[8,2,32,1024]{3,2,1,0:T(8,128)(2,1)S(1)}, u32[]{:S(2)}, u32[]{:S(2)}) %collective-permute-start.34) | collective-permute-done | bytes 1048608 | tf_op jit(solution)/shard_map/ppermute | solution.py:44
  371.2 18.4 %state_modes.1 = f32[2,64,128]{2,1,0:T(8,128)} custom-call(s32[88]{0:T(128)} %concatenate.77.meta, f32[8,512,128]{2,1,0:T(8,128)} %get-tuple-element.248.cross_ref, f32[64,32,128]{2,1,0:T(8,128)} %get-tuple-element.249.far_re, f32[64,32,128]{2,1,0:T(8,128)} %get-tuple-element.250.far_im, f32[64,64,128]{2,1,0:T(8,128)} %get-tuple-element.251.near_re, ...), custom_call_target="tpu_custom_call" | custom-call | flops 220000000 | bytes 550000 | tf_op jit(solution)/shard_map/state_modes/pallas_call | solution.py:202
  406.3 7.7 %input_grad.1 = bf16[3,256,1024]{2,1,0:T(8,128)(2,1)} custom-call(s32[88]{0:T(128)} %concatenate.77.meta, bf16[8,800,128]{2,1,0:T(8,128)(2,1)} %copy-done.4, bf16[3,256,1024]{2,1,0:T(8,128)(2,1)} %bitcast.209, f32[3,256,1024]{2,1,0:T(8,128)} %get-tuple-element.262.grad_resid_ref, bf16[1024,1024]{1,0:T(8,128)(2,1)} %get-tuple-element.263.perm_ref), custom_call_target="tpu_custom_call" | custom-call | flops 32212254 | bytes 80530 | tf_op jit(solution)/shard_map/input_grad/pallas_call | solution.py:202
  414.1 4.7 %collective-permute-done.40 = bf16[2,128,1024]{2,1,0:T(8,128)(2,1)S(1)} collective-permute-done((bf16[2,128,1024]{2,1,0:T(8,128)(2,1)S(1)}, bf16[2,128,1024]{2,1,0:T(8,128)(2,1)S(1)}, u32[]{:S(2)}, u32[]{:S(2)}) %collective-permute-start.40) | collective-permute-done | bytes 524320 | tf_op jit(solution)/shard_map/ppermute | solution.py:44
  432.1 9.6 %collective-permute-done.41 = bf16[2,32,2048]{2,1,0:T(8,128)(2,1)} collective-permute-done((bf16[2,32,2048]{2,1,0:T(8,128)(2,1)S(1)}, bf16[2,32,2048]{2,1,0:T(8,128)(2,1)}, u32[]{:S(2)}, u32[]{:S(2)}) %collective-permute-start.41) | collective-permute-done | bytes 262176 | tf_op jit(solution)/shard_map/ppermute | solution.py:44
  443.0 4.0 add_add_fusion
  (338 shorter events, 138.8 us)
Async XLA Ops:
  25.2 22.4 %collective-permute-start.7 = (bf16[2,32,4096]{2,1,0:T(8,128)(2,1)}, bf16[2,32,4096]{2,1,0:T(8,128)(2,1)S(1)}, u32[]{:S(2)}, u32[]{:S(2)}) collective-permute-start(bf16[2,32,4096]{2,1,0:T(8,128)(2,1)} %pad_maximum_fusion.4), channel_id=1, source_target_pairs={{0,2},{1,3},{2,0},{3,1},{4,6},{5,7},{6,4},{7,5},{8,10},{9,11},{10,... | collective-permute-start | bytes 1572872 | tf_op jit(solution)/shard_map/ppermute | solution.py:44
  26.2 21.4 %collective-permute-start.8 = (bf16[1,32,2048]{2,1,0:T(8,128)(2,1)}, bf16[1,32,2048]{2,1,0:T(8,128)(2,1)}, u32[]{:S(2)}, u32[]{:S(2)}) collective-permute-start(bf16[1,32,2048]{2,1,0:T(8,128)(2,1)} %bitcast.16), channel_id=1, source_target_pairs={{0,4},{1,5},{2,6},{3,7},{4,0},{5,1},{6,2},{7,3},{8,12},{9,13},{10,... | collective-permute-start | bytes 393224 | tf_op jit(solution)/shard_map/ppermute | solution.py:44
  29.5 44.5 %all-to-all-start = ((bf16[8,784,128]{2,1,0:T(8,128)(2,1)}), bf16[8,784,128]{2,1,0:T(8,128)(2,1)S(1)}, u32[]{:S(2)}, u32[]{:S(2)}) async-start(bf16[8,784,128]{2,1,0:T(8,128)(2,1)} %get-tuple-element.154), calls=%async_computation | async-start | bytes 3211264 | tf_op jit(solution)/shard_map/all_to_all | solution.py:106
  48.7 32.8 %collective-permute-start.9 = (bf16[4,32,4096]{2,1,0:T(8,128)(2,1)}, bf16[4,32,4096]{2,1,0:T(8,128)(2,1)}, u32[]{:S(2)}, u32[]{:S(2)}) collective-permute-start(bf16[4,32,4096]{2,1,0:T(8,128)(2,1)} %pad_maximum_fusion.1), channel_id=1, source_target_pairs={{0,1},{1,0},{2,3},{3,2},{4,5},{5,4},{6,7},{7,6},{8,9},{9,8},{10,11... | collective-permute-start | bytes 3145736 | tf_op jit(solution)/shard_map/ppermute | solution.py:44
  52.3 26.9 %collective-permute-start.10 = (bf16[2,32,2048]{2,1,0:T(8,128)(2,1)}, bf16[2,32,2048]{2,1,0:T(8,128)(2,1)}, u32[]{:S(2)}, u32[]{:S(2)}) collective-permute-start(bf16[2,32,2048]{2,1,0:T(8,128)(2,1)} %pad_maximum_fusion.7), channel_id=1, source_target_pairs={{0,2},{1,3},{2,0},{3,1},{4,6},{5,7},{6,4},{7,5},{8,10},{9,11},{10,... | collective-permute-start | bytes 786440 | tf_op jit(solution)/shard_map/ppermute | solution.py:44
  82.9 47.0 %collective-permute-start.16 = (bf16[256,4096]{1,0:T(8,128)(2,1)S(1)}, bf16[256,4096]{1,0:T(8,128)(2,1)}, u32[]{:S(2)}, u32[]{:S(2)}) collective-permute-start(bf16[256,4096]{1,0:T(8,128)(2,1)S(1)} %bitcast.203), channel_id=1, source_target_pairs={{0,16},{8,24},{16,0},{24,8},{1,17},{9,25},{17,1},{25,9},{2,18},{10... | collective-permute-start | bytes 6291464 | tf_op jit(solution)/shard_map/ppermute | solution.py:44
  86.3 20.9 %collective-permute-start.11 = (bf16[4,32,2048]{2,1,0:T(8,128)(2,1)}, bf16[4,32,2048]{2,1,0:T(8,128)(2,1)}, u32[]{:S(2)}, u32[]{:S(2)}) collective-permute-start(bf16[4,32,2048]{2,1,0:T(8,128)(2,1)} %pad_maximum_fusion.5), channel_id=1, source_target_pairs={{0,1},{1,0},{2,3},{3,2},{4,5},{5,4},{6,7},{7,6},{8,9},{9,8},{10,11... | collective-permute-start | bytes 1572872 | tf_op jit(solution)/shard_map/ppermute | solution.py:44
  86.3 20.9 %collective-permute-start.12 = (bf16[1,128,1024]{2,1,0:T(8,128)(2,1)S(1)}, bf16[1,128,1024]{2,1,0:T(8,128)(2,1)S(1)}, u32[]{:S(2)}, u32[]{:S(2)}) collective-permute-start(bf16[1,128,1024]{2,1,0:T(8,128)(2,1)S(1)} %bitcast.232), channel_id=1, source_target_pairs={{0,4},{1,5},{2,6},{3,7},{4,0},{5,1},{6,2},{7,3},{8,12},{9,13},{10,... | collective-permute-start | bytes 786440 | tf_op jit(solution)/shard_map/ppermute | solution.py:44
  89.6 17.6 %collective-permute-start.13 = (bf16[1,128,1024]{2,1,0:T(8,128)(2,1)S(1)}, bf16[1,128,1024]{2,1,0:T(8,128)(2,1)S(1)}, u32[]{:S(2)}, u32[]{:S(2)}) collective-permute-start(bf16[1,128,1024]{2,1,0:T(8,128)(2,1)S(1)} %bitcast.233), channel_id=1, source_target_pairs={{0,2},{1,3},{2,0},{3,1},{4,6},{5,7},{6,4},{7,5},{8,10},{9,11},{10,... | collective-permute-start | bytes 786440 | tf_op jit(solution)/shard_map/ppermute | solution.py:44
  107.3 53.6 %all-to-all-start.1 = ((bf16[8,768,128]{2,1,0:T(8,128)(2,1)}), bf16[8,768,128]{2,1,0:T(8,128)(2,1)}, u32[]{:S(2)}, u32[]{:S(2)}) async-start(bf16[8,768,128]{2,1,0:T(8,128)(2,1)} %get-tuple-element.176), calls=%async_computation.1 | async-start | bytes 3145728 | tf_op jit(solution)/shard_map/all_to_all | solution.py:106
  129.9 23.6 %collective-permute-start.17 = (bf16[256,2048]{1,0:T(8,128)(2,1)S(1)}, bf16[256,2048]{1,0:T(8,128)(2,1)}, u32[]{:S(2)}, u32[]{:S(2)}) collective-permute-start(bf16[256,2048]{1,0:T(8,128)(2,1)S(1)} %bitcast.211), channel_id=1, source_target_pairs={{0,16},{8,24},{16,0},{24,8},{1,17},{9,25},{17,1},{25,9},{2,18},{10... | collective-permute-start | bytes 3145736 | tf_op jit(solution)/shard_map/ppermute | solution.py:44
  131.4 22.8 %collective-permute-start.18 = (bf16[256,2048]{1,0:T(8,128)(2,1)S(1)}, bf16[256,2048]{1,0:T(8,128)(2,1)S(1)}, u32[]{:S(2)}, u32[]{:S(2)}) collective-permute-start(bf16[256,2048]{1,0:T(8,128)(2,1)S(1)} %bitcast.212), channel_id=1, source_target_pairs={{0,8},{8,0},{16,24},{24,16},{1,9},{9,1},{17,25},{25,17},{2,10},{10... | collective-permute-start | bytes 3145736 | tf_op jit(solution)/shard_map/ppermute | solution.py:44
  131.4 29.5 %collective-permute-start.15 = (bf16[4,128,1024]{2,1,0:T(8,128)(2,1)S(1)}, bf16[4,128,1024]{2,1,0:T(8,128)(2,1)}, u32[]{:S(2)}, u32[]{:S(2)}) collective-permute-start(bf16[4,128,1024]{2,1,0:T(8,128)(2,1)S(1)} %pad_maximum_fusion.2), channel_id=1, source_target_pairs={{0,1},{1,0},{2,3},{3,2},{4,5},{5,4},{6,7},{7,6},{8,9},{9,8},{10,11... | collective-permute-start | bytes 3145736 | tf_op jit(solution)/shard_map/ppermute | solution.py:44
  153.5 22.5 %collective-permute-start.21 = (bf16[256,4096]{1,0:T(8,128)(2,1)S(1)}, bf16[256,4096]{1,0:T(8,128)(2,1)}, u32[]{:S(2)}, u32[]{:S(2)}) collective-permute-start(bf16[256,4096]{1,0:T(8,128)(2,1)S(1)} %bitcast.204), channel_id=1, source_target_pairs={{0,8},{8,0},{16,24},{24,16},{1,9},{9,1},{17,25},{25,17},{2,10},{10... | collective-permute-start | bytes 6291464 | tf_op jit(solution)/shard_map/ppermute | solution.py:44
  154.1 21.8 %collective-permute-start.22 = (bf16[256,4096]{1,0:T(8,128)(2,1)}, bf16[256,4096]{1,0:T(8,128)(2,1)}, u32[]{:S(2)}, u32[]{:S(2)}) collective-permute-start(bf16[256,4096]{1,0:T(8,128)(2,1)} %collective-permute-done.16.refs_6_), channel_id=1, source_target_pairs={{0,8},{8,0},{16,24},{24,16},{1,9},{9,1},{17,25},{25,17},{2,10},{10... | collective-permute-start | bytes 6291464 | tf_op jit(solution)/shard_map/ppermute | solution.py:44
  163.2 48.3 %collective-permute-start.23 = (bf16[1024,1024]{1,0:T(8,128)(2,1)}, bf16[1024,1024]{1,0:T(8,128)(2,1)}, u32[]{:S(2)}, u32[]{:S(2)}) collective-permute-start(bf16[1024,1024]{1,0:T(8,128)(2,1)} %bitcast.217), channel_id=1, source_target_pairs={{0,16},{8,24},{16,0},{24,8},{1,17},{9,25},{17,1},{25,9},{2,18},{10... | collective-permute-start | bytes 6291464 | tf_op jit(solution)/shard_map/ppermute | solution.py:44
  211.5 44.5 %collective-permute-start.27 = (bf16[1,1024,1024]{2,1,0:T(8,128)(2,1)}, bf16[1,1024,1024]{2,1,0:T(8,128)(2,1)}, u32[]{:S(2)}, u32[]{:S(2)}) collective-permute-start(bf16[1,1024,1024]{2,1,0:T(8,128)(2,1)} %bitcast.253), channel_id=1, source_target_pairs={{0,8},{8,0},{16,24},{24,16},{1,9},{9,1},{17,25},{25,17},{2,10},{10... | collective-permute-start | bytes 6291464 | tf_op jit(solution)/shard_map/ppermute | solution.py:44
  217.9 38.2 %collective-permute-start.26 = (bf16[8,2,32,1024]{3,2,1,0:T(8,128)(2,1)}, bf16[8,2,32,1024]{3,2,1,0:T(8,128)(2,1)S(1)}, u32[]{:S(2)}, u32[]{:S(2)}) collective-permute-start(bf16[8,2,32,1024]{3,2,1,0:T(8,128)(2,1)} %fusion.4), channel_id=1, source_target_pairs={{0,16},{8,24},{16,0},{24,8},{1,17},{9,25},{17,1},{25,9},{2,18},{10... | collective-permute-start | bytes 3145736 | tf_op jit(solution)/shard_map/ppermute | solution.py:44
  271.7 42.5 %all-to-all-start.2 = ((bf16[8,768,128]{2,1,0:T(8,128)(2,1)}), bf16[8,768,128]{2,1,0:T(8,128)(2,1)S(1)}, u32[]{:S(2)}, u32[]{:S(2)}) async-start(bf16[8,768,128]{2,1,0:T(8,128)(2,1)} %get-tuple-element.209), calls=%async_computation.2 | async-start | bytes 3145728 | tf_op jit(solution)/shard_map/all_to_all | solution.py:106
  283.0 53.3 %collective-permute-start.31 = (bf16[1024,1024]{1,0:T(8,128)(2,1)}, bf16[1024,1024]{1,0:T(8,128)(2,1)}, u32[]{:S(2)}, u32[]{:S(2)}) collective-permute-start(bf16[1024,1024]{1,0:T(8,128)(2,1)} %fusion), channel_id=1, source_target_pairs={{0,16},{8,24},{16,0},{24,8},{1,17},{9,25},{17,1},{25,9},{2,18},{10... | collective-permute-start | bytes 6291464 | tf_op jit(solution)/shard_map/ppermute | solution.py:44
  289.3 47.0 %collective-permute-start.30 = (bf16[4,2,32,1024]{3,2,1,0:T(8,128)(2,1)}, bf16[4,2,32,1024]{3,2,1,0:T(8,128)(2,1)S(1)}, u32[]{:S(2)}, u32[]{:S(2)}) collective-permute-start(bf16[4,2,32,1024]{3,2,1,0:T(8,128)(2,1)} %fusion.10), channel_id=1, source_target_pairs={{0,1},{1,0},{2,3},{3,2},{4,5},{5,4},{6,7},{7,6},{8,9},{9,8},{10,11... | collective-permute-start | bytes 1572872 | tf_op jit(solution)/shard_map/ppermute | solution.py:44
  337.1 52.6 %all-to-all-start.3 = ((bf16[8,800,128]{2,1,0:T(8,128)(2,1)}), bf16[8,800,128]{2,1,0:T(8,128)(2,1)S(1)}, u32[]{:S(2)}, u32[]{:S(2)}) async-start(bf16[8,800,128]{2,1,0:T(8,128)(2,1)} %get-tuple-element.258), calls=%async_computation.3 | async-start | bytes 3276800 | tf_op jit(solution)/shard_map/all_to_all | solution.py:106
  342.0 25.0 %collective-permute-start.34 = (bf16[8,2,32,1024]{3,2,1,0:T(8,128)(2,1)}, bf16[8,2,32,1024]{3,2,1,0:T(8,128)(2,1)S(1)}, u32[]{:S(2)}, u32[]{:S(2)}) collective-permute-start(bf16[8,2,32,1024]{3,2,1,0:T(8,128)(2,1)} %fusion.3), channel_id=1, source_target_pairs={{0,16},{8,24},{16,0},{24,8},{1,17},{9,25},{17,1},{25,9},{2,18},{10... | collective-permute-start | bytes 3145736 | tf_op jit(solution)/shard_map/ppermute | solution.py:44
  348.7 43.7 %collective-permute-start.37 = (bf16[4,128,1024]{2,1,0:T(8,128)(2,1)}, bf16[4,128,1024]{2,1,0:T(8,128)(2,1)}, u32[]{:S(2)}, u32[]{:S(2)}) collective-permute-start(bf16[4,128,1024]{2,1,0:T(8,128)(2,1)} %fusion.2), channel_id=1, source_target_pairs={{0,1},{1,0},{2,3},{3,2},{4,5},{5,4},{6,7},{7,6},{8,9},{9,8},{10,11... | collective-permute-start | bytes 3145736 | tf_op jit(solution)/shard_map/ppermute | solution.py:44
  352.0 37.6 %collective-permute-start.36 = (bf16[2,2,32,1024]{3,2,1,0:T(8,128)(2,1)S(1)}, bf16[2,2,32,1024]{3,2,1,0:T(8,128)(2,1)S(1)}, u32[]{:S(2)}, u32[]{:S(2)}) collective-permute-start(bf16[2,2,32,1024]{3,2,1,0:T(8,128)(2,1)S(1)} %fusion.23), channel_id=1, source_target_pairs={{0,2},{1,3},{2,0},{3,1},{4,6},{5,7},{6,4},{7,5},{8,10},{9,11},{10,... | collective-permute-start | bytes 786440 | tf_op jit(solution)/shard_map/ppermute | solution.py:44
  368.1 27.4 %collective-permute-start.35 = (bf16[4,2,32,1024]{3,2,1,0:T(8,128)(2,1)}, bf16[4,2,32,1024]{3,2,1,0:T(8,128)(2,1)}, u32[]{:S(2)}, u32[]{:S(2)}) collective-permute-start(bf16[4,2,32,1024]{3,2,1,0:T(8,128)(2,1)} %add_convert_fusion.1), channel_id=1, source_target_pairs={{0,1},{1,0},{2,3},{3,2},{4,5},{5,4},{6,7},{7,6},{8,9},{9,8},{10,11... | collective-permute-start | bytes 1572872 | tf_op jit(solution)/shard_map/ppermute | solution.py:44
  369.9 29.3 %collective-permute-start.33 = (bf16[8,32,2048]{2,1,0:T(8,128)(2,1)}, bf16[8,32,2048]{2,1,0:T(8,128)(2,1)}, u32[]{:S(2)}, u32[]{:S(2)}) collective-permute-start(bf16[8,32,2048]{2,1,0:T(8,128)(2,1)} %fusion.1), channel_id=1, source_target_pairs={{0,16},{8,24},{16,0},{24,8},{1,17},{9,25},{17,1},{25,9},{2,18},{10... | collective-permute-start | bytes 3145736 | tf_op jit(solution)/shard_map/ppermute | solution.py:44
  392.4 56.3 %collective-permute-start.48 = (bf16[1,2,32,1024]{3,2,1,0:T(8,128)(2,1)}, bf16[1,2,32,1024]{3,2,1,0:T(8,128)(2,1)}, u32[]{:S(2)}, u32[]{:S(2)}) collective-permute-start(bf16[1,2,32,1024]{3,2,1,0:T(8,128)(2,1)} %fusion.39), channel_id=1, source_target_pairs={{0,4},{1,5},{2,6},{3,7},{4,0},{5,1},{6,2},{7,3},{8,12},{9,13},{10,... | collective-permute-start | bytes 393224 | tf_op jit(solution)/shard_map/ppermute | solution.py:44
  401.4 17.3 %collective-permute-start.39 = (bf16[4,32,2048]{2,1,0:T(8,128)(2,1)}, bf16[4,32,2048]{2,1,0:T(8,128)(2,1)}, u32[]{:S(2)}, u32[]{:S(2)}) collective-permute-start(bf16[4,32,2048]{2,1,0:T(8,128)(2,1)} %fusion.6), channel_id=1, source_target_pairs={{0,1},{1,0},{2,3},{3,2},{4,5},{5,4},{6,7},{7,6},{8,9},{9,8},{10,11... | collective-permute-start | bytes 1572872 | tf_op jit(solution)/shard_map/ppermute | solution.py:44
  420.9 27.9 %collective-permute-start.49 = (bf16[1,128,1024]{2,1,0:T(8,128)(2,1)}, bf16[1,128,1024]{2,1,0:T(8,128)(2,1)}, u32[]{:S(2)}, u32[]{:S(2)}) collective-permute-start(bf16[1,128,1024]{2,1,0:T(8,128)(2,1)} %fusion.20), channel_id=1, source_target_pairs={{0,4},{1,5},{2,6},{3,7},{4,0},{5,1},{6,2},{7,3},{8,12},{9,13},{10,... | collective-permute-start | bytes 786440 | tf_op jit(solution)/shard_map/ppermute | solution.py:44
  424.0 17.7 %collective-permute-start.41 = (bf16[2,32,2048]{2,1,0:T(8,128)(2,1)S(1)}, bf16[2,32,2048]{2,1,0:T(8,128)(2,1)}, u32[]{:S(2)}, u32[]{:S(2)}) collective-permute-start(bf16[2,32,2048]{2,1,0:T(8,128)(2,1)S(1)} %fusion.17), channel_id=1, source_target_pairs={{0,2},{1,3},{2,0},{3,1},{4,6},{5,7},{6,4},{7,5},{8,10},{9,11},{10,... | collective-permute-start | bytes 786440 | tf_op jit(solution)/shard_map/ppermute | solution.py:44
  428.6 20.1 %collective-permute-start.47 = (bf16[1,2,32,1024]{3,2,1,0:T(8,128)(2,1)S(1)}, bf16[1,2,32,1024]{3,2,1,0:T(8,128)(2,1)S(1)}, u32[]{:S(2)}, u32[]{:S(2)}) collective-permute-start(bf16[1,2,32,1024]{3,2,1,0:T(8,128)(2,1)S(1)} %add_convert_fusion.3), channel_id=1, source_target_pairs={{0,4},{1,5},{2,6},{3,7},{4,0},{5,1},{6,2},{7,3},{8,12},{9,13},{10,... | collective-permute-start | bytes 393224 | tf_op jit(solution)/shard_map/ppermute | solution.py:44
  (79 other events, 866.0 us)

commit v4 on v3

--- a/solution.py
+++ b/solution.py
@@ -1367,6 +1367,9 @@
     blank = jnp.zeros((seq_size, extra_rows * chan - 2 * small_grads.shape[1]), bf16)
     extra = jnp.concatenate([high.astype(bf16), rest, blank], axis=1)
     extra = extra.reshape(seq_size, extra_rows, chan)
+    out_a, out_b, resid = after((out_a, out_b, resid), in_b_other)
+    output = resid + (out_a + out_b + vec_two[2:3]).reshape(resid.shape)
+    output = output.astype(bf16)
     (out_a_sum,) = low_sum(grad_out_a[: half // 2], out_a_came)
     out_a_sum = [v.reshape(seq_size, -1, width) for v in out_a_sum]
     grads_in, extra, out_a_sum, in_a_own, near, far, input_mult = together(
@@ -1375,7 +1378,7 @@
 
     moved_back, cross, state_sums = back_call(
         meta,
-        after(grads_in, in_b_other, in_b_near),
+        after(grads_in, in_b_other, in_b_near, output),
         normed,
         drive_spec,
         mixed,
@@ -1440,11 +1443,8 @@
     sum_glu.middle()
     glu_last = sum_glu.upper()
     glu_last_came = last_swap(glu_last)
-    out_a, out_b, resid = after((out_a, out_b, resid), glu_last)
-    output = resid + (out_a + out_b + vec_two[2:3]).reshape(resid.shape)
-    output = output.astype(bf16)
     in_a_last_came, out_last_came, in_b_last_came = after(
-        (in_a_last_came, out_last_came, in_b_last_came), output
+        (in_a_last_came, out_last_came, in_b_last_came), glu_last
     )
     raw_modes, state_sums = after((raw_modes, state_sums), input_grad)
 

time: 461 us -> 463 us (level)
  transfers between devices with their start and end apart: 54 -> 54, of which waited for: 17 -> 18; matrix products, arithmetic and copies ran while one was open for 19% -> 20% of each run, Pallas kernels for 37% -> 37%
where the time goes in v4:
time: 463 us; the launch traced here: 459 us
  Pallas kernels  186 us (40%)
  waiting for transfers between devices  93.5 us (20%)
  other arithmetic  72.4 us (16%)
  starting transfers between devices  70.4 us (15%)
  local copies, waits for them, and re-layouts  34.5 us (7%)
    pallas_call x11, Pallas kernels, call(): pl.pallas_call(kernel, grid_spec=pltpu.PrefetchScalarGridSpec(num_scalar_...  186 us
    ppermute x50, waiting for transfers between devices, swap(): return lax.ppermute(value, axis, [(i, i ^ bit) for i in range(size)])  81.6 us
    ppermute x50, starting transfers between devices, swap(): return lax.ppermute(value, axis, [(i, i ^ bit) for i in range(size)])  49.8 us
    all_to_all x4, starting transfers between devices, exchange(): return lax.all_to_all(parts, 'seq', 0, 0)  20.6 us
    convert_element_type x12, other arithmetic, upper(): return self.total(self.terms[0].shape[0] // 2).astype(bf16)  20.5 us
    convert_element_type x4, other arithmetic, rounded(): return Sum(*terms).total().astype(bf16)  13.5 us
    all_to_all x4, waiting for transfers between devices, exchange(): return lax.all_to_all(parts, 'seq', 0, 0)  11.9 us
    concatenate x7, other arithmetic, join(): return jnp.concatenate(parts, axis=0)  9.42 us
  transfers between devices with their start and end apart: 54, of which 18 were waited for; matrix products, arithmetic and copies ran while one was open for 20% of the time, Pallas kernels for 37%

profile of v4, /device:TPU:0, one launch (start us, length us, event | category | flops | bytes accessed | tf_op | source)
XLA Modules:
  0.0 458.9 jit_solution(274717195055414454)
XLA Ops:
  3.6 3.0 collective-permute-start
  14.3 5.6 %norm_one.1 = (bf16[8,784,128]{2,1,0:T(8,128)(2,1)}, bf16[1024,1024]{1,0:T(8,128)(2,1)}) custom-call(s32[1]{0:T(128)} %bitcast.1.meta, bf16[3,256,1024]{2,1,0:T(8,128)(2,1)} %bitcast.207, bf16[16,128]{1,0:T(8,128)(2,1)} %pad.5.extra_ref), custom_call_target="tpu_custom_call" | custom-call | flops 32212254 | bytes 80530 | tf_op jit(solution)/shard_map/norm_one/pallas_call | solution.py:202
  19.9 3.5 collective-permute-done.3
  26.2 3.3 collective-permute-start.8
  29.5 4.1 all-to-all-start
  53.8 16.8 %state_kernel.1.spec_ref = f32[8,2,256,128]{3,2,1,0:T(8,128)} custom-call(s32[88]{0:T(128)} %concatenate.77.meta, f32[64,32,128]{2,1,0:T(8,128)} %get-tuple-element.164.lift_re, f32[64,32,128]{2,1,0:T(8,128)} %get-tuple-element.166.lift_im, f32[64,64,128]{2,1,0:T(8,128)} %get-tuple-element.256.near_re, f32[64,64,128]{2,1,0:T(8,128)} %get-tuple-element.257.near_im, ...), custom_call_target="tpu_custom_call" | custom-call | flops 220000000 | bytes 550000 | tf_op jit(solution)/shard_map/state_kernel/pallas_call | solution.py:202
  70.5 3.5 all-to-all-done.normed_ref
  86.3 3.3 collective-permute-start.12
  92.5 12.9 %state_conv.1 = (f32[3,8,512,128]{3,2,1,0:T(8,128)}, f32[3,8,256,128]{3,2,1,0:T(8,128)}, bf16[8,768,128]{2,1,0:T(8,128)(2,1)}) custom-call(s32[88]{0:T(128)} %concatenate.77.meta, bf16[8,784,128]{2,1,0:T(8,128)(2,1)} %copy-done.1, f32[8,128]{1,0:T(8,128)} %concatenate.82.vec_ref, f32[8,2,256,128]{3,2,1,0:T(8,128)} %state_kernel.1.spec_ref, ...), custom_call_target="tpu_custom_call" | custom-call | flops 300000000 | bytes 750000 | tf_op jit(solution)/shard_map/state_conv/pallas_call | solution.py:202
  107.3 7.6 %all-to-all-start.1 = ((bf16[8,768,128]{2,1,0:T(8,128)(2,1)}), bf16[8,768,128]{2,1,0:T(8,128)(2,1)}, u32[]{:S(2)}, u32[]{:S(2)}) async-start(bf16[8,768,128]{2,1,0:T(8,128)(2,1)} %get-tuple-element.176), calls=%async_computation.1 | async-start | bytes 3145728 | tf_op jit(solution)/shard_map/all_to_all | solution.py:106
  116.5 13.4 %collective-permute-done.16.refs_6_ = bf16[256,4096]{1,0:T(8,128)(2,1)} collective-permute-done((bf16[256,4096]{1,0:T(8,128)(2,1)S(1)}, bf16[256,4096]{1,0:T(8,128)(2,1)}, u32[]{:S(2)}, u32[]{:S(2)}) %collective-permute-start.16) | collective-permute-done | bytes 2097184 | tf_op jit(solution)/shard_map/ppermute | solution.py:44
  131.4 22.1 %collective-permute-done.17.refs_6_.refs_7_ = bf16[256,2048]{1,0:T(8,128)(2,1)} collective-permute-done((bf16[256,2048]{1,0:T(8,128)(2,1)S(1)}, bf16[256,2048]{1,0:T(8,128)(2,1)}, u32[]{:S(2)}, u32[]{:S(2)}) %collective-permute-start.17) | collective-permute-done | bytes 1048608 | tf_op jit(solution)/shard_map/ppermute | solution.py:44
  156.4 4.5 collective-permute-done.15
  164.1 11.9 %gated_unit.1 = (bf16[768,1024]{1,0:T(8,128)(2,1)}, f32[3,256,1024]{2,1,0:T(8,128)}, f32[3,256,2048]{2,1,0:T(8,128)}, bf16[768,1024]{1,0:T(8,128)(2,1)}, bf16[10...) custom-call(s32[88]{0:T(128)} %concatenate.77.meta, bf16[8,768,128]{2,1,0:T(8,128)(2,1)} %all-to-all-done.1.refs_0_, ...), custom_call_target="tpu_custom_call" | custom-call | flops 96636768 | bytes 241591 | tf_op jit(solution)/shard_map/gated_unit/pallas_call | solution.py:202
  176.0 34.1 %feed_forward.2 = (f32[768,1024]{1,0:T(8,128)}, f32[2,1,1024]{2,1,0:T(1,128)}, f32[768,1024]{1,0:T(8,128)}, bf16[1024,1024]{1,0:T(8,128)(2,1)}, bf16[1024,1024]{...) custom-call(s32[88]{0:T(128)} %concatenate.77.meta, ...), custom_call_target="tpu_custom_call" | custom-call | flops 386547072 | bytes 966367 | tf_op jit(solution)/shard_map/feed_forward/pallas_call | solution.py:202
  214.5 3.4 fusion.4
  221.9 34.6 %feed_forward.3 = (f32[768,1024]{1,0:T(8,128)}, f32[2,1,1024]{2,1,0:T(1,128)}, f32[768,1024]{1,0:T(8,128)}, bf16[1024,1024]{1,0:T(8,128)(2,1)}, bf16[1024,1024]{...) custom-call(s32[88]{0:T(128)} %concatenate.77.meta, ...), custom_call_target="tpu_custom_call" | custom-call | flops 386547072 | bytes 966367 | tf_op jit(solution)/shard_map/feed_forward/pallas_call | solution.py:202
  257.4 15.0 %gated_back.1 = (f32[3,256,1024]{2,1,0:T(8,128)}, bf16[768,2048]{1,0:T(8,128)(2,1)}, f32[8,2048]{1,0:T(8,128)}, f32[8,1024]{1,0:T(8,128)}, bf16[8,768,128]{2,1,0:T(8,128)(2,1)}) custom-call(s32[88]{0:T(128)} %concatenate.77.meta, f32[768,1024]{1,0:T(8,128)} %get-tuple-element.197.refs_0_, f32[768,1024]{1,0:T(8,128)} %get-tuple-element.206.refs_1_, ...), custom_call_target="tpu_custom_call" | custom-call | flops 64424508 | bytes 161061 | tf_op jit(solution)/shard_map/gated_back/pallas_call | solution.py:202
  275.7 5.0 %all-to-all-start.2 = ((bf16[8,768,128]{2,1,0:T(8,128)(2,1)}), bf16[8,768,128]{2,1,0:T(8,128)(2,1)S(1)}, u32[]{:S(2)}, u32[]{:S(2)}) async-start(bf16[8,768,128]{2,1,0:T(8,128)(2,1)} %get-tuple-element.210), calls=%async_computation.2 | async-start | bytes 3145728 | tf_op jit(solution)/shard_map/all_to_all | solution.py:106
  283.1 4.5 fusion
  289.6 8.2 %gated_weight.1 = (bf16[8,32,2048]{2,1,0:T(8,128)(2,1)}, bf16[8,32,2048]{2,1,0:T(8,128)(2,1)}, bf16[2,8,32,2048]{3,2,1,0:T(8,128)(2,1)}) custom-call(s32[88]{0:T(128)} %concatenate.77.meta, bf16[768,1024]{1,0:T(8,128)(2,1)} %get-tuple-element.203.act_ref, bf16[768,2048]{1,0:T(8,128)(2,1)} %get-tuple-element.214.grad_ref), custom_call_target="tpu_custom_call" | custom-call | flops 64424508 | bytes 161061 | tf_op jit(solution)/shard_map/gated_weight/pallas_call | solution.py:202
  297.8 3.1 fusion.3
  305.0 3.1 add_add_fusion
  309.8 8.4 %all-to-all-done.2.grads_ref = bf16[8,768,128]{2,1,0:T(8,128)(2,1)S(1)} async-done(((bf16[8,768,128]{2,1,0:T(8,128)(2,1)}), bf16[8,768,128]{2,1,0:T(8,128)(2,1)S(1)}, u32[]{:S(2)}, u32[]{:S(2)}) %all-to-all-start.2) | async-done | bytes 1572896 | tf_op jit(solution)/shard_map/all_to_all | solution.py:106
  319.4 21.0 %state_back.1 = (bf16[8,800,128]{2,1,0:T(8,128)(2,1)}, f32[8,512,128]{2,1,0:T(8,128)}, f32[8,128]{1,0:T(8,128)}) custom-call(s32[88]{0:T(128)} %concatenate.77.meta, bf16[8,768,128]{2,1,0:T(8,128)(2,1)} %copy-done.5, bf16[8,784,128]{2,1,0:T(8,128)(2,1)} %copy-done.1, f32[3,8,512,128]{3,2,1,0:T(8,128)} %get-tuple-element.235.drive_ref, ...), custom_call_target="tpu_custom_call" | custom-call | flops 400000000 | bytes 1000000 | tf_op jit(solution)/shard_map/state_back/pallas_call | solution.py:202
  341.2 3.9 all-to-all-start.3
  349.0 3.0 fusion.2
  359.4 10.8 %collective-permute-done.33 = bf16[8,2,32,1024]{3,2,1,0:T(8,128)(2,1)S(1)} collective-permute-done((bf16[8,2,32,1024]{3,2,1,0:T(8,128)(2,1)}, bf16[8,2,32,1024]{3,2,1,0:T(8,128)(2,1)S(1)}, u32[]{:S(2)}, u32[]{:S(2)}) %collective-permute-start.33) | collective-permute-done | bytes 1048608 | tf_op jit(solution)/shard_map/ppermute | solution.py:44
  374.5 18.4 %state_modes.1 = f32[2,64,128]{2,1,0:T(8,128)} custom-call(s32[88]{0:T(128)} %concatenate.77.meta, f32[8,512,128]{2,1,0:T(8,128)} %get-tuple-element.253.cross_ref, f32[64,32,128]{2,1,0:T(8,128)} %get-tuple-element.254.far_re, f32[64,32,128]{2,1,0:T(8,128)} %get-tuple-element.255.far_im, f32[64,64,128]{2,1,0:T(8,128)} %get-tuple-element.256.near_re, ...), custom_call_target="tpu_custom_call" | custom-call | flops 220000000 | bytes 550000 | tf_op jit(solution)/shard_map/state_modes/pallas_call | solution.py:202
  410.4 7.7 %input_grad.1 = bf16[3,256,1024]{2,1,0:T(8,128)(2,1)} custom-call(s32[88]{0:T(128)} %concatenate.77.meta, bf16[8,800,128]{2,1,0:T(8,128)(2,1)} %copy-done.4, bf16[3,256,1024]{2,1,0:T(8,128)(2,1)} %bitcast.209, f32[3,256,1024]{2,1,0:T(8,128)} %get-tuple-element.267.grad_resid_ref, bf16[1024,1024]{1,0:T(8,128)(2,1)} %get-tuple-element.268.perm_ref), custom_call_target="tpu_custom_call" | custom-call | flops 32212254 | bytes 80530 | tf_op jit(solution)/shard_map/input_grad/pallas_call | solution.py:202
  418.1 4.1 collective-permute-done.40
  439.1 8.4 %collective-permute-done.43 = bf16[2,32,2048]{2,1,0:T(8,128)(2,1)} collective-permute-done((bf16[2,32,2048]{2,1,0:T(8,128)(2,1)S(1)}, bf16[2,32,2048]{2,1,0:T(8,128)(2,1)}, u32[]{:S(2)}, u32[]{:S(2)}) %collective-permute-start.43) | collective-permute-done | bytes 262176 | tf_op jit(solution)/shard_map/ppermute | solution.py:44
  (346 shorter events, 145.0 us)
Async XLA Ops:
  25.2 22.3 %collective-permute-start.7 = (bf16[2,32,4096]{2,1,0:T(8,128)(2,1)}, bf16[2,32,4096]{2,1,0:T(8,128)(2,1)S(1)}, u32[]{:S(2)}, u32[]{:S(2)}) collective-permute-start(bf16[2,32,4096]{2,1,0:T(8,128)(2,1)} %pad_maximum_fusion.4), channel_id=1, source_target_pairs={{0,2},{1,3},{2,0},{3,1},{4,6},{5,7},{6,4},{7,5},{8,10},{9,11},{10,... | collective-permute-start | bytes 1572872 | tf_op jit(solution)/shard_map/ppermute | solution.py:44
  26.2 21.4 %collective-permute-start.8 = (bf16[1,32,2048]{2,1,0:T(8,128)(2,1)}, bf16[1,32,2048]{2,1,0:T(8,128)(2,1)}, u32[]{:S(2)}, u32[]{:S(2)}) collective-permute-start(bf16[1,32,2048]{2,1,0:T(8,128)(2,1)} %bitcast.16), channel_id=1, source_target_pairs={{0,4},{1,5},{2,6},{3,7},{4,0},{5,1},{6,2},{7,3},{8,12},{9,13},{10,... | collective-permute-start | bytes 393224 | tf_op jit(solution)/shard_map/ppermute | solution.py:44
  29.5 44.5 %all-to-all-start = ((bf16[8,784,128]{2,1,0:T(8,128)(2,1)}), bf16[8,784,128]{2,1,0:T(8,128)(2,1)S(1)}, u32[]{:S(2)}, u32[]{:S(2)}) async-start(bf16[8,784,128]{2,1,0:T(8,128)(2,1)} %get-tuple-element.154), calls=%async_computation | async-start | bytes 3211264 | tf_op jit(solution)/shard_map/all_to_all | solution.py:106
  48.6 32.8 %collective-permute-start.9 = (bf16[4,32,4096]{2,1,0:T(8,128)(2,1)}, bf16[4,32,4096]{2,1,0:T(8,128)(2,1)}, u32[]{:S(2)}, u32[]{:S(2)}) collective-permute-start(bf16[4,32,4096]{2,1,0:T(8,128)(2,1)} %pad_maximum_fusion.1), channel_id=1, source_target_pairs={{0,1},{1,0},{2,3},{3,2},{4,5},{5,4},{6,7},{7,6},{8,9},{9,8},{10,11... | collective-permute-start | bytes 3145736 | tf_op jit(solution)/shard_map/ppermute | solution.py:44
  52.3 26.9 %collective-permute-start.10 = (bf16[2,32,2048]{2,1,0:T(8,128)(2,1)}, bf16[2,32,2048]{2,1,0:T(8,128)(2,1)}, u32[]{:S(2)}, u32[]{:S(2)}) collective-permute-start(bf16[2,32,2048]{2,1,0:T(8,128)(2,1)} %pad_maximum_fusion.7), channel_id=1, source_target_pairs={{0,2},{1,3},{2,0},{3,1},{4,6},{5,7},{6,4},{7,5},{8,10},{9,11},{10,... | collective-permute-start | bytes 786440 | tf_op jit(solution)/shard_map/ppermute | solution.py:44
  82.9 47.0 %collective-permute-start.16 = (bf16[256,4096]{1,0:T(8,128)(2,1)S(1)}, bf16[256,4096]{1,0:T(8,128)(2,1)}, u32[]{:S(2)}, u32[]{:S(2)}) collective-permute-start(bf16[256,4096]{1,0:T(8,128)(2,1)S(1)} %bitcast.203), channel_id=1, source_target_pairs={{0,16},{8,24},{16,0},{24,8},{1,17},{9,25},{17,1},{25,9},{2,18},{10... | collective-permute-start | bytes 6291464 | tf_op jit(solution)/shard_map/ppermute | solution.py:44
  86.3 20.9 %collective-permute-start.11 = (bf16[4,32,2048]{2,1,0:T(8,128)(2,1)}, bf16[4,32,2048]{2,1,0:T(8,128)(2,1)}, u32[]{:S(2)}, u32[]{:S(2)}) collective-permute-start(bf16[4,32,2048]{2,1,0:T(8,128)(2,1)} %pad_maximum_fusion.5), channel_id=1, source_target_pairs={{0,1},{1,0},{2,3},{3,2},{4,5},{5,4},{6,7},{7,6},{8,9},{9,8},{10,11... | collective-permute-start | bytes 1572872 | tf_op jit(solution)/shard_map/ppermute | solution.py:44
  86.3 20.9 %collective-permute-start.12 = (bf16[1,128,1024]{2,1,0:T(8,128)(2,1)S(1)}, bf16[1,128,1024]{2,1,0:T(8,128)(2,1)S(1)}, u32[]{:S(2)}, u32[]{:S(2)}) collective-permute-start(bf16[1,128,1024]{2,1,0:T(8,128)(2,1)S(1)} %bitcast.232), channel_id=1, source_target_pairs={{0,4},{1,5},{2,6},{3,7},{4,0},{5,1},{6,2},{7,3},{8,12},{9,13},{10,... | collective-permute-start | bytes 786440 | tf_op jit(solution)/shard_map/ppermute | solution.py:44
  89.6 17.6 %collective-permute-start.13 = (bf16[1,128,1024]{2,1,0:T(8,128)(2,1)S(1)}, bf16[1,128,1024]{2,1,0:T(8,128)(2,1)S(1)}, u32[]{:S(2)}, u32[]{:S(2)}) collective-permute-start(bf16[1,128,1024]{2,1,0:T(8,128)(2,1)S(1)} %bitcast.233), channel_id=1, source_target_pairs={{0,2},{1,3},{2,0},{3,1},{4,6},{5,7},{6,4},{7,5},{8,10},{9,11},{10,... | collective-permute-start | bytes 786440 | tf_op jit(solution)/shard_map/ppermute | solution.py:44
  107.3 53.6 %all-to-all-start.1 = ((bf16[8,768,128]{2,1,0:T(8,128)(2,1)}), bf16[8,768,128]{2,1,0:T(8,128)(2,1)}, u32[]{:S(2)}, u32[]{:S(2)}) async-start(bf16[8,768,128]{2,1,0:T(8,128)(2,1)} %get-tuple-element.176), calls=%async_computation.1 | async-start | bytes 3145728 | tf_op jit(solution)/shard_map/all_to_all | solution.py:106
  129.9 23.6 %collective-permute-start.17 = (bf16[256,2048]{1,0:T(8,128)(2,1)S(1)}, bf16[256,2048]{1,0:T(8,128)(2,1)}, u32[]{:S(2)}, u32[]{:S(2)}) collective-permute-start(bf16[256,2048]{1,0:T(8,128)(2,1)S(1)} %bitcast.211), channel_id=1, source_target_pairs={{0,16},{8,24},{16,0},{24,8},{1,17},{9,25},{17,1},{25,9},{2,18},{10... | collective-permute-start | bytes 3145736 | tf_op jit(solution)/shard_map/ppermute | solution.py:44
  131.4 22.8 %collective-permute-start.18 = (bf16[256,2048]{1,0:T(8,128)(2,1)S(1)}, bf16[256,2048]{1,0:T(8,128)(2,1)S(1)}, u32[]{:S(2)}, u32[]{:S(2)}) collective-permute-start(bf16[256,2048]{1,0:T(8,128)(2,1)S(1)} %bitcast.212), channel_id=1, source_target_pairs={{0,8},{8,0},{16,24},{24,16},{1,9},{9,1},{17,25},{25,17},{2,10},{10... | collective-permute-start | bytes 3145736 | tf_op jit(solution)/shard_map/ppermute | solution.py:44
  131.4 29.5 %collective-permute-start.15 = (bf16[4,128,1024]{2,1,0:T(8,128)(2,1)S(1)}, bf16[4,128,1024]{2,1,0:T(8,128)(2,1)}, u32[]{:S(2)}, u32[]{:S(2)}) collective-permute-start(bf16[4,128,1024]{2,1,0:T(8,128)(2,1)S(1)} %pad_maximum_fusion.2), channel_id=1, source_target_pairs={{0,1},{1,0},{2,3},{3,2},{4,5},{5,4},{6,7},{7,6},{8,9},{9,8},{10,11... | collective-permute-start | bytes 3145736 | tf_op jit(solution)/shard_map/ppermute | solution.py:44
  153.4 22.5 %collective-permute-start.22 = (bf16[256,4096]{1,0:T(8,128)(2,1)S(1)}, bf16[256,4096]{1,0:T(8,128)(2,1)}, u32[]{:S(2)}, u32[]{:S(2)}) collective-permute-start(bf16[256,4096]{1,0:T(8,128)(2,1)S(1)} %bitcast.204), channel_id=1, source_target_pairs={{0,8},{8,0},{16,24},{24,16},{1,9},{9,1},{17,25},{25,17},{2,10},{10... | collective-permute-start | bytes 6291464 | tf_op jit(solution)/shard_map/ppermute | solution.py:44
  154.1 21.9 %collective-permute-start.23 = (bf16[256,4096]{1,0:T(8,128)(2,1)}, bf16[256,4096]{1,0:T(8,128)(2,1)}, u32[]{:S(2)}, u32[]{:S(2)}) collective-permute-start(bf16[256,4096]{1,0:T(8,128)(2,1)} %collective-permute-done.16.refs_6_), channel_id=1, source_target_pairs={{0,8},{8,0},{16,24},{24,16},{1,9},{9,1},{17,25},{25,17},{2,10},{10... | collective-permute-start | bytes 6291464 | tf_op jit(solution)/shard_map/ppermute | solution.py:44
  163.2 48.3 %collective-permute-start.20 = (bf16[1024,1024]{1,0:T(8,128)(2,1)}, bf16[1024,1024]{1,0:T(8,128)(2,1)}, u32[]{:S(2)}, u32[]{:S(2)}) collective-permute-start(bf16[1024,1024]{1,0:T(8,128)(2,1)} %bitcast.217), channel_id=1, source_target_pairs={{0,16},{8,24},{16,0},{24,8},{1,17},{9,25},{17,1},{25,9},{2,18},{10... | collective-permute-start | bytes 6291464 | tf_op jit(solution)/shard_map/ppermute | solution.py:44
  211.5 45.0 %collective-permute-start.27 = (bf16[1,1024,1024]{2,1,0:T(8,128)(2,1)}, bf16[1,1024,1024]{2,1,0:T(8,128)(2,1)}, u32[]{:S(2)}, u32[]{:S(2)}) collective-permute-start(bf16[1,1024,1024]{2,1,0:T(8,128)(2,1)} %bitcast.253), channel_id=1, source_target_pairs={{0,8},{8,0},{16,24},{24,16},{1,9},{9,1},{17,25},{25,17},{2,10},{10... | collective-permute-start | bytes 6291464 | tf_op jit(solution)/shard_map/ppermute | solution.py:44
  217.9 38.5 %collective-permute-start.26 = (bf16[8,2,32,1024]{3,2,1,0:T(8,128)(2,1)}, bf16[8,2,32,1024]{3,2,1,0:T(8,128)(2,1)S(1)}, u32[]{:S(2)}, u32[]{:S(2)}) collective-permute-start(bf16[8,2,32,1024]{3,2,1,0:T(8,128)(2,1)} %fusion.4), channel_id=1, source_target_pairs={{0,16},{8,24},{16,0},{24,8},{1,17},{9,25},{17,1},{25,9},{2,18},{10... | collective-permute-start | bytes 3145736 | tf_op jit(solution)/shard_map/ppermute | solution.py:44
  272.8 25.0 %collective-permute-start.29 = (bf16[2,8,2,32,1024]{4,3,2,1,0:T(8,128)(2,1)}, bf16[2,8,2,32,1024]{4,3,2,1,0:T(8,128)(2,1)}, u32[]{:S(2)}, u32[]{:S(2)}) collective-permute-start(bf16[2,8,2,32,1024]{4,3,2,1,0:T(8,128)(2,1)} %get-tuple-element.218), channel_id=1, source_target_pairs={{0,8},{8,0},{16,24},{24,16},{1,9},{9,1},{17,25},{25,17},{2,10},{10... | collective-permute-start | bytes 6291464 | tf_op jit(solution)/shard_map/ppermute | solution.py:44
  275.7 42.5 %all-to-all-start.2 = ((bf16[8,768,128]{2,1,0:T(8,128)(2,1)}), bf16[8,768,128]{2,1,0:T(8,128)(2,1)S(1)}, u32[]{:S(2)}, u32[]{:S(2)}) async-start(bf16[8,768,128]{2,1,0:T(8,128)(2,1)} %get-tuple-element.210), calls=%async_computation.2 | async-start | bytes 3145728 | tf_op jit(solution)/shard_map/all_to_all | solution.py:106
  287.6 52.8 %collective-permute-start.31 = (bf16[1024,1024]{1,0:T(8,128)(2,1)}, bf16[1024,1024]{1,0:T(8,128)(2,1)}, u32[]{:S(2)}, u32[]{:S(2)}) collective-permute-start(bf16[1024,1024]{1,0:T(8,128)(2,1)} %fusion), channel_id=1, source_target_pairs={{0,16},{8,24},{16,0},{24,8},{1,17},{9,25},{17,1},{25,9},{2,18},{10... | collective-permute-start | bytes 6291464 | tf_op jit(solution)/shard_map/ppermute | solution.py:44
  303.0 37.4 %collective-permute-start.30 = (bf16[4,2,32,1024]{3,2,1,0:T(8,128)(2,1)}, bf16[4,2,32,1024]{3,2,1,0:T(8,128)(2,1)S(1)}, u32[]{:S(2)}, u32[]{:S(2)}) collective-permute-start(bf16[4,2,32,1024]{3,2,1,0:T(8,128)(2,1)} %fusion.10), channel_id=1, source_target_pairs={{0,1},{1,0},{2,3},{3,2},{4,5},{5,4},{6,7},{7,6},{8,9},{9,8},{10,11... | collective-permute-start | bytes 1572872 | tf_op jit(solution)/shard_map/ppermute | solution.py:44
  341.2 51.7 %all-to-all-start.3 = ((bf16[8,800,128]{2,1,0:T(8,128)(2,1)}), bf16[8,800,128]{2,1,0:T(8,128)(2,1)S(1)}, u32[]{:S(2)}, u32[]{:S(2)}) async-start(bf16[8,800,128]{2,1,0:T(8,128)(2,1)} %get-tuple-element.240), calls=%async_computation.3 | async-start | bytes 3276800 | tf_op jit(solution)/shard_map/all_to_all | solution.py:106
  345.1 25.1 %collective-permute-start.33 = (bf16[8,2,32,1024]{3,2,1,0:T(8,128)(2,1)}, bf16[8,2,32,1024]{3,2,1,0:T(8,128)(2,1)S(1)}, u32[]{:S(2)}, u32[]{:S(2)}) collective-permute-start(bf16[8,2,32,1024]{3,2,1,0:T(8,128)(2,1)} %fusion.3), channel_id=1, source_target_pairs={{0,16},{8,24},{16,0},{24,8},{1,17},{9,25},{17,1},{25,9},{2,18},{10... | collective-permute-start | bytes 3145736 | tf_op jit(solution)/shard_map/ppermute | solution.py:44
  351.9 43.7 %collective-permute-start.32 = (bf16[4,128,1024]{2,1,0:T(8,128)(2,1)}, bf16[4,128,1024]{2,1,0:T(8,128)(2,1)}, u32[]{:S(2)}, u32[]{:S(2)}) collective-permute-start(bf16[4,128,1024]{2,1,0:T(8,128)(2,1)} %fusion.2), channel_id=1, source_target_pairs={{0,1},{1,0},{2,3},{3,2},{4,5},{5,4},{6,7},{7,6},{8,9},{9,8},{10,11... | collective-permute-start | bytes 3145736 | tf_op jit(solution)/shard_map/ppermute | solution.py:44
  355.2 37.6 %collective-permute-start.37 = (bf16[2,2,32,1024]{3,2,1,0:T(8,128)(2,1)S(1)}, bf16[2,2,32,1024]{3,2,1,0:T(8,128)(2,1)S(1)}, u32[]{:S(2)}, u32[]{:S(2)}) collective-permute-start(bf16[2,2,32,1024]{3,2,1,0:T(8,128)(2,1)S(1)} %fusion.23), channel_id=1, source_target_pairs={{0,2},{1,3},{2,0},{3,1},{4,6},{5,7},{6,4},{7,5},{8,10},{9,11},{10,... | collective-permute-start | bytes 786440 | tf_op jit(solution)/shard_map/ppermute | solution.py:44
  371.3 28.0 %collective-permute-start.36 = (bf16[4,2,32,1024]{3,2,1,0:T(8,128)(2,1)}, bf16[4,2,32,1024]{3,2,1,0:T(8,128)(2,1)}, u32[]{:S(2)}, u32[]{:S(2)}) collective-permute-start(bf16[4,2,32,1024]{3,2,1,0:T(8,128)(2,1)} %add_convert_fusion.1), channel_id=1, source_target_pairs={{0,1},{1,0},{2,3},{3,2},{4,5},{5,4},{6,7},{7,6},{8,9},{9,8},{10,11... | collective-permute-start | bytes 1572872 | tf_op jit(solution)/shard_map/ppermute | solution.py:44
  373.1 30.1 %collective-permute-start.35 = (bf16[8,32,2048]{2,1,0:T(8,128)(2,1)}, bf16[8,32,2048]{2,1,0:T(8,128)(2,1)}, u32[]{:S(2)}, u32[]{:S(2)}) collective-permute-start(bf16[8,32,2048]{2,1,0:T(8,128)(2,1)} %fusion.1), channel_id=1, source_target_pairs={{0,16},{8,24},{16,0},{24,8},{1,17},{9,25},{17,1},{25,9},{2,18},{10... | collective-permute-start | bytes 3145736 | tf_op jit(solution)/shard_map/ppermute | solution.py:44
  395.6 53.2 %collective-permute-start.48 = (bf16[1,2,32,1024]{3,2,1,0:T(8,128)(2,1)}, bf16[1,2,32,1024]{3,2,1,0:T(8,128)(2,1)}, u32[]{:S(2)}, u32[]{:S(2)}) collective-permute-start(bf16[1,2,32,1024]{3,2,1,0:T(8,128)(2,1)} %fusion.43), channel_id=1, source_target_pairs={{0,4},{1,5},{2,6},{3,7},{4,0},{5,1},{6,2},{7,3},{8,12},{9,13},{10,... | collective-permute-start | bytes 393224 | tf_op jit(solution)/shard_map/ppermute | solution.py:44
  405.5 16.8 %collective-permute-start.39 = (bf16[4,32,2048]{2,1,0:T(8,128)(2,1)}, bf16[4,32,2048]{2,1,0:T(8,128)(2,1)}, u32[]{:S(2)}, u32[]{:S(2)}) collective-permute-start(bf16[4,32,2048]{2,1,0:T(8,128)(2,1)} %fusion.6), channel_id=1, source_target_pairs={{0,1},{1,0},{2,3},{3,2},{4,5},{5,4},{6,7},{7,6},{8,9},{9,8},{10,11... | collective-permute-start | bytes 1572872 | tf_op jit(solution)/shard_map/ppermute | solution.py:44
  424.5 24.2 %collective-permute-start.49 = (bf16[1,128,1024]{2,1,0:T(8,128)(2,1)}, bf16[1,128,1024]{2,1,0:T(8,128)(2,1)}, u32[]{:S(2)}, u32[]{:S(2)}) collective-permute-start(bf16[1,128,1024]{2,1,0:T(8,128)(2,1)} %fusion.20), channel_id=1, source_target_pairs={{0,4},{1,5},{2,6},{3,7},{4,0},{5,1},{6,2},{7,3},{8,12},{9,13},{10,... | collective-permute-start | bytes 786440 | tf_op jit(solution)/shard_map/ppermute | solution.py:44
  429.5 18.0 %collective-permute-start.43 = (bf16[2,32,2048]{2,1,0:T(8,128)(2,1)S(1)}, bf16[2,32,2048]{2,1,0:T(8,128)(2,1)}, u32[]{:S(2)}, u32[]{:S(2)}) collective-permute-start(bf16[2,32,2048]{2,1,0:T(8,128)(2,1)S(1)} %fusion.17), channel_id=1, source_target_pairs={{0,2},{1,3},{2,0},{3,1},{4,6},{5,7},{6,4},{7,5},{8,10},{9,11},{10,... | collective-permute-start | bytes 786440 | tf_op jit(solution)/shard_map/ppermute | solution.py:44
  (83 other events, 919.1 us)

commit v5 on v3

--- a/solution.py
+++ b/solution.py
@@ -1250,9 +1250,9 @@
     )
     active_own, glu_3, out_1 = together((active_own, glu_3, out_1))
 
-    active = exchange(active_own)
     out_w = gather_more(join(ffn_out_weight[None], *out_1), 1)
     out_3 = near_swap(out_w)
+    active = exchange(after(active_own, out_w))
     glu_w = join(glu_w, after(glu_3, out_w)).reshape(-1, 2 * width)
     glu_top = top_swap(after(glu_w, in_top))
     in_parts = weave(over_low([in_w]), over_low([in_top]))

time: 461 us -> 461 us (level)
  transfers between devices with their start and end apart: 54 -> 54, of which waited for: 17 -> 17; matrix products, arithmetic and copies ran while one was open for 19% -> 20% of each run, Pallas kernels for 37% -> 37%
where the time goes in v5:
time: 461 us; the launch traced here: 457 us
  Pallas kernels  186 us (40%)
  waiting for transfers between devices  95.5 us (21%)
  other arithmetic  72.2 us (16%)
  starting transfers between devices  69.7 us (15%)
  local copies, waits for them, and re-layouts  32.1 us (7%)
    pallas_call x11, Pallas kernels, call(): pl.pallas_call(kernel, grid_spec=pltpu.PrefetchScalarGridSpec(num_scalar_...  186 us
    ppermute x50, waiting for transfers between devices, swap(): return lax.ppermute(value, axis, [(i, i ^ bit) for i in range(size)])  81 us
    ppermute x50, starting transfers between devices, swap(): return lax.ppermute(value, axis, [(i, i ^ bit) for i in range(size)])  49.8 us
    convert_element_type x12, other arithmetic, upper(): return self.total(self.terms[0].shape[0] // 2).astype(bf16)  20.6 us
    all_to_all x4, starting transfers between devices, exchange(): return lax.all_to_all(parts, 'seq', 0, 0)  19.9 us
    all_to_all x4, waiting for transfers between devices, exchange(): return lax.all_to_all(parts, 'seq', 0, 0)  14.5 us
    convert_element_type x4, other arithmetic, rounded(): return Sum(*terms).total().astype(bf16)  12.8 us
    concatenate x7, other arithmetic, join(): return jnp.concatenate(parts, axis=0)  9.68 us
  transfers between devices with their start and end apart: 54, of which 17 were waited for; matrix products, arithmetic and copies ran while one was open for 20% of the time, Pallas kernels for 37%

profile of v5, /device:TPU:0, one launch (start us, length us, event | category | flops | bytes accessed | tf_op | source)
XLA Modules:
  0.0 457.1 jit_solution(7308457931088219581)
XLA Ops:
  3.6 3.0 collective-permute-start
  14.3 5.6 %norm_one.1 = (bf16[8,784,128]{2,1,0:T(8,128)(2,1)}, bf16[1024,1024]{1,0:T(8,128)(2,1)}) custom-call(s32[1]{0:T(128)} %bitcast.1.meta, bf16[3,256,1024]{2,1,0:T(8,128)(2,1)} %bitcast.207, bf16[16,128]{1,0:T(8,128)(2,1)} %pad.5.extra_ref), custom_call_target="tpu_custom_call" | custom-call | flops 32212254 | bytes 80530 | tf_op jit(solution)/shard_map/norm_one/pallas_call | solution.py:202
  19.9 3.5 collective-permute-done.3
  26.2 3.3 collective-permute-start.8
  29.5 4.1 all-to-all-start
  53.8 16.8 %state_kernel.1.spec_ref = f32[8,2,256,128]{3,2,1,0:T(8,128)} custom-call(s32[88]{0:T(128)} %concatenate.77.meta, f32[64,32,128]{2,1,0:T(8,128)} %get-tuple-element.165.lift_re, f32[64,32,128]{2,1,0:T(8,128)} %get-tuple-element.167.lift_im, f32[64,64,128]{2,1,0:T(8,128)} %get-tuple-element.253.near_re, f32[64,64,128]{2,1,0:T(8,128)} %get-tuple-element.254.near_im, ...), custom_call_target="tpu_custom_call" | custom-call | flops 220000000 | bytes 550000 | tf_op jit(solution)/shard_map/state_kernel/pallas_call | solution.py:202
  70.6 3.4 all-to-all-done.normed_ref
  85.6 3.4 collective-permute-start.12
  91.8 12.9 %state_conv.1 = (f32[3,8,512,128]{3,2,1,0:T(8,128)}, f32[3,8,256,128]{3,2,1,0:T(8,128)}, bf16[8,768,128]{2,1,0:T(8,128)(2,1)}) custom-call(s32[88]{0:T(128)} %concatenate.77.meta, bf16[8,784,128]{2,1,0:T(8,128)(2,1)} %copy-done.1, f32[8,128]{1,0:T(8,128)} %concatenate.82.vec_ref, f32[8,2,256,128]{3,2,1,0:T(8,128)} %state_kernel.1.spec_ref, ...), custom_call_target="tpu_custom_call" | custom-call | flops 300000000 | bytes 750000 | tf_op jit(solution)/shard_map/state_conv/pallas_call | solution.py:202
  108.4 6.9 %all-to-all-start.1 = ((bf16[8,768,128]{2,1,0:T(8,128)(2,1)}), bf16[8,768,128]{2,1,0:T(8,128)(2,1)}, u32[]{:S(2)}, u32[]{:S(2)}) async-start(bf16[8,768,128]{2,1,0:T(8,128)(2,1)} %get-tuple-element.181), calls=%async_computation.1 | async-start | bytes 3145728 | tf_op jit(solution)/shard_map/all_to_all | solution.py:106
  116.8 13.1 %collective-permute-done.16.refs_6_ = bf16[256,4096]{1,0:T(8,128)(2,1)} collective-permute-done((bf16[256,4096]{1,0:T(8,128)(2,1)S(1)}, bf16[256,4096]{1,0:T(8,128)(2,1)}, u32[]{:S(2)}, u32[]{:S(2)}) %collective-permute-start.16) | collective-permute-done | bytes 2097184 | tf_op jit(solution)/shard_map/ppermute | solution.py:44
  131.4 22.1 %collective-permute-done.17.refs_6_.refs_7_ = bf16[256,2048]{1,0:T(8,128)(2,1)} collective-permute-done((bf16[256,2048]{1,0:T(8,128)(2,1)S(1)}, bf16[256,2048]{1,0:T(8,128)(2,1)}, u32[]{:S(2)}, u32[]{:S(2)}) %collective-permute-start.17) | collective-permute-done | bytes 1048608 | tf_op jit(solution)/shard_map/ppermute | solution.py:44
  156.4 4.8 %collective-permute-done.15 = bf16[4,128,1024]{2,1,0:T(8,128)(2,1)} collective-permute-done((bf16[4,128,1024]{2,1,0:T(8,128)(2,1)S(1)}, bf16[4,128,1024]{2,1,0:T(8,128)(2,1)}, u32[]{:S(2)}, u32[]{:S(2)}) %collective-permute-start.15) | collective-permute-done | bytes 1048608 | tf_op jit(solution)/shard_map/ppermute | solution.py:44
  164.2 11.9 %gated_unit.1 = (bf16[768,1024]{1,0:T(8,128)(2,1)}, f32[3,256,1024]{2,1,0:T(8,128)}, f32[3,256,2048]{2,1,0:T(8,128)}, bf16[768,1024]{1,0:T(8,128)(2,1)}, bf16[10...) custom-call(s32[88]{0:T(128)} %concatenate.77.meta, bf16[8,768,128]{2,1,0:T(8,128)(2,1)} %all-to-all-done.1.refs_0_, ...), custom_call_target="tpu_custom_call" | custom-call | flops 96636768 | bytes 241591 | tf_op jit(solution)/shard_map/gated_unit/pallas_call | solution.py:202
  176.2 34.1 %feed_forward.2 = (f32[768,1024]{1,0:T(8,128)}, f32[2,1,1024]{2,1,0:T(1,128)}, f32[768,1024]{1,0:T(8,128)}, bf16[1024,1024]{1,0:T(8,128)(2,1)}, bf16[1024,1024]{...) custom-call(s32[88]{0:T(128)} %concatenate.77.meta, ...), custom_call_target="tpu_custom_call" | custom-call | flops 386547072 | bytes 966367 | tf_op jit(solution)/shard_map/feed_forward/pallas_call | solution.py:202
  214.7 3.3 fusion.4
  222.0 34.2 %feed_forward.3 = (f32[768,1024]{1,0:T(8,128)}, f32[2,1,1024]{2,1,0:T(1,128)}, f32[768,1024]{1,0:T(8,128)}, bf16[1024,1024]{1,0:T(8,128)(2,1)}, bf16[1024,1024]{...) custom-call(s32[88]{0:T(128)} %concatenate.77.meta, ...), custom_call_target="tpu_custom_call" | custom-call | flops 386547072 | bytes 966367 | tf_op jit(solution)/shard_map/feed_forward/pallas_call | solution.py:202
  256.2 15.0 %gated_back.1 = (f32[3,256,1024]{2,1,0:T(8,128)}, bf16[768,2048]{1,0:T(8,128)(2,1)}, f32[8,2048]{1,0:T(8,128)}, f32[8,1024]{1,0:T(8,128)}, bf16[8,768,128]{2,1,0:T(8,128)(2,1)}) custom-call(s32[88]{0:T(128)} %concatenate.77.meta, f32[768,1024]{1,0:T(8,128)} %get-tuple-element.200.refs_0_, f32[768,1024]{1,0:T(8,128)} %get-tuple-element.207.refs_1_, ...), custom_call_target="tpu_custom_call" | custom-call | flops 64424508 | bytes 161061 | tf_op jit(solution)/shard_map/gated_back/pallas_call | solution.py:202
  271.9 5.0 %all-to-all-start.2 = ((bf16[8,768,128]{2,1,0:T(8,128)(2,1)}), bf16[8,768,128]{2,1,0:T(8,128)(2,1)S(1)}, u32[]{:S(2)}, u32[]{:S(2)}) async-start(bf16[8,768,128]{2,1,0:T(8,128)(2,1)} %get-tuple-element.211), calls=%async_computation.2 | async-start | bytes 3145728 | tf_op jit(solution)/shard_map/all_to_all | solution.py:106
  279.2 3.9 fusion
  292.1 8.1 %gated_weight.1 = (bf16[8,32,2048]{2,1,0:T(8,128)(2,1)}, bf16[8,32,2048]{2,1,0:T(8,128)(2,1)}, bf16[2,8,32,2048]{3,2,1,0:T(8,128)(2,1)}) custom-call(s32[88]{0:T(128)} %concatenate.77.meta, bf16[768,1024]{1,0:T(8,128)(2,1)} %get-tuple-element.195.act_ref, bf16[768,2048]{1,0:T(8,128)(2,1)} %get-tuple-element.215.grad_ref), custom_call_target="tpu_custom_call" | custom-call | flops 64424508 | bytes 161061 | tf_op jit(solution)/shard_map/gated_weight/pallas_call | solution.py:202
  300.2 3.0 fusion.3
  303.2 11.0 %all-to-all-done.2.grads_ref = bf16[8,768,128]{2,1,0:T(8,128)(2,1)S(1)} async-done(((bf16[8,768,128]{2,1,0:T(8,128)(2,1)}), bf16[8,768,128]{2,1,0:T(8,128)(2,1)S(1)}, u32[]{:S(2)}, u32[]{:S(2)}) %all-to-all-start.2) | async-done | bytes 1572896 | tf_op jit(solution)/shard_map/all_to_all | solution.py:106
  315.4 21.0 %state_back.1 = (bf16[8,800,128]{2,1,0:T(8,128)(2,1)}, f32[8,512,128]{2,1,0:T(8,128)}, f32[8,128]{1,0:T(8,128)}) custom-call(s32[88]{0:T(128)} %concatenate.77.meta, bf16[8,768,128]{2,1,0:T(8,128)(2,1)} %copy-done.5, bf16[8,784,128]{2,1,0:T(8,128)(2,1)} %copy-done.1, f32[3,8,512,128]{3,2,1,0:T(8,128)} %get-tuple-element.233.drive_ref, ...), custom_call_target="tpu_custom_call" | custom-call | flops 400000000 | bytes 1000000 | tf_op jit(solution)/shard_map/state_back/pallas_call | solution.py:202
  337.2 3.9 all-to-all-start.3
  345.8 3.0 fusion.2
  356.2 10.8 %collective-permute-done.34 = bf16[8,2,32,1024]{3,2,1,0:T(8,128)(2,1)S(1)} collective-permute-done((bf16[8,2,32,1024]{3,2,1,0:T(8,128)(2,1)}, bf16[8,2,32,1024]{3,2,1,0:T(8,128)(2,1)S(1)}, u32[]{:S(2)}, u32[]{:S(2)}) %collective-permute-start.34) | collective-permute-done | bytes 1048608 | tf_op jit(solution)/shard_map/ppermute | solution.py:44
  371.3 18.4 %state_modes.1 = f32[2,64,128]{2,1,0:T(8,128)} custom-call(s32[88]{0:T(128)} %concatenate.77.meta, f32[8,512,128]{2,1,0:T(8,128)} %get-tuple-element.250.cross_ref, f32[64,32,128]{2,1,0:T(8,128)} %get-tuple-element.251.far_re, f32[64,32,128]{2,1,0:T(8,128)} %get-tuple-element.252.far_im, f32[64,64,128]{2,1,0:T(8,128)} %get-tuple-element.253.near_re, ...), custom_call_target="tpu_custom_call" | custom-call | flops 220000000 | bytes 550000 | tf_op jit(solution)/shard_map/state_modes/pallas_call | solution.py:202
  406.4 7.7 %input_grad.1 = bf16[3,256,1024]{2,1,0:T(8,128)(2,1)} custom-call(s32[88]{0:T(128)} %concatenate.77.meta, bf16[8,800,128]{2,1,0:T(8,128)(2,1)} %copy-done.4, bf16[3,256,1024]{2,1,0:T(8,128)(2,1)} %bitcast.209, f32[3,256,1024]{2,1,0:T(8,128)} %get-tuple-element.264.grad_resid_ref, bf16[1024,1024]{1,0:T(8,128)(2,1)} %get-tuple-element.265.perm_ref), custom_call_target="tpu_custom_call" | custom-call | flops 32212254 | bytes 80530 | tf_op jit(solution)/shard_map/input_grad/pallas_call | solution.py:202
  414.2 4.7 %collective-permute-done.40 = bf16[2,128,1024]{2,1,0:T(8,128)(2,1)S(1)} collective-permute-done((bf16[2,128,1024]{2,1,0:T(8,128)(2,1)S(1)}, bf16[2,128,1024]{2,1,0:T(8,128)(2,1)S(1)}, u32[]{:S(2)}, u32[]{:S(2)}) %collective-permute-start.40) | collective-permute-done | bytes 524320 | tf_op jit(solution)/shard_map/ppermute | solution.py:44
  432.2 9.6 %collective-permute-done.41 = bf16[2,32,2048]{2,1,0:T(8,128)(2,1)} collective-permute-done((bf16[2,32,2048]{2,1,0:T(8,128)(2,1)S(1)}, bf16[2,32,2048]{2,1,0:T(8,128)(2,1)}, u32[]{:S(2)}, u32[]{:S(2)}) %collective-permute-start.41) | collective-permute-done | bytes 262176 | tf_op jit(solution)/shard_map/ppermute | solution.py:44
  443.1 4.0 add_add_fusion
  (338 shorter events, 139.7 us)
Async XLA Ops:
  25.2 22.4 %collective-permute-start.7 = (bf16[2,32,4096]{2,1,0:T(8,128)(2,1)}, bf16[2,32,4096]{2,1,0:T(8,128)(2,1)S(1)}, u32[]{:S(2)}, u32[]{:S(2)}) collective-permute-start(bf16[2,32,4096]{2,1,0:T(8,128)(2,1)} %pad_maximum_fusion.4), channel_id=1, source_target_pairs={{0,2},{1,3},{2,0},{3,1},{4,6},{5,7},{6,4},{7,5},{8,10},{9,11},{10,... | collective-permute-start | bytes 1572872 | tf_op jit(solution)/shard_map/ppermute | solution.py:44
  26.2 21.4 %collective-permute-start.8 = (bf16[1,32,2048]{2,1,0:T(8,128)(2,1)}, bf16[1,32,2048]{2,1,0:T(8,128)(2,1)}, u32[]{:S(2)}, u32[]{:S(2)}) collective-permute-start(bf16[1,32,2048]{2,1,0:T(8,128)(2,1)} %bitcast.16), channel_id=1, source_target_pairs={{0,4},{1,5},{2,6},{3,7},{4,0},{5,1},{6,2},{7,3},{8,12},{9,13},{10,... | collective-permute-start | bytes 393224 | tf_op jit(solution)/shard_map/ppermute | solution.py:44
  29.5 44.5 %all-to-all-start = ((bf16[8,784,128]{2,1,0:T(8,128)(2,1)}), bf16[8,784,128]{2,1,0:T(8,128)(2,1)S(1)}, u32[]{:S(2)}, u32[]{:S(2)}) async-start(bf16[8,784,128]{2,1,0:T(8,128)(2,1)} %get-tuple-element.155), calls=%async_computation | async-start | bytes 3211264 | tf_op jit(solution)/shard_map/all_to_all | solution.py:106
  48.7 32.8 %collective-permute-start.9 = (bf16[4,32,4096]{2,1,0:T(8,128)(2,1)}, bf16[4,32,4096]{2,1,0:T(8,128)(2,1)}, u32[]{:S(2)}, u32[]{:S(2)}) collective-permute-start(bf16[4,32,4096]{2,1,0:T(8,128)(2,1)} %pad_maximum_fusion.1), channel_id=1, source_target_pairs={{0,1},{1,0},{2,3},{3,2},{4,5},{5,4},{6,7},{7,6},{8,9},{9,8},{10,11... | collective-permute-start | bytes 3145736 | tf_op jit(solution)/shard_map/ppermute | solution.py:44
  52.3 26.9 %collective-permute-start.10 = (bf16[2,32,2048]{2,1,0:T(8,128)(2,1)}, bf16[2,32,2048]{2,1,0:T(8,128)(2,1)}, u32[]{:S(2)}, u32[]{:S(2)}) collective-permute-start(bf16[2,32,2048]{2,1,0:T(8,128)(2,1)} %pad_maximum_fusion.7), channel_id=1, source_target_pairs={{0,2},{1,3},{2,0},{3,1},{4,6},{5,7},{6,4},{7,5},{8,10},{9,11},{10,... | collective-permute-start | bytes 786440 | tf_op jit(solution)/shard_map/ppermute | solution.py:44
  82.9 47.0 %collective-permute-start.16 = (bf16[256,4096]{1,0:T(8,128)(2,1)S(1)}, bf16[256,4096]{1,0:T(8,128)(2,1)}, u32[]{:S(2)}, u32[]{:S(2)}) collective-permute-start(bf16[256,4096]{1,0:T(8,128)(2,1)S(1)} %bitcast.203), channel_id=1, source_target_pairs={{0,16},{8,24},{16,0},{24,8},{1,17},{9,25},{17,1},{25,9},{2,18},{10... | collective-permute-start | bytes 6291464 | tf_op jit(solution)/shard_map/ppermute | solution.py:44
  85.5 21.1 %collective-permute-start.11 = (bf16[4,32,2048]{2,1,0:T(8,128)(2,1)S(1)}, bf16[4,32,2048]{2,1,0:T(8,128)(2,1)}, u32[]{:S(2)}, u32[]{:S(2)}) collective-permute-start(bf16[4,32,2048]{2,1,0:T(8,128)(2,1)S(1)} %pad_maximum_fusion.5), channel_id=1, source_target_pairs={{0,1},{1,0},{2,3},{3,2},{4,5},{5,4},{6,7},{7,6},{8,9},{9,8},{10,11... | collective-permute-start | bytes 1572872 | tf_op jit(solution)/shard_map/ppermute | solution.py:44
  85.6 20.9 %collective-permute-start.12 = (bf16[1,128,1024]{2,1,0:T(8,128)(2,1)S(1)}, bf16[1,128,1024]{2,1,0:T(8,128)(2,1)S(1)}, u32[]{:S(2)}, u32[]{:S(2)}) collective-permute-start(bf16[1,128,1024]{2,1,0:T(8,128)(2,1)S(1)} %bitcast.232), channel_id=1, source_target_pairs={{0,4},{1,5},{2,6},{3,7},{4,0},{5,1},{6,2},{7,3},{8,12},{9,13},{10,... | collective-permute-start | bytes 786440 | tf_op jit(solution)/shard_map/ppermute | solution.py:44
  89.0 17.6 %collective-permute-start.13 = (bf16[1,128,1024]{2,1,0:T(8,128)(2,1)S(1)}, bf16[1,128,1024]{2,1,0:T(8,128)(2,1)S(1)}, u32[]{:S(2)}, u32[]{:S(2)}) collective-permute-start(bf16[1,128,1024]{2,1,0:T(8,128)(2,1)S(1)} %bitcast.233), channel_id=1, source_target_pairs={{0,2},{1,3},{2,0},{3,1},{4,6},{5,7},{6,4},{7,5},{8,10},{9,11},{10,... | collective-permute-start | bytes 786440 | tf_op jit(solution)/shard_map/ppermute | solution.py:44
  108.4 52.8 %all-to-all-start.1 = ((bf16[8,768,128]{2,1,0:T(8,128)(2,1)}), bf16[8,768,128]{2,1,0:T(8,128)(2,1)}, u32[]{:S(2)}, u32[]{:S(2)}) async-start(bf16[8,768,128]{2,1,0:T(8,128)(2,1)} %get-tuple-element.181), calls=%async_computation.1 | async-start | bytes 3145728 | tf_op jit(solution)/shard_map/all_to_all | solution.py:106
  129.9 23.6 %collective-permute-start.17 = (bf16[256,2048]{1,0:T(8,128)(2,1)S(1)}, bf16[256,2048]{1,0:T(8,128)(2,1)}, u32[]{:S(2)}, u32[]{:S(2)}) collective-permute-start(bf16[256,2048]{1,0:T(8,128)(2,1)S(1)} %bitcast.211), channel_id=1, source_target_pairs={{0,16},{8,24},{16,0},{24,8},{1,17},{9,25},{17,1},{25,9},{2,18},{10... | collective-permute-start | bytes 3145736 | tf_op jit(solution)/shard_map/ppermute | solution.py:44
  131.4 22.8 %collective-permute-start.18 = (bf16[256,2048]{1,0:T(8,128)(2,1)S(1)}, bf16[256,2048]{1,0:T(8,128)(2,1)S(1)}, u32[]{:S(2)}, u32[]{:S(2)}) collective-permute-start(bf16[256,2048]{1,0:T(8,128)(2,1)S(1)} %bitcast.212), channel_id=1, source_target_pairs={{0,8},{8,0},{16,24},{24,16},{1,9},{9,1},{17,25},{25,17},{2,10},{10... | collective-permute-start | bytes 3145736 | tf_op jit(solution)/shard_map/ppermute | solution.py:44
  131.4 29.8 %collective-permute-start.15 = (bf16[4,128,1024]{2,1,0:T(8,128)(2,1)S(1)}, bf16[4,128,1024]{2,1,0:T(8,128)(2,1)}, u32[]{:S(2)}, u32[]{:S(2)}) collective-permute-start(bf16[4,128,1024]{2,1,0:T(8,128)(2,1)S(1)} %copy-done.22), channel_id=1, source_target_pairs={{0,1},{1,0},{2,3},{3,2},{4,5},{5,4},{6,7},{7,6},{8,9},{9,8},{10,11... | collective-permute-start | bytes 3145736 | tf_op jit(solution)/shard_map/ppermute | solution.py:44
  153.5 22.7 %collective-permute-start.21 = (bf16[256,4096]{1,0:T(8,128)(2,1)S(1)}, bf16[256,4096]{1,0:T(8,128)(2,1)}, u32[]{:S(2)}, u32[]{:S(2)}) collective-permute-start(bf16[256,4096]{1,0:T(8,128)(2,1)S(1)} %bitcast.204), channel_id=1, source_target_pairs={{0,8},{8,0},{16,24},{24,16},{1,9},{9,1},{17,25},{25,17},{2,10},{10... | collective-permute-start | bytes 6291464 | tf_op jit(solution)/shard_map/ppermute | solution.py:44
  154.1 22.0 %collective-permute-start.22 = (bf16[256,4096]{1,0:T(8,128)(2,1)}, bf16[256,4096]{1,0:T(8,128)(2,1)}, u32[]{:S(2)}, u32[]{:S(2)}) collective-permute-start(bf16[256,4096]{1,0:T(8,128)(2,1)} %collective-permute-done.16.refs_6_), channel_id=1, source_target_pairs={{0,8},{8,0},{16,24},{24,16},{1,9},{9,1},{17,25},{25,17},{2,10},{10... | collective-permute-start | bytes 6291464 | tf_op jit(solution)/shard_map/ppermute | solution.py:44
  163.5 48.3 %collective-permute-start.23 = (bf16[1024,1024]{1,0:T(8,128)(2,1)}, bf16[1024,1024]{1,0:T(8,128)(2,1)}, u32[]{:S(2)}, u32[]{:S(2)}) collective-permute-start(bf16[1024,1024]{1,0:T(8,128)(2,1)} %bitcast.217), channel_id=1, source_target_pairs={{0,16},{8,24},{16,0},{24,8},{1,17},{9,25},{17,1},{25,9},{2,18},{10... | collective-permute-start | bytes 6291464 | tf_op jit(solution)/shard_map/ppermute | solution.py:44
  211.8 44.4 %collective-permute-start.27 = (bf16[1,1024,1024]{2,1,0:T(8,128)(2,1)}, bf16[1,1024,1024]{2,1,0:T(8,128)(2,1)}, u32[]{:S(2)}, u32[]{:S(2)}) collective-permute-start(bf16[1,1024,1024]{2,1,0:T(8,128)(2,1)} %bitcast.253), channel_id=1, source_target_pairs={{0,8},{8,0},{16,24},{24,16},{1,9},{9,1},{17,25},{25,17},{2,10},{10... | collective-permute-start | bytes 6291464 | tf_op jit(solution)/shard_map/ppermute | solution.py:44
  218.1 38.2 %collective-permute-start.26 = (bf16[8,2,32,1024]{3,2,1,0:T(8,128)(2,1)}, bf16[8,2,32,1024]{3,2,1,0:T(8,128)(2,1)S(1)}, u32[]{:S(2)}, u32[]{:S(2)}) collective-permute-start(bf16[8,2,32,1024]{3,2,1,0:T(8,128)(2,1)} %fusion.4), channel_id=1, source_target_pairs={{0,16},{8,24},{16,0},{24,8},{1,17},{9,25},{17,1},{25,9},{2,18},{10... | collective-permute-start | bytes 3145736 | tf_op jit(solution)/shard_map/ppermute | solution.py:44
  271.9 42.4 %all-to-all-start.2 = ((bf16[8,768,128]{2,1,0:T(8,128)(2,1)}), bf16[8,768,128]{2,1,0:T(8,128)(2,1)S(1)}, u32[]{:S(2)}, u32[]{:S(2)}) async-start(bf16[8,768,128]{2,1,0:T(8,128)(2,1)} %get-tuple-element.211), calls=%async_computation.2 | async-start | bytes 3145728 | tf_op jit(solution)/shard_map/all_to_all | solution.py:106
  283.1 53.3 %collective-permute-start.31 = (bf16[1024,1024]{1,0:T(8,128)(2,1)}, bf16[1024,1024]{1,0:T(8,128)(2,1)}, u32[]{:S(2)}, u32[]{:S(2)}) collective-permute-start(bf16[1024,1024]{1,0:T(8,128)(2,1)} %fusion), channel_id=1, source_target_pairs={{0,16},{8,24},{16,0},{24,8},{1,17},{9,25},{17,1},{25,9},{2,18},{10... | collective-permute-start | bytes 6291464 | tf_op jit(solution)/shard_map/ppermute | solution.py:44
  289.4 47.0 %collective-permute-start.30 = (bf16[4,2,32,1024]{3,2,1,0:T(8,128)(2,1)}, bf16[4,2,32,1024]{3,2,1,0:T(8,128)(2,1)S(1)}, u32[]{:S(2)}, u32[]{:S(2)}) collective-permute-start(bf16[4,2,32,1024]{3,2,1,0:T(8,128)(2,1)} %fusion.10), channel_id=1, source_target_pairs={{0,1},{1,0},{2,3},{3,2},{4,5},{5,4},{6,7},{7,6},{8,9},{9,8},{10,11... | collective-permute-start | bytes 1572872 | tf_op jit(solution)/shard_map/ppermute | solution.py:44
  337.2 52.6 %all-to-all-start.3 = ((bf16[8,800,128]{2,1,0:T(8,128)(2,1)}), bf16[8,800,128]{2,1,0:T(8,128)(2,1)S(1)}, u32[]{:S(2)}, u32[]{:S(2)}) async-start(bf16[8,800,128]{2,1,0:T(8,128)(2,1)} %get-tuple-element.260), calls=%async_computation.3 | async-start | bytes 3276800 | tf_op jit(solution)/shard_map/all_to_all | solution.py:106
  342.0 25.0 %collective-permute-start.34 = (bf16[8,2,32,1024]{3,2,1,0:T(8,128)(2,1)}, bf16[8,2,32,1024]{3,2,1,0:T(8,128)(2,1)S(1)}, u32[]{:S(2)}, u32[]{:S(2)}) collective-permute-start(bf16[8,2,32,1024]{3,2,1,0:T(8,128)(2,1)} %fusion.3), channel_id=1, source_target_pairs={{0,16},{8,24},{16,0},{24,8},{1,17},{9,25},{17,1},{25,9},{2,18},{10... | collective-permute-start | bytes 3145736 | tf_op jit(solution)/shard_map/ppermute | solution.py:44
  348.8 43.7 %collective-permute-start.37 = (bf16[4,128,1024]{2,1,0:T(8,128)(2,1)}, bf16[4,128,1024]{2,1,0:T(8,128)(2,1)}, u32[]{:S(2)}, u32[]{:S(2)}) collective-permute-start(bf16[4,128,1024]{2,1,0:T(8,128)(2,1)} %fusion.2), channel_id=1, source_target_pairs={{0,1},{1,0},{2,3},{3,2},{4,5},{5,4},{6,7},{7,6},{8,9},{9,8},{10,11... | collective-permute-start | bytes 3145736 | tf_op jit(solution)/shard_map/ppermute | solution.py:44
  352.1 37.6 %collective-permute-start.36 = (bf16[2,2,32,1024]{3,2,1,0:T(8,128)(2,1)S(1)}, bf16[2,2,32,1024]{3,2,1,0:T(8,128)(2,1)S(1)}, u32[]{:S(2)}, u32[]{:S(2)}) collective-permute-start(bf16[2,2,32,1024]{3,2,1,0:T(8,128)(2,1)S(1)} %fusion.23), channel_id=1, source_target_pairs={{0,2},{1,3},{2,0},{3,1},{4,6},{5,7},{6,4},{7,5},{8,10},{9,11},{10,... | collective-permute-start | bytes 786440 | tf_op jit(solution)/shard_map/ppermute | solution.py:44
  368.2 27.4 %collective-permute-start.35 = (bf16[4,2,32,1024]{3,2,1,0:T(8,128)(2,1)}, bf16[4,2,32,1024]{3,2,1,0:T(8,128)(2,1)}, u32[]{:S(2)}, u32[]{:S(2)}) collective-permute-start(bf16[4,2,32,1024]{3,2,1,0:T(8,128)(2,1)} %add_convert_fusion.1), channel_id=1, source_target_pairs={{0,1},{1,0},{2,3},{3,2},{4,5},{5,4},{6,7},{7,6},{8,9},{9,8},{10,11... | collective-permute-start | bytes 1572872 | tf_op jit(solution)/shard_map/ppermute | solution.py:44
  369.9 29.3 %collective-permute-start.33 = (bf16[8,32,2048]{2,1,0:T(8,128)(2,1)}, bf16[8,32,2048]{2,1,0:T(8,128)(2,1)}, u32[]{:S(2)}, u32[]{:S(2)}) collective-permute-start(bf16[8,32,2048]{2,1,0:T(8,128)(2,1)} %fusion.1), channel_id=1, source_target_pairs={{0,16},{8,24},{16,0},{24,8},{1,17},{9,25},{17,1},{25,9},{2,18},{10... | collective-permute-start | bytes 3145736 | tf_op jit(solution)/shard_map/ppermute | solution.py:44
  392.5 56.3 %collective-permute-start.48 = (bf16[1,2,32,1024]{3,2,1,0:T(8,128)(2,1)}, bf16[1,2,32,1024]{3,2,1,0:T(8,128)(2,1)}, u32[]{:S(2)}, u32[]{:S(2)}) collective-permute-start(bf16[1,2,32,1024]{3,2,1,0:T(8,128)(2,1)} %fusion.39), channel_id=1, source_target_pairs={{0,4},{1,5},{2,6},{3,7},{4,0},{5,1},{6,2},{7,3},{8,12},{9,13},{10,... | collective-permute-start | bytes 393224 | tf_op jit(solution)/shard_map/ppermute | solution.py:44
  401.5 17.3 %collective-permute-start.39 = (bf16[4,32,2048]{2,1,0:T(8,128)(2,1)}, bf16[4,32,2048]{2,1,0:T(8,128)(2,1)}, u32[]{:S(2)}, u32[]{:S(2)}) collective-permute-start(bf16[4,32,2048]{2,1,0:T(8,128)(2,1)} %fusion.6), channel_id=1, source_target_pairs={{0,1},{1,0},{2,3},{3,2},{4,5},{5,4},{6,7},{7,6},{8,9},{9,8},{10,11... | collective-permute-start | bytes 1572872 | tf_op jit(solution)/shard_map/ppermute | solution.py:44
  420.9 27.9 %collective-permute-start.49 = (bf16[1,128,1024]{2,1,0:T(8,128)(2,1)}, bf16[1,128,1024]{2,1,0:T(8,128)(2,1)}, u32[]{:S(2)}, u32[]{:S(2)}) collective-permute-start(bf16[1,128,1024]{2,1,0:T(8,128)(2,1)} %fusion.20), channel_id=1, source_target_pairs={{0,4},{1,5},{2,6},{3,7},{4,0},{5,1},{6,2},{7,3},{8,12},{9,13},{10,... | collective-permute-start | bytes 786440 | tf_op jit(solution)/shard_map/ppermute | solution.py:44
  424.1 17.7 %collective-permute-start.41 = (bf16[2,32,2048]{2,1,0:T(8,128)(2,1)S(1)}, bf16[2,32,2048]{2,1,0:T(8,128)(2,1)}, u32[]{:S(2)}, u32[]{:S(2)}) collective-permute-start(bf16[2,32,2048]{2,1,0:T(8,128)(2,1)S(1)} %fusion.17), channel_id=1, source_target_pairs={{0,2},{1,3},{2,0},{3,1},{4,6},{5,7},{6,4},{7,5},{8,10},{9,11},{10,... | collective-permute-start | bytes 786440 | tf_op jit(solution)/shard_map/ppermute | solution.py:44
  428.7 20.1 %collective-permute-start.47 = (bf16[1,2,32,1024]{3,2,1,0:T(8,128)(2,1)S(1)}, bf16[1,2,32,1024]{3,2,1,0:T(8,128)(2,1)S(1)}, u32[]{:S(2)}, u32[]{:S(2)}) collective-permute-start(bf16[1,2,32,1024]{3,2,1,0:T(8,128)(2,1)S(1)} %add_convert_fusion.3), channel_id=1, source_target_pairs={{0,4},{1,5},{2,6},{3,7},{4,0},{5,1},{6,2},{7,3},{8,12},{9,13},{10,... | collective-permute-start | bytes 393224 | tf_op jit(solution)/shard_map/ppermute | solution.py:44
  (79 other events, 851.5 us)
